TPU v7x, 32 devices: a whole 2x2x4 slice. The times are simulated.
32 devices in a mesh: dp: 8 (over z, y), tensor: 4 (over x, core).
Axes of the slice: x: 2, y: 2, z: 4, core: 2. Of those that a mesh axis runs over, the one named last changes fastest.
Arguments:
- content: bfloat16 [16384, 768], P(('dp', 'tensor')), may hold values from -6 to 6
- query_stream: bfloat16 [16384, 768], P(('dp', 'tensor')), may hold values from -6 to 6
- cot_content: bfloat16 [16384, 768], P(('dp', 'tensor')), may hold values from -6 to 6
- cot_query: bfloat16 [16384, 768], P(('dp', 'tensor')), may hold values from -6 to 6
- doc_lengths: int32 [32, 8], P('dp'), may hold values from 1 to 256, as said below
- rank_order: int32 [32, 512], P('dp'), may hold values from 0 to 511, as said below
- pred_counts: int32 [32], P('dp'), may hold values from 64 to 127
- w_qkv: bfloat16 [3, 768, 768], P(None, None, 'tensor'), may hold values from -0.21875 to 0.21875
- bias_qv: bfloat16 [2, 768], P(None, 'tensor'), may hold values from -1.5 to 1.5
- w_attn_out: bfloat16 [768, 768], P('tensor'), may hold values from -0.875 to 0.875
- b_attn_out: bfloat16 [768], replicated, may hold values from -2.5 to 2.5
- norm1_gain: float32 [768], replicated, may hold values from 0.1 to 1.9
- norm1_shift: float32 [768], replicated, may hold values from -2.5 to 2.5
- w_in: bfloat16 [768, 3072], P(None, 'tensor'), may hold values from -0.21875 to 0.21875
- b_in: bfloat16 [3072], P('tensor'), may hold values from -2.5 to 2.5
- w_out: bfloat16 [3072, 768], P('tensor'), may hold values from -0.109375 to 0.109375
- b_out: bfloat16 [768], replicated, may hold values from -2.5 to 2.5
- norm2_gain: float32 [768], replicated, may hold values from 0.1 to 1.9
- norm2_shift: float32 [768], replicated, may hold values from -2.5 to 2.5
- rel_table: bfloat16 [32, 12], P(None, 'tensor'), may hold values from -4 to 4
Outputs:
- out_content: bfloat16 [16384, 768], P(('dp', 'tensor'))
- out_query: bfloat16 [16384, 768], P(('dp', 'tensor'))
- grad_content: float32 [16384, 768], P(('dp', 'tensor'))
- grad_query: float32 [16384, 768], P(('dp', 'tensor'))
- grad_w_qkv: float32 [3, 768, 768], P(None, 'dp', 'tensor')
- grad_bias_qv: float32 [2, 768], P(None, 'tensor')
- grad_w_attn_out: float32 [768, 768], P('tensor', 'dp')
- grad_b_attn_out: float32 [768], replicated
- grad_norm1_gain: float32 [768], replicated
- grad_norm1_shift: float32 [768], replicated
- grad_w_in: float32 [768, 3072], P('dp', 'tensor')
- grad_b_in: float32 [3072], P('tensor')
- grad_w_out: float32 [3072, 768], P('tensor', 'dp')
- grad_b_out: float32 [768], replicated
- grad_norm2_gain: float32 [768], replicated
- grad_norm2_shift: float32 [768], replicated
- grad_rel_table: float32 [32, 12], P(None, 'tensor')
Inputs may be any that keep to these rules, and one draw needn't show every extreme that they name: `doc_lengths`: each row's 8 lengths sum to 512; one of them is 256. `rank_order`: each row is a permutation of 0 to 511; the first position of every document has a rank below 8.
All inputs are finite; a program needn't handle non-finite values.
Results may differ from a plain program's by a relative error of at most 0.015.
The roundings to bfloat16 on the way count: a program that leaves them out, or rounds other values in their place, can miss the bound.
Values may be sent and summed in bfloat16 or wider, within the bound.
A program may use at most 192 MiB of HBM per device.

v0:
```python
import math

import jax
import jax.numpy as jnp
from jax import lax
from jax.sharding import PartitionSpec as P

EDGES = (1, 2, 3, 4, 5, 6, 7, 8, 12, 16, 23, 32, 46, 64, 91)
NEGATIVE = -1e30
EPSILON = 1e-05
HIGHEST = lax.Precision.HIGHEST
CONTRACT_ROWS = (((0,), (0,)), ((), ()))
CONTRACT_COLS = (((1,), (1,)), ((), ()))


def bucket_ids(length):
    places = jnp.arange(length, dtype=jnp.int32)
    offsets = places[None, :] - places[:, None]
    distance = jnp.abs(offsets)
    result = jnp.where(offsets > 0, 16, 0).astype(jnp.int32)
    for boundary in EDGES:
        result = result + (distance >= boundary).astype(jnp.int32)
    return result


def stream_masks(lengths_row, rank_row, pred_count):
    length = rank_row.shape[0]
    places = jnp.arange(length, dtype=jnp.int32)
    doc_ends = jnp.cumsum(lengths_row)
    doc_ids = jnp.sum((places[:, None] >= doc_ends[None, :]).astype(jnp.int32), axis=1)
    same_doc = doc_ids[:, None] == doc_ids[None, :]
    unmasked = rank_row[None, :] < length - pred_count
    earlier = rank_row[None, :] < rank_row[:, None]
    itself = places[:, None] == places[None, :]
    content_mask = same_doc & (unmasked | earlier | itself)
    query_mask = same_doc & (unmasked | earlier)
    return (content_mask, query_mask)


def layer_norm(rows_in, gain_vec, norm_shift):
    mean_row = jnp.mean(rows_in, axis=-1, keepdims=True)
    centred = rows_in - mean_row
    variance = jnp.mean(centred * centred, axis=-1, keepdims=True)
    return centred * lax.rsqrt(variance + EPSILON) * gain_vec + norm_shift


def exact_gelu(values_in):
    return jax.nn.gelu(values_in, approximate=False)


def plain_dot(rows_in, weight):
    return jnp.dot(rows_in, weight, preferred_element_type=jnp.float32)


def left_dot(left_rows, right_rows):
    return lax.dot_general(left_rows, right_rows, CONTRACT_ROWS, preferred_element_type=jnp.float32)


def back_dot(grad_rows, weight):
    return lax.dot_general(grad_rows, weight, CONTRACT_COLS, preferred_element_type=jnp.float32)


def onehot_block(bucket_rows, count):
    return (bucket_rows[:, :, None] == jnp.arange(count, dtype=jnp.int32)[None, None, :]).astype(
        jnp.float32
    )


def table_bias(buckets, table_vals):
    length = buckets.shape[0]
    blocked = buckets.reshape(8, length // 8, length)

    def one_block(bucket_rows):
        return jnp.einsum(
            "ijb,bh->hij",
            onehot_block(bucket_rows, table_vals.shape[0]),
            table_vals,
            precision=HIGHEST,
        )

    pieces = lax.map(one_block, blocked)
    return jnp.transpose(pieces, (1, 0, 2, 3)).reshape(table_vals.shape[1], length, length)


def table_grad(buckets, grad_sum, count):
    length = buckets.shape[0]
    blocked_ids = buckets.reshape(8, length // 8, length)
    blocked_grads = jnp.transpose(
        grad_sum.reshape(grad_sum.shape[0], 8, length // 8, length), (1, 0, 2, 3)
    )

    def one_block(item_set):
        bucket_rows, grad_rows = item_set
        return jnp.einsum(
            "hij,ijb->bh", grad_rows, onehot_block(bucket_rows, count), precision=HIGHEST
        )

    return jnp.sum(lax.map(one_block, (blocked_ids, blocked_grads)), axis=0)


def scores_of(queries, keys_all, pos_bias, vis_mask):
    scale = 1.0 / math.sqrt(queries.shape[-1])
    raw_scores = (
        jnp.einsum("ihd,jhd->hij", queries, keys_all, preferred_element_type=jnp.float32) * scale
        + pos_bias
    )
    return jnp.where(vis_mask[None], raw_scores, NEGATIVE)


def attend_forward(queries, keys_all, values, pos_bias, vis_mask):
    masked = scores_of(queries, keys_all, pos_bias, vis_mask)
    row_max = jnp.max(masked, axis=-1, keepdims=True)
    exp_terms = jnp.exp(masked - row_max)
    row_total = jnp.sum(exp_terms, axis=-1, keepdims=True)
    prob_low = (exp_terms / row_total).astype(jnp.bfloat16)
    mixed = jnp.einsum("hij,jhd->ihd", prob_low, values, preferred_element_type=jnp.float32)
    return (mixed.astype(jnp.bfloat16), (row_max + jnp.log(row_total))[:, :, 0])


def attend_backward(queries, keys_all, values, pos_bias, vis_mask, log_total, grad_mixed):
    scale = 1.0 / math.sqrt(queries.shape[-1])
    masked = scores_of(queries, keys_all, pos_bias, vis_mask)
    probs = jnp.exp(masked - log_total[:, :, None])
    grad_probs = jnp.einsum("ihd,jhd->hij", grad_mixed, values, preferred_element_type=jnp.float32)
    inner = jnp.sum(grad_probs * probs, axis=-1, keepdims=True)
    grad_scores = (probs * (grad_probs - inner)).astype(jnp.bfloat16)
    grad_queries = (
        jnp.einsum("hij,jhd->ihd", grad_scores, keys_all, preferred_element_type=jnp.float32)
        * scale
    )
    grad_keys = (
        jnp.einsum("hij,ihd->jhd", grad_scores, queries, preferred_element_type=jnp.float32) * scale
    )
    grad_values = jnp.einsum(
        "hij,ihd->jhd", probs.astype(jnp.bfloat16), grad_mixed, preferred_element_type=jnp.float32
    )
    return (grad_queries, grad_keys, grad_values, grad_scores)


def local(
    content,
    query_stream,
    cot_content,
    cot_query,
    doc_lengths,
    rank_order,
    pred_counts,
    w_qkv,
    bias_qv,
    w_attn_out,
    b_attn_out,
    norm1_gain,
    norm1_shift,
    w_in,
    b_in,
    w_out,
    b_out,
    norm2_gain,
    norm2_shift,
    rel_table,
):
    length = rank_order.shape[1]
    buckets = bucket_ids(length)
    lengths_use, ranks_use, counts_use = (doc_lengths, rank_order, pred_counts)
    weights_use = (w_qkv, bias_qv, w_attn_out, w_in, b_in, w_out, rel_table)
    rows_c, rows_g = (
        lax.all_gather(content, "tensor", axis=0, tiled=True),
        lax.all_gather(query_stream, "tensor", axis=0, tiled=True),
    )
    qkv_use, bias_qv_use, attn_out_use, w_in_use, b_in_use, w_out_use, table_use = weights_use
    seq_count = rows_c.shape[0] // length
    head_count = table_use.shape[1]
    width_local = qkv_use.shape[2]
    head_size = width_local // head_count
    masks_c, masks_g = jax.vmap(stream_masks)(lengths_use, ranks_use, counts_use)
    pos_bias = table_bias(buckets, table_use.astype(jnp.float32))
    bias_query = bias_qv_use[0].astype(jnp.float32)
    bias_value = bias_qv_use[1].astype(jnp.float32)
    q_content = (plain_dot(rows_c, qkv_use[0]) + bias_query).astype(jnp.bfloat16)
    keys_all = plain_dot(rows_c, qkv_use[1]).astype(jnp.bfloat16)
    values = (plain_dot(rows_c, qkv_use[2]) + bias_value).astype(jnp.bfloat16)
    q_query = (plain_dot(rows_g, qkv_use[0]) + bias_query).astype(jnp.bfloat16)

    def by_heads(rows_in):
        return rows_in.reshape(seq_count, length, head_count, head_size)

    def flat_rows(heads_in):
        return heads_in.reshape(seq_count * length, width_local)

    heads_c, heads_g = (by_heads(q_content), by_heads(q_query))
    heads_k, heads_v = (by_heads(keys_all), by_heads(values))

    def attend_both(item_set):
        query_one, query_two, key_rows, value_rows, mask_one, mask_two = item_set
        mixed_one, log_one = attend_forward(query_one, key_rows, value_rows, pos_bias, mask_one)
        mixed_two, log_two = attend_forward(query_two, key_rows, value_rows, pos_bias, mask_two)
        return (mixed_one, mixed_two, log_one, log_two)

    mixed_c, mixed_g, log_c, log_g = lax.map(
        attend_both, (heads_c, heads_g, heads_k, heads_v, masks_c, masks_g)
    )
    attn_c = flat_rows(mixed_c)
    attn_g = flat_rows(mixed_g)
    proj_c = plain_dot(attn_c, attn_out_use)
    proj_g = plain_dot(attn_g, attn_out_use)
    proj_c, proj_g = (
        lax.psum_scatter(proj_c, "tensor", scatter_dimension=0, tiled=True),
        lax.psum_scatter(proj_g, "tensor", scatter_dimension=0, tiled=True),
    )
    bias_attn = b_attn_out.astype(jnp.float32)
    res1_c = content.astype(jnp.float32) + proj_c + bias_attn
    res1_g = query_stream.astype(jnp.float32) + proj_g + bias_attn
    norm1_c, pullback1_c = jax.vjp(layer_norm, res1_c, norm1_gain, norm1_shift)
    norm1_g, pullback1_g = jax.vjp(layer_norm, res1_g, norm1_gain, norm1_shift)
    hidden_c = norm1_c.astype(jnp.bfloat16)
    hidden_g = norm1_g.astype(jnp.bfloat16)
    hid_all_c, hid_all_g = (
        lax.all_gather(hidden_c, "tensor", axis=0, tiled=True),
        lax.all_gather(hidden_g, "tensor", axis=0, tiled=True),
    )
    shift_in = b_in_use.astype(jnp.float32)
    act_c, gelu_pull_c = jax.vjp(exact_gelu, plain_dot(hid_all_c, w_in_use) + shift_in)
    act_g, gelu_pull_g = jax.vjp(exact_gelu, plain_dot(hid_all_g, w_in_use) + shift_in)
    act_low_c = act_c.astype(jnp.bfloat16)
    act_low_g = act_g.astype(jnp.bfloat16)
    ffn_c = plain_dot(act_low_c, w_out_use)
    ffn_g = plain_dot(act_low_g, w_out_use)
    ffn_c, ffn_g = (
        lax.psum_scatter(ffn_c, "tensor", scatter_dimension=0, tiled=True),
        lax.psum_scatter(ffn_g, "tensor", scatter_dimension=0, tiled=True),
    )
    bias_ffn = b_out.astype(jnp.float32)
    res2_c = hidden_c.astype(jnp.float32) + ffn_c + bias_ffn
    res2_g = hidden_g.astype(jnp.float32) + ffn_g + bias_ffn
    out_c, pullback2_c = jax.vjp(layer_norm, res2_c, norm2_gain, norm2_shift)
    out_g, pullback2_g = jax.vjp(layer_norm, res2_g, norm2_gain, norm2_shift)
    dres2_c, gain2_c, shift2_c = pullback2_c(cot_content.astype(jnp.float32))
    dres2_g, gain2_g, shift2_g = pullback2_g(cot_query.astype(jnp.float32))
    low2_c = dres2_c.astype(jnp.bfloat16)
    low2_g = dres2_g.astype(jnp.bfloat16)
    dall2_c, dall2_g = (
        lax.all_gather(low2_c, "tensor", axis=0, tiled=True),
        lax.all_gather(low2_g, "tensor", axis=0, tiled=True),
    )
    grad_w_out_part = left_dot(act_low_c, dall2_c) + left_dot(act_low_g, dall2_g)
    dpre_c = gelu_pull_c(back_dot(dall2_c, w_out_use))[0].astype(jnp.bfloat16)
    dpre_g = gelu_pull_g(back_dot(dall2_g, w_out_use))[0].astype(jnp.bfloat16)
    grad_w_in_part = left_dot(hid_all_c, dpre_c) + left_dot(hid_all_g, dpre_g)
    grad_b_in_part = jnp.sum(dpre_c, axis=0, dtype=jnp.float32) + jnp.sum(
        dpre_g, axis=0, dtype=jnp.float32
    )
    dhid_c = back_dot(dpre_c, w_in_use)
    dhid_g = back_dot(dpre_g, w_in_use)
    dhid_c, dhid_g = (
        lax.psum_scatter(dhid_c, "tensor", scatter_dimension=0, tiled=True),
        lax.psum_scatter(dhid_g, "tensor", scatter_dimension=0, tiled=True),
    )
    dres1_c, gain1_c, shift1_c = pullback1_c(dres2_c + dhid_c)
    dres1_g, gain1_g, shift1_g = pullback1_g(dres2_g + dhid_g)
    low1_c = dres1_c.astype(jnp.bfloat16)
    low1_g = dres1_g.astype(jnp.bfloat16)
    dall1_c, dall1_g = (
        lax.all_gather(low1_c, "tensor", axis=0, tiled=True),
        lax.all_gather(low1_g, "tensor", axis=0, tiled=True),
    )
    grad_attn_out_part = left_dot(attn_c, dall1_c) + left_dot(attn_g, dall1_g)
    dattn_c = back_dot(dall1_c, attn_out_use).astype(jnp.bfloat16)
    dattn_g = back_dot(dall1_g, attn_out_use).astype(jnp.bfloat16)

    def attend_grads(accum, item_set):
        (
            query_one,
            query_two,
            key_rows,
            value_rows,
            mask_one,
            mask_two,
            log_one,
            log_two,
            grad_one,
            grad_two,
        ) = item_set
        dq_one, dk_one, dv_one, ds_one = attend_backward(
            query_one, key_rows, value_rows, pos_bias, mask_one, log_one, grad_one
        )
        dq_two, dk_two, dv_two, ds_two = attend_backward(
            query_two, key_rows, value_rows, pos_bias, mask_two, log_two, grad_two
        )
        accum = accum + ds_one.astype(jnp.float32) + ds_two.astype(jnp.float32)
        return (
            accum,
            (
                dq_one.astype(jnp.bfloat16),
                dq_two.astype(jnp.bfloat16),
                (dk_one + dk_two).astype(jnp.bfloat16),
                (dv_one + dv_two).astype(jnp.bfloat16),
            ),
        )

    grad_sum, grad_heads = lax.scan(
        attend_grads,
        jnp.zeros((head_count, length, length), jnp.float32),
        (
            heads_c,
            heads_g,
            heads_k,
            heads_v,
            masks_c,
            masks_g,
            log_c,
            log_g,
            by_heads(dattn_c),
            by_heads(dattn_g),
        ),
    )
    grad_q_content = flat_rows(grad_heads[0])
    grad_q_query = flat_rows(grad_heads[1])
    grad_keys = flat_rows(grad_heads[2])
    grad_values = flat_rows(grad_heads[3])
    grad_table_part = table_grad(buckets, grad_sum, table_use.shape[0])
    grad_qkv_part = jnp.stack(
        [
            left_dot(rows_c, grad_q_content) + left_dot(rows_g, grad_q_query),
            left_dot(rows_c, grad_keys),
            left_dot(rows_c, grad_values),
        ]
    )
    grad_bias_qv_part = jnp.stack(
        [
            jnp.sum(grad_q_content, axis=0, dtype=jnp.float32)
            + jnp.sum(grad_q_query, axis=0, dtype=jnp.float32),
            jnp.sum(grad_values, axis=0, dtype=jnp.float32),
        ]
    )
    din_c = (
        back_dot(grad_q_content, qkv_use[0])
        + back_dot(grad_keys, qkv_use[1])
        + back_dot(grad_values, qkv_use[2])
    )
    din_g = back_dot(grad_q_query, qkv_use[0])
    din_c, din_g = (
        lax.psum_scatter(
            din_c.astype(jnp.bfloat16), "tensor", scatter_dimension=0, tiled=True
        ).astype(jnp.float32),
        lax.psum_scatter(
            din_g.astype(jnp.bfloat16), "tensor", scatter_dimension=0, tiled=True
        ).astype(jnp.float32),
    )
    grad_content = dres1_c + din_c
    grad_query = dres1_g + din_g
    grad_w_qkv, grad_w_attn_out, grad_w_in, grad_w_out = (
        lax.psum_scatter(grad_qkv_part, "dp", scatter_dimension=1, tiled=True),
        lax.psum_scatter(grad_attn_out_part, "dp", scatter_dimension=1, tiled=True),
        lax.psum_scatter(grad_w_in_part, "dp", scatter_dimension=0, tiled=True),
        lax.psum_scatter(grad_w_out_part, "dp", scatter_dimension=1, tiled=True),
    )
    grad_bias_qv, grad_b_in, grad_rel_table = lax.psum(
        (grad_bias_qv_part, grad_b_in_part, grad_table_part), "dp"
    )
    shared = lax.psum(
        (
            jnp.sum(dres1_c, axis=0) + jnp.sum(dres1_g, axis=0),
            gain1_c + gain1_g,
            shift1_c + shift1_g,
            jnp.sum(dres2_c, axis=0) + jnp.sum(dres2_g, axis=0),
            gain2_c + gain2_g,
            shift2_c + shift2_g,
        ),
        ("dp", "tensor"),
    )
    return (
        out_c.astype(jnp.bfloat16),
        out_g.astype(jnp.bfloat16),
        grad_content,
        grad_query,
        grad_w_qkv,
        grad_bias_qv,
        grad_w_attn_out,
        shared[0],
        shared[1],
        shared[2],
        grad_w_in,
        grad_b_in,
        grad_w_out,
        shared[3],
        shared[4],
        shared[5],
        grad_rel_table,
    )


def solution(mesh):
    in_specs = (
        P(("dp", "tensor"), None),
        P(("dp", "tensor"), None),
        P(("dp", "tensor"), None),
        P(("dp", "tensor"), None),
        P("dp", None),
        P("dp", None),
        P("dp"),
        P(None, None, "tensor"),
        P(None, "tensor"),
        P("tensor", None),
        P(),
        P(),
        P(),
        P(None, "tensor"),
        P("tensor"),
        P("tensor", None),
        P(),
        P(),
        P(),
        P(None, "tensor"),
    )
    out_specs = (
        P(("dp", "tensor"), None),
        P(("dp", "tensor"), None),
        P(("dp", "tensor"), None),
        P(("dp", "tensor"), None),
        P(None, "dp", "tensor"),
        P(None, "tensor"),
        P("tensor", "dp"),
        P(),
        P(),
        P(),
        P("dp", "tensor"),
        P("tensor"),
        P("tensor", "dp"),
        P(),
        P(),
        P(),
        P(None, "tensor"),
    )
    return jax.shard_map(local, mesh=mesh, in_specs=in_specs, out_specs=out_specs, check_vma=False)
```

profile of v0, /device:TPU:0, one launch (start us, length us, event | category | flops | bytes accessed | tf_op | source)
XLA Modules:
  0.0 1212.3 jit_solution(10622219546484871451)
XLA Ops:
  11.3 18.0 %while.55 = (s32[]{:T(128)}, f32[8,3,64,512]{3,2,0,1:T(8,128)}, s32[8,64,512]{2,1,0:T(8,128)S(1)}, f32[32,3]{0,1:T(4,128)S(1)}, s32[]{:T(128)}) while((s32[]{:T(128)}, f32[8,3,64,512]{3,2,0,1:T(8,128)}, s32[8,64,512]{2,1,0:T(8,128)S(1)}, f32[32,3]{0,1:T(4,128)S(1)}, s32[]{:T(128)}) %tuple.158), condition=%wide.region_3.4_spmd, body=%wide.region_2.3_spmd.sunk | while | flops 38797312 | bytes 1573825 | solution.py:81
  53.7 17.3 %all-gather.11.cloned.1.call-done = bf16[2048,768]{1,0:T(8,128)(2,1)} async-done(((bf16[512,768]{1,0:T(8,128)(2,1)}), bf16[2048,768]{1,0:T(8,128)(2,1)}) %all-gather.11.cloned.1.call-update) | async-done | bytes 3145744 | tf_op jit(solution)/shard_map/all_gather | solution.py:168
  78.7 41.5 %while.56 = (s32[]{:T(128)}, bf16[4,512,3,64]{1,3,2,0:T(8,128)(2,1)}, bf16[4,512,3,64]{1,3,2,0:T(8,128)(2,1)}, f32[4,3,512]{2,1,0:T(4,128)}, f32[4,3,512]{2,1,0:...) while((s32[]{:T(128)}, ...), condition=%wide.region_9.10_spmd, body=%wide.region_4.9_spmd.sunk | while | flops 417002496 | bytes 44156088 | solution.py:199
  135.1 50.9 %reduce-scatter.17.cloned.1.call-done = f32[512,768]{1,0:T(8,128)} async-done(((f32[2048,768]{1,0:T(8,128)}), f32[512,768]{1,0:T(8,128)}) %reduce-scatter.17.cloned.1.call-update) | async-done | bytes 1572880 | tf_op jit(solution)/shard_map/reduce_scatter | solution.py:207
  185.9 60.9 %reduce-scatter.21.cloned.1.call-done = f32[512,768]{1,0:T(8,128)} async-done(((f32[2048,768]{1,0:T(8,128)}), f32[512,768]{1,0:T(8,128)}) %reduce-scatter.21.cloned.1.call-update) | async-done | bytes 1572880 | tf_op jit(solution)/shard_map/reduce_scatter | solution.py:208
  252.8 28.1 %all-gather.13.cloned.1.call-done = bf16[2048,768]{1,0:T(8,128)(2,1)} async-done(((bf16[512,768]{1,0:T(8,128)(2,1)}), bf16[2048,768]{1,0:T(8,128)(2,1)}) %all-gather.13.cloned.1.call-update) | async-done | bytes 3145744 | tf_op jit(solution)/shard_map/all_gather | solution.py:218
  280.9 7.2 fusion.178
  288.1 23.4 %all-gather.15.cloned.1.call-done = bf16[2048,768]{1,0:T(8,128)(2,1)} async-done(((bf16[512,768]{1,0:T(8,128)(2,1)}), bf16[2048,768]{1,0:T(8,128)(2,1)}) %all-gather.15.cloned.1.call-update) | async-done | bytes 3145744 | tf_op jit(solution)/shard_map/all_gather | solution.py:219
  311.5 31.9 %multiply_convert_fusion.2 = (bf16[2048,768]{1,0:T(8,128)(2,1)}, f32[2048,768]{1,0:T(8,128)}, bf16[2048,768]{1,0:T(8,128)(2,1)S(1)}, f32[2048,768]{1,0:T(8,128)}, f32[2048,768]{1,0:T(8,128)}) fusion(f32[768]{0:T(1024)S(1)} %convert_element_type.298, f32[2048,768]{1,0:T(8,128)} %fusion.178, bf16[2048,768]{1,0:T(8,128)(2,1)} %all-gather.15.cloned.1.call-done, ...), kind=kOutput, calls=%fused_computation.134 | convolution fusion | flops 2623537152 | bytes 35785728 | tf_op jit(solution)/shard_map/dot_general | solution.py:52
  349.6 7.9 fusion.181
  358.2 49.9 %reduce-scatter.19.cloned.1.call-done = f32[512,768]{1,0:T(8,128)} async-done(((f32[2048,768]{1,0:T(8,128)}), f32[512,768]{1,0:T(8,128)}) %reduce-scatter.19.cloned.1.call-update) | async-done | bytes 1572880 | tf_op jit(solution)/shard_map/reduce_scatter | solution.py:229
  408.1 61.1 %reduce-scatter.23.cloned.1.call-done = f32[512,768]{1,0:T(8,128)} async-done(((f32[2048,768]{1,0:T(8,128)}), f32[512,768]{1,0:T(8,128)}) %reduce-scatter.23.cloned.1.call-update) | async-done | bytes 1572880 | tf_op jit(solution)/shard_map/reduce_scatter | solution.py:230
  482.2 26.6 %all-gather.17.cloned.1.call-done = bf16[2048,768]{1,0:T(8,128)(2,1)} async-done(((bf16[512,768]{1,0:T(8,128)(2,1)}), bf16[2048,768]{1,0:T(8,128)(2,1)}) %all-gather.17.cloned.1.call-update) | async-done | bytes 3145744 | tf_op jit(solution)/shard_map/all_gather | solution.py:242
  508.9 7.6 fusion.182
  516.4 22.4 %all-gather.21.cloned.1.call-done = bf16[2048,768]{1,0:T(8,128)(2,1)} async-done(((bf16[512,768]{1,0:T(8,128)(2,1)}), bf16[2048,768]{1,0:T(8,128)(2,1)}) %all-gather.21.cloned.1.call-update) | async-done | bytes 3145744 | tf_op jit(solution)/shard_map/all_gather | solution.py:243
  538.8 17.9 %convert_reduce_fusion = (f32[768]{0:T(1024)}, bf16[2048,768]{1,0:T(8,128)(2,1)}, f32[768]{0:T(1024)}, bf16[2048,768]{1,0:T(8,128)(2,1)S(1)}) fusion(f32[2048,768]{1,0:T(8,128)} %get-tuple-element.593, f32[2048,768]{1,0:T(8,128)} %get-tuple-element.652, f32[768]{0:T(1024)S(1)} %convert_element_type.298, f32[2048,768]{1,0:T(8,128)} %fusion.182, ...), kind=kOutput, calls=%fused_computation.129 | convolution fusion | flops 2469394944 | bytes 42083328 | tf_op jit(solution)/shard_map/dot_general | solution.py:60
  562.9 7.9 fusion.184
  571.0 50.4 %reduce-scatter.25.cloned.1.call-done = f32[512,768]{1,0:T(8,128)} async-done(((f32[2048,768]{1,0:T(8,128)}), f32[512,768]{1,0:T(8,128)}) %reduce-scatter.25.cloned.1.call-update) | async-done | bytes 1572880 | tf_op jit(solution)/shard_map/reduce_scatter | solution.py:255
  621.4 61.0 %reduce-scatter.27.cloned.1.call-done = f32[512,768]{1,0:T(8,128)} async-done(((f32[2048,768]{1,0:T(8,128)}), f32[512,768]{1,0:T(8,128)}) %reduce-scatter.27.cloned.1.call-update) | async-done | bytes 1572880 | tf_op jit(solution)/shard_map/reduce_scatter | solution.py:256
  694.4 26.9 %all-gather.19.cloned.1.call-done = bf16[2048,768]{1,0:T(8,128)(2,1)} async-done(((bf16[512,768]{1,0:T(8,128)(2,1)}), bf16[2048,768]{1,0:T(8,128)(2,1)}) %all-gather.19.cloned.1.call-update) | async-done | bytes 3145744 | tf_op jit(solution)/shard_map/all_gather | solution.py:263
  724.0 27.3 %all-gather.23.cloned.1.call-done = bf16[2048,768]{1,0:T(8,128)(2,1)} async-done(((bf16[512,768]{1,0:T(8,128)(2,1)}), bf16[2048,768]{1,0:T(8,128)(2,1)}) %all-gather.23.cloned.1.call-update) | async-done | bytes 3145744 | tf_op jit(solution)/shard_map/all_gather | solution.py:264
  773.4 120.1 %while.58 = (s32[]{:T(128)}, f32[3,512,512]{1,2,0:T(8,128)}, bf16[4,512,3,64]{1,3,2,0:T(8,128)(2,1)}, bf16[4,512,3,64]{1,3,2,0:T(8,128)(2,1)}, bf16[4,512,3,64]{...) while((s32[]{:T(128)}, f32[3,512,512]{1,2,0:T(8,128)}, ...), condition=%wide.region_35.36_spmd.clone, body=%wide.region_32.35_spmd.clone.sunk | while | flops 1027175424 | bytes 132588392 | solution.py:300
  786.5 8.5 fusion.306
  815.9 9.4 fusion.306
  846.0 9.4 fusion.306
  876.2 9.4 fusion.306
  943.2 40.8 %all-reduce = (f32[768]{0:T(1024)}, f32[768]{0:T(1024)}, f32[768]{0:T(1024)}, f32[768]{0:T(1024)}, f32[768]{0:T(1024)}, /*index=5*/f32[768]{0:T(1024)}) all-reduce(f32[768]{0:T(1024)S(1)} %add.484, f32[768]{0:T(1024)S(1)} %add.485, f32[768]{0:T(1024)S(1)} %add.486, ...), channel_id=1, replica_groups=mesh['dp'=8,'tensor'=4] {'dp','tensor'}, use_global_device_ids=true, to_apply=%region_46.47 | all-reduce | flops 4608 | bytes 36864 | tf_op jit(solution)/shard_map/psum | solution.py:360
  989.9 32.9 %while.57 = (s32[]{:T(128)}, f32[8,32,3]{1,2,0:T(4,128)S(1)}, s32[8,64,512]{2,1,0:T(8,128)}, f32[8,3,64,512]{3,2,0,1:T(8,128)}, s32[]{:T(128)}) while((s32[]{:T(128)}, f32[8,32,3]{1,2,0:T(4,128)S(1)}, s32[8,64,512]{2,1,0:T(8,128)}, f32[8,3,64,512]{3,2,0,1:T(8,128)}, s32[]{:T(128)}) %tuple.218), condition=%wide.region_68.69_spmd, body=%wide.region_67.68_spmd.sunk | while | flops 38797312 | bytes 1574985 | solution.py:98
  1022.9 22.1 %all-reduce.1 = (f32[2,192]{1,0:T(2,128)}, f32[768]{0:T(1024)}, f32[32,3]{0,1:T(4,128)}) all-reduce(f32[2,192]{1,0:T(2,128)S(1)} %pad_maximum_fusion.1, f32[768]{0:T(1024)S(1)} %add.488, f32[32,3]{0,1:T(4,128)S(1)} %reduce_sum.449), channel_id=1, replica_groups=mesh['dp'=8,'tensor'=4] {'dp'}, use_global_device_ids=true, to_apply=%region_42.43 | all-reduce | flops 1248 | bytes 9984 | tf_op jit(solution)/shard_map/psum | solution.py:357
  1051.6 8.2 reduce-scatter.29.cloned.1.call-done
  1062.3 70.8 %reduce-scatter.35.cloned.1.call-done = f32[768,96]{0,1:T(8,128)} async-done(((f32[768,768]{0,1:T(8,128)}), f32[768,96]{0,1:T(8,128)}) %reduce-scatter.35.cloned.1.call-update) | async-done | bytes 294928 | tf_op jit(solution)/shard_map/reduce_scatter | solution.py:355
  1133.1 72.0 %reduce-scatter.33.cloned.1.call-done = f32[96,768]{1,0:T(8,128)} async-done(((f32[768,768]{1,0:T(8,128)}), f32[96,768]{1,0:T(8,128)}) %reduce-scatter.33.cloned.1.call-update) | async-done | bytes 294928 | tf_op jit(solution)/shard_map/reduce_scatter | solution.py:354
  (550 shorter events, 358.3 us)
Async XLA Ops:
  7.2 273.7 %copy-start = (bf16[768,768]{1,0:T(8,128)(2,1)S(1)}, bf16[768,768]{1,0:T(8,128)(2,1)}, u32[]{:S(2)}) copy-start(bf16[768,768]{1,0:T(8,128)(2,1)} %param.41) | copy-start | bytes 3538948
  7.2 33.7 %all-gather.9.cloned.1.call-start = ((), (), s32[]{:S(2)}) async-start(), calls=%async_computation.12 | async-start | bytes 3932160 | tf_op jit(solution)/shard_map/all_gather | solution.py:167
  7.9 63.1 %all-gather.11.cloned.1.call-start = ((), (), s32[]{:S(2)}) async-start(), calls=%async_computation.13 | async-start | bytes 3932160 | tf_op jit(solution)/shard_map/all_gather | solution.py:168
  8.7 177.3 %reduce-scatter.17.cloned.1.call-start = ((), (), s32[]{:S(2)}) async-start(), calls=%async_computation.14 | async-start | bytes 7864320 | tf_op jit(solution)/shard_map/reduce_scatter | solution.py:207
  127.4 119.4 %reduce-scatter.21.cloned.1.call-start = ((), (), s32[]{:S(2)}) async-start(), calls=%async_computation.17 | async-start | bytes 7864320 | tf_op jit(solution)/shard_map/reduce_scatter | solution.py:208
  134.4 112.5 %copy-start.38 = (bf16[512,768]{1,0:T(8,128)(2,1)S(1)}, bf16[512,768]{1,0:T(8,128)(2,1)}, u32[]{:S(2)}) copy-start(bf16[512,768]{1,0:T(8,128)(2,1)} %param.28) | copy-start | bytes 2359300
  134.4 112.5 %copy-start.39 = (bf16[512,768]{1,0:T(8,128)(2,1)S(1)}, bf16[512,768]{1,0:T(8,128)(2,1)}, u32[]{:S(2)}) copy-start(bf16[512,768]{1,0:T(8,128)(2,1)} %param.29) | copy-start | bytes 2359300
  134.4 146.5 %all-gather.13.cloned.1.call-start = ((), (), s32[]{:S(2)}) async-start(), calls=%async_computation.15 | async-start | bytes 3932160 | tf_op jit(solution)/shard_map/all_gather | solution.py:218
  252.2 59.3 %all-gather.15.cloned.1.call-start = ((), (), s32[]{:S(2)}) async-start(), calls=%async_computation.18 | async-start | bytes 3932160 | tf_op jit(solution)/shard_map/all_gather | solution.py:219
  252.8 155.3 %reduce-scatter.19.cloned.1.call-start = ((), (), s32[]{:S(2)}) async-start(), calls=%async_computation.16 | async-start | bytes 7864320 | tf_op jit(solution)/shard_map/reduce_scatter | solution.py:229
  349.6 119.6 %reduce-scatter.23.cloned.1.call-start = ((), (), s32[]{:S(2)}) async-start(), calls=%async_computation.19 | async-start | bytes 7864320 | tf_op jit(solution)/shard_map/reduce_scatter | solution.py:230
  357.5 111.7 %copy-start.31 = (bf16[512,768]{1,0:T(8,128)(2,1)S(1)}, bf16[512,768]{1,0:T(8,128)(2,1)}, u32[]{:S(2)}) copy-start(bf16[512,768]{1,0:T(8,128)(2,1)} %get-tuple-element.631) | copy-start | bytes 2359300
  357.5 111.7 %copy-start.32 = (bf16[512,768]{1,0:T(8,128)(2,1)S(1)}, bf16[512,768]{1,0:T(8,128)(2,1)}, u32[]{:S(2)}) copy-start(bf16[512,768]{1,0:T(8,128)(2,1)} %get-tuple-element.632) | copy-start | bytes 2359300
  357.5 151.3 %all-gather.17.cloned.1.call-start = ((), (), s32[]{:S(2)}) async-start(), calls=%async_computation.20 | async-start | bytes 3932160 | tf_op jit(solution)/shard_map/all_gather | solution.py:242
  480.1 58.7 %all-gather.21.cloned.1.call-start = ((), (), s32[]{:S(2)}) async-start(), calls=%async_computation.23 | async-start | bytes 3932160 | tf_op jit(solution)/shard_map/all_gather | solution.py:243
  481.9 139.5 %reduce-scatter.25.cloned.1.call-start = ((), (), s32[]{:S(2)}) async-start(), calls=%async_computation.21 | async-start | bytes 7864320 | tf_op jit(solution)/shard_map/reduce_scatter | solution.py:255
  562.9 119.5 %reduce-scatter.27.cloned.1.call-start = ((), (), s32[]{:S(2)}) async-start(), calls=%async_computation.24 | async-start | bytes 7864320 | tf_op jit(solution)/shard_map/reduce_scatter | solution.py:256
  570.9 111.5 %copy-start.10 = (f32[512,768]{1,0:T(8,128)S(1)}, f32[512,768]{1,0:T(8,128)}, u32[]{:S(2)}) copy-start(f32[512,768]{1,0:T(8,128)} %copy-done.9) | copy-start | bytes 4718596
  570.9 111.5 %copy-start.53 = (f32[512]{0:T(512)S(1)}, f32[512]{0:T(512)}, u32[]{:S(2)}) copy-start(f32[512]{0:T(512)} %copy-done.52) | copy-start | bytes 6148
  570.9 111.5 %copy-start.55 = (f32[512]{0:T(512)S(1)}, f32[512]{0:T(512)}, u32[]{:S(2)}) copy-start(f32[512]{0:T(512)} %copy-done.54) | copy-start | bytes 6148
  570.9 111.5 %copy-start.57 = (f32[768]{0:T(1024)S(1)}, f32[768]{0:T(1024)}, u32[]{:S(2)}) copy-start(f32[768]{0:T(1024)} %param.39) | copy-start | bytes 9220
  570.9 111.5 %copy-start.59 = (f32[512]{0:T(512)S(1)}, f32[512]{0:T(512)}, u32[]{:S(2)}) copy-start(f32[512]{0:T(512)} %copy-done.58) | copy-start | bytes 6148
  570.9 116.7 %copy-start.69 = (f32[512]{0:T(512)S(1)}, f32[512]{0:T(512)}, u32[]{:S(2)}) copy-start(f32[512]{0:T(512)} %copy-done.68) | copy-start | bytes 6148
  570.9 116.7 %copy-start.67 = (f32[512]{0:T(512)S(1)}, f32[512]{0:T(512)}, u32[]{:S(2)}) copy-start(f32[512]{0:T(512)} %copy-done.66) | copy-start | bytes 6148
  571.0 150.3 %all-gather.19.cloned.1.call-start = ((), (), s32[]{:S(2)}) async-start(), calls=%async_computation.22 | async-start | bytes 3932160 | tf_op jit(solution)/shard_map/all_gather | solution.py:263
  692.6 58.7 %all-gather.23.cloned.1.call-start = ((), (), s32[]{:S(2)}) async-start(), calls=%async_computation.25 | async-start | bytes 3932160 | tf_op jit(solution)/shard_map/all_gather | solution.py:264
  694.4 350.6 %reduce-scatter.39.cloned.1.call-start = ((), (), s32[]{:S(2)}) async-start(), calls=%async_computation.31 | async-start | bytes 884736
  755.1 291.5 %reduce-scatter.37.cloned.1.call-start = ((), (), s32[]{:S(2)}) async-start(), calls=%async_computation.30 | async-start | bytes 2211840
  912.8 135.8 %reduce-scatter.31.cloned.1.call-start = ((), (), s32[]{:S(2)}) async-start(), calls=%async_computation.27 | async-start | bytes 3932160 | tf_op jit(solution)/shard_map/reduce_scatter | solution.py:345
  916.4 143.4 %reduce-scatter.29.cloned.1.call-start = ((), (), s32[]{:S(2)}) async-start(), calls=%async_computation.26 | async-start | bytes 3932160 | tf_op jit(solution)/shard_map/reduce_scatter | solution.py:342
  922.5 210.5 %reduce-scatter.35.cloned.1.call-start = ((), (), s32[]{:S(2)}) async-start(), calls=%async_computation.29 | async-start | bytes 2654208 | tf_op jit(solution)/shard_map/reduce_scatter | solution.py:355
  932.7 272.4 %reduce-scatter.33.cloned.1.call-start = ((), (), s32[]{:S(2)}) async-start(), calls=%async_computation.28 | async-start | bytes 2654208 | tf_op jit(solution)/shard_map/reduce_scatter | solution.py:354
  (111 other events, 883.2 us)
Sparse Core Ops, SparseCore 0:
  9.6 31.2 all-gather.8
  42.4 28.5 all-gather.10
  127.6 58.3 reduce-scatter.16
  188.5 58.3 reduce-scatter.20
  252.3 28.5 all-gather.12
  282.9 28.5 all-gather.14
  349.7 58.3 reduce-scatter.18
  410.8 58.3 reduce-scatter.22
  480.3 28.5 all-gather.16
  510.3 28.5 all-gather.20
  563.0 58.3 reduce-scatter.24
  624.0 58.3 reduce-scatter.26
  692.7 28.5 all-gather.18
  722.7 28.5 all-gather.22
  755.3 62.5 reduce-scatter.38
  912.9 66.8 reduce-scatter.36
  982.1 37.1 reduce-scatter.30
  1021.9 37.9 reduce-scatter.28
  1063.9 69.1 reduce-scatter.34
  1137.0 68.0 reduce-scatter.32
where the time goes:
time: 1220 us; the launch traced here: 1210 us
  waiting for transfers between devices  663 us (54%)
  matrix products  284 us (23%)
  local copies, waits for them, and re-layouts  97.8 us (8%)
  other arithmetic  85.7 us (7%)
  blocking collectives  62.9 us (5%)
  between operations  16.1 us (1%)
    dot_general x10, matrix products, plain_dot(): return jnp.dot(rows_in, weight, preferred_element_type=jnp.float32)  72.2 us
    reduce_scatter x1, waiting for transfers between devices, local(): lax.psum_scatter(grad_w_in_part, 'dp', scatter_dimension=0, tiled=True)  72 us
    reduce_scatter x1, waiting for transfers between devices, local(): lax.psum_scatter(grad_w_out_part, 'dp', scatter_dimension=1, tiled=True)  70.8 us
    reduce_scatter x1, waiting for transfers between devices, local(): lax.psum_scatter(ffn_g, 'tensor', scatter_dimension=0, tiled=True)  61.1 us
    reduce_scatter x1, waiting for transfers between devices, local(): lax.psum_scatter(dhid_g, 'tensor', scatter_dimension=0, tiled=True)  61 us
    reduce_scatter x1, waiting for transfers between devices, local(): lax.psum_scatter(proj_g, 'tensor', scatter_dimension=0, tiled=True)  60.9 us
    dot_general x10, matrix products, back_dot(): lax.dot_general(grad_rows, weight, CONTRACT_COLS, preferred_element_type=...  54.4 us
    reduce_scatter x1, waiting for transfers between devices, local(): lax.psum_scatter(proj_c, 'tensor', scatter_dimension=0, tiled=True)  50.9 us
  transfers between devices with their start and end apart: 20, of which 17 were waited for; matrix products, arithmetic and copies ran while one was open for 26% of the time, Pallas kernels for 0%

commit v1 on v0

v1 whole, which is shorter than its diff:
```python
import functools

import jax
import jax.numpy as jnp
from jax import lax
from jax.experimental import pallas as pl
from jax.experimental.pallas import tpu as pltpu
from jax.sharding import PartitionSpec as P

EDGES = (1, 2, 3, 4, 5, 6, 7, 8, 12, 16, 23, 32, 46, 64, 91)
EPSILON = 1e-05
F32 = jnp.float32
BF16 = jnp.bfloat16
S = 512
HALF = 256
D = 768
HD = 64
SLOTS = 4
SLOT_HEADS = 3
QW = SLOT_HEADS * HD
NEGATIVE = -1e30
ROWS = D // 8
HROWS = D // 2
MESH = pl.DeviceIdType.MESH


def nn(a, b):
    return jnp.dot(a, b, preferred_element_type=F32)


def nt(a, b):
    return lax.dot_general(a, b, (((1,), (1,)), ((), ())), preferred_element_type=F32)


def tn(a, b):
    return lax.dot_general(a, b, (((0,), (0,)), ((), ())), preferred_element_type=F32)


def iota(shape, axis):
    return lax.broadcasted_iota(jnp.int32, shape, axis)


def bucket_onehot():
    lanes = iota((32, S), 1)
    offset = jnp.where(lanes < HALF, -lanes, S - lanes)
    distance = jnp.abs(offset)
    bucket = jnp.where(offset > 0, 16, 0)
    for edge in EDGES:
        bucket = bucket + (distance >= edge).astype(jnp.int32)
    return (bucket == iota((32, S), 0)).astype(F32)


def gelu_pair(v):
    cdf = 0.5 + 0.5 * lax.erf(v * 0.7071067811865476)
    return v * cdf, cdf + v * (jnp.exp(-0.5 * v * v) * 0.3989422804014327)


def row_mean(v):
    return jnp.sum(v, axis=-1, keepdims=True) * (1.0 / D)


def col_sum(v):
    return jnp.sum(v, axis=0, keepdims=True)


def kernel(
    stride,
    dl, pc, rank, x_hbm, g_hbm, cc_hbm, cg_hbm, wq_in, wo_in, wi_in, w2_in, sm_in, vectors,
    oc_hbm, og_hbm, gc_hbm, gg_hbm, stash, g_res, sm_res,
    perm, unperm, xin, hid, tA, tB, attn, qkv, qg, xhat, rstd1, act, dg, acc,
    mask, square, lines, wq, wo, wi, w2, wsm,
    ga, gb, rca, rcb, rxa, ryb, smx, smy, smz, smw, r1, r2, r3, r4,
    lsem, xs, xr, cs, cr, ss, sr, os, orr, ps, pr, credit,
):
    b_attn, n1g, n1s, b_out, n2g, n2s = (vectors.at[k:k + 1] for k in range(6))
    bias = dsacc = square
    text = diag = lines
    t = lax.axis_index("tensor")
    d = lax.axis_index("dp")
    yb = lax.rem(lax.div(d, stride), 2)
    zb = lax.rem(lax.div(d, 2 * stride), 4)
    zbit = lax.rem(zb, 2)
    z_of = (zb, zb + 1 - 2 * zbit, lax.rem(zb + 2, 4), 3 - zb)
    core = (d, t + 1 - 2 * lax.rem(t, 2))
    xdev = (d, lax.rem(t + 2, 4))
    diagonal = (d, 3 - t)
    ydev = (d + stride - 2 * stride * yb, t)
    zdev = [None] + [(d + 2 * stride * (z_of[k] - zb), t) for k in (1, 2, 3)]

    barrier = pltpu.get_barrier_semaphore()
    for who in (core, xdev, diagonal, ydev, zdev[1], zdev[2], zdev[3]):
        pl.semaphore_signal(barrier, inc=1, device_id=who, device_id_type=MESH)
    pl.semaphore_wait(barrier, 7)

    def remote(src, dst, send, recv, who):
        return pltpu.make_async_remote_copy(
            src_ref=src, dst_ref=dst, send_sem=send, recv_sem=recv, device_id=who, device_id_type=MESH
        )

    parts = (
        (wq_in, lambda s, lo, n: wq.at[s, pl.ds(lo, n)], 3 * QW, 2),
        (wo_in, lambda s, lo, n: wo.at[pl.ds(s * QW + lo, n)], QW, 1),
        (wi_in, lambda s, lo, n: wi.at[s, pl.ds(lo, n)], D, 2),
        (w2_in, lambda s, lo, n: w2.at[s, pl.ds(lo, n)], D, 2),
    )
    items = []
    for p, (_, _, n, count) in enumerate(parts):
        for i in range(count):
            items.append((p, n // 2, i * (n // 2 // count), n // 2 // count))

    def mine(i, other):
        p, half, lo, n = items[i]
        return pl.multiple_of((1 - yb if other else yb) * half + lo, 16), n

    def x_copy(i):
        src, place, _, _ = parts[items[i][0]]
        lo, n = mine(i, False)
        return remote(src.at[pl.ds(lo, n)], place(2, lo, n), xs.at[i, 0], xr.at[i, 0], xdev)

    def y_copy(i):
        place = parts[items[i][0]][1]
        lo, n = mine(i, False)
        return remote(place(2, lo, n), place(2, lo, n), xs.at[i, 1], xr.at[i, 1], ydev)

    def c_copy(i, other):
        place = parts[items[i][0]][1]
        lo, n = mine(i, other)
        k = 3 if other else 2
        return remote(place(2, lo, n), place(3, lo, n), xs.at[i, k], xr.at[i, k], core)

    def core_copy(p):
        src, place, n, _ = parts[p]
        return remote(src, place(1, 0, n), cs.at[p], cr.at[p], core)

    def small_copy(k):
        return remote(sm_in, wsm.at[k], ss.at[k - 1], sr.at[k - 1], (core, xdev, diagonal)[k - 1])

    def own_copy(p):
        src, place, n, _ = parts[p]
        return pltpu.make_async_copy(src, place(0, 0, n), lsem.at[2 + p])

    def small_own():
        return pltpu.make_async_copy(sm_in, wsm.at[0], lsem.at[6])

    def arrived_x(i):
        x_copy(i).wait_recv()
        y_copy(i).start()
        c_copy(i, False).start()

    def arrived_y(i):
        y_copy(i).wait_recv()
        c_copy(i, True).start()

    def arrived_core(i):
        c_copy(i, False).wait_recv()
        c_copy(i, True).wait_recv()

    def fetch(one, two):
        return [
            pltpu.make_async_copy(one, xin.at[0:S], lsem.at[0]),
            pltpu.make_async_copy(two, xin.at[S:2 * S], lsem.at[1]),
        ]

    def stash_copy(s, back):
        ends = (stash.at[s], dg.at[s]) if back else (dg.at[s], stash.at[s])
        return pltpu.make_async_copy(ends[0], ends[1], lsem.at[7 + s])

    small_own().start()
    own_copy(0).start()
    rows_in = fetch(x_hbm, g_hbm)
    for copy in rows_in:
        copy.start()
    for k in (1, 2, 3):
        small_copy(k).start()
    core_copy(0).start()
    for i in range(len(items)):
        x_copy(i).start()
    for p in (1, 2, 3):
        core_copy(p).start()
        own_copy(p).start()

    end = jnp.int32(0)
    start = jnp.int32(0)
    ends = []
    for k in range(8):
        length = dl[t, k]
        start = jnp.where(length == HALF, end, start)
        end = end + length
        ends.append(end)
    limit = (S - pc[t]).astype(F32)
    rows = iota((S, 1), 0)
    lanes = iota((1, S), 1)
    source_r = (rows + start) & (S - 1)
    source_l = (lanes + start) & (S - 1)
    perm[...] = jnp.where(source_r == lanes, 1.0, 0.0).astype(BF16)
    unperm[...] = jnp.where(((rows - start) & (S - 1)) == lanes, 1.0, 0.0).astype(BF16)
    doc_r = jnp.zeros((S, 1), F32)
    doc_l = jnp.zeros((1, S), F32)
    for e in ends:
        doc_r = doc_r + jnp.where(source_r >= e, 1.0, 0.0)
        doc_l = doc_l + jnp.where(source_l >= e, 1.0, 0.0)
    rank_row = rank[pl.ds(t, 1), :]
    sub = iota((16, S), 0)
    pieces = jnp.where(sub == 0, rank_row >> 4, jnp.where(sub == 1, rank_row & 15, 0))
    pieces = pieces.astype(F32).astype(BF16)
    ranks = nt(pieces, perm[...])
    rank_l = 16.0 * ranks[0:1] + ranks[1:2]
    ranks = nt(perm[...], pieces)
    rank_r = 16.0 * ranks[:, 0:1] + ranks[:, 1:2]
    lim_c = jnp.maximum(limit - 1.0, rank_l)
    lim_g = jnp.maximum(limit, rank_l) - 1.0
    for b in range(2):
        c = slice(HALF * b, HALF * b + HALF)
        same = doc_r[c] == doc_l[:, c]
        mask[b, :, 0:HALF] = jnp.where(same & (rank_r[c] <= lim_c[:, c]), 0.0, NEGATIVE).astype(BF16)
        mask[b, :, HALF:S] = jnp.where(same & (rank_r[c] <= lim_g[:, c]), 0.0, NEGATIVE).astype(BF16)
    onehot = bucket_onehot()
    smx[...] = jnp.zeros(smx.shape, F32)

    def transposed(dst, src):
        for st in range(2):
            r = slice(st * S, st * S + S)
            flipped = src[r].T
            for k in range(8):
                to = (k % 2) * 4 * ROWS + (k // 2) * ROWS
                dst[to:to + ROWS, r] = flipped[k * ROWS:k * ROWS + ROWS]

    def permuted(dst):
        for copy in rows_in:
            copy.wait()
        for st in range(2):
            r = slice(st * S, st * S + S)
            for f in (slice(0, HROWS), slice(HROWS, D)):
                dst[r, f] = nn(perm[...], xin[r, f]).astype(BF16)

    xp = hid
    permuted(xp)
    small_own().wait()
    own_copy(0).wait()

    def prob_at(s, h, b, st):
        k = 2 * b + st
        return dg.at[s, k * HALF:k * HALF + HALF, pl.ds(pl.multiple_of(h * HALF, HALF), HALF)]

    @pl.loop(0, SLOTS)
    def _(s):
        @pl.when(s == 1)
        def _():
            core_copy(0).wait_recv()
            small_copy(1).wait_recv()
            arrived_x(0)

        @pl.when(s == 2)
        def _():
            arrived_x(1)
            small_copy(2).wait_recv()
            arrived_y(0)
            arrived_y(1)

        @pl.when(s == 3)
        def _():
            arrived_x(2)
            small_copy(3).wait_recv()
            arrived_core(0)
            arrived_core(1)

        small = wsm[s].astype(BF16)
        table = nn(small[:, 0:32], onehot.astype(BF16))
        text[pl.ds(pl.multiple_of(8 * s, 8), 8), :] = table[3:11]
        sel = jnp.where(iota((16, 128), 0) == 1, 1.0, 0.0).astype(BF16)
        bq = tn(small[:, 0:QW], sel)[:, 0:1]
        sel = jnp.where(iota((16, 128), 0) == 2, 1.0, 0.0).astype(BF16)
        bv = tn(small[:, 0:QW], sel)[:, 0:1]
        r = nt(wq[s], xp[0:S])
        qkv[s, 0:QW] = ((r[0:QW] + bq).astype(BF16) * 0.125).astype(BF16)
        qkv[s, QW:2 * QW] = r[QW:2 * QW].astype(BF16)
        qkv[s, 2 * QW:3 * QW] = (r[2 * QW:3 * QW] + bv).astype(BF16)
        qg[s] = ((nt(wq[s, 0:QW], xp[S:2 * S]) + bq).astype(BF16) * 0.125).astype(BF16)

        @pl.loop(0, SLOT_HEADS)
        def _(h):
            hr = pl.multiple_of(h * HD, HD)
            rowvec = text[pl.ds(8 * s + h, 1), :]
            rolled = pltpu.roll(jnp.broadcast_to(rowvec, (HALF, S)), 0, 1, stride=1, stride_axis=0)
            bias[...] = rolled[:, 0:HALF]
            for b in range(2):
                c = slice(HALF * b, HALF * b + HALF)
                kT = qkv[s, pl.ds(QW + hr, HD), c]
                vT = qkv[s, pl.ds(2 * QW + hr, HD), c]
                for st in range(2):
                    qT = qkv[s, pl.ds(hr, HD), c] if st == 0 else qg[s, pl.ds(hr, HD), c]
                    l = slice(HALF * st, HALF * st + HALF)
                    sc = tn(kT, qT) + bias[...] + mask[b, :, l].astype(F32)
                    e = jnp.exp(sc - jnp.max(sc, axis=0, keepdims=True))
                    p = (e * (1.0 / jnp.sum(e, axis=0, keepdims=True))).astype(BF16)
                    prob_at(s, h, b, st)[...] = p
                    to = slice(st * S + HALF * b, st * S + HALF * b + HALF)
                    tA[pl.ds(pl.multiple_of(s * QW + hr, HD), HD), to] = nn(vT, p).astype(BF16)

        for k in range(SLOTS):
            @pl.when(s == k)
            def _():
                stash_copy(k, False).start()

    arrived_y(2)
    own_copy(1).wait()
    core_copy(1).wait_recv()
    for st in range(2):
        r = slice(st * S, st * S + S)
        attn[r] = nt(unperm[...], tA[:, r]).astype(BF16)
    arrived_core(2)
    for r in (slice(k * HALF, k * HALF + HALF) for k in range(4)):
        res = xin[r].astype(F32) + nn(attn[r], wo[...]) + b_attn[...]
        cen = res - row_mean(res)
        rs = lax.rsqrt(row_mean(cen * cen) + EPSILON)
        xh = cen * rs
        xhat[r] = xh.astype(BF16)
        rstd1[r] = rs
        hid[r] = (xh * n1g[...] + n1s[...]).astype(BF16)
    transposed(tB, hid)
    rows_in = fetch(cc_hbm, cg_hbm)
    for copy in rows_in:
        copy.start()

    own_copy(2).wait()
    own_copy(3).wait()

    @pl.loop(0, SLOTS)
    def _(s):
        @pl.when(s == 0)
        def _():
            arrived_x(3)

        @pl.when(s == 1)
        def _():
            core_copy(2).wait_recv()

        @pl.when(s == 2)
        def _():
            arrived_x(4)
            arrived_y(3)
            arrived_y(4)

        @pl.when(s == 3)
        def _():
            arrived_x(5)
            arrived_core(3)
            arrived_core(4)

        for k in range(SLOTS):
            @pl.when(s == k)
            def _():
                stash_copy(k, False).wait()
        for st in range(2):
            r = slice(st * S, st * S + S)
            for j in range(0, D, 256):
                pre = nn(hid[r], wi[s, :, j:j + 256]) + wsm[s, 0:1, j:j + 256]
                a, g = gelu_pair(pre)
                act[s, r, j:j + 256] = a.astype(BF16)
                dg[s, r, j:j + 256] = g.astype(BF16)

    for r in (slice(0, S), slice(S, 2 * S)):
        acc[r] = nn(act[0, r], w2[0])

    @pl.loop(1, SLOTS)
    def _(s):
        @pl.when(s == 1)
        def _():
            core_copy(3).wait_recv()

        @pl.when(s == 2)
        def _():
            arrived_x(6)
            arrived_y(5)
            arrived_y(6)

        @pl.when(s == 3)
        def _():
            arrived_core(5)
            arrived_core(6)

        for r in (slice(0, S), slice(S, 2 * S)):
            acc[r] += nn(act[s, r], w2[s])

    for copy in rows_in:
        copy.wait()

    @pl.loop(0, 4)
    def _(i):
        r = pl.ds(pl.multiple_of(i * HALF, HALF), HALF)
        res = hid[r, :].astype(F32) + acc[r, :] + b_out[...]
        cen = res - row_mean(res)
        rs = lax.rsqrt(row_mean(cen * cen) + EPSILON)
        xh = cen * rs
        cot = xin[r, :].astype(F32)
        hid[r, :] = (xh * n2g[...] + n2s[...]).astype(BF16)
        dxh = cot * n2g[...]
        dres = rs * (dxh - row_mean(dxh) - xh * row_mean(dxh * xh))
        acc[r, :] = dres
        xin[r, :] = dres.astype(BF16)
        smx[2, 3:4] += col_sum(dres)
        smx[2, 4:5] += col_sum(cot * xh)
        smx[2, 5:6] += col_sum(cot)

    dlow = xin
    transposed(tA, dlow)
    rows_out = [
        pltpu.make_async_copy(hid.at[0:S], oc_hbm, lsem.at[0]),
        pltpu.make_async_copy(hid.at[S:2 * S], og_hbm, lsem.at[1]),
    ]
    for copy in rows_out:
        copy.start()

    own_half = pl.ds(pl.multiple_of(yb * HROWS, HROWS), HROWS)
    other_half = pl.ds(pl.multiple_of((1 - yb) * HROWS, HROWS), HROWS)

    def block(k):
        return pl.ds(pl.multiple_of(yb * HROWS + z_of[k] * ROWS, ROWS), ROWS)

    def add(dst, src, rows_d=None, rows_s=None):
        count = dst.shape[0] if rows_d is None else HROWS

        @pl.loop(0, count // ROWS)
        def _(i):
            step = pl.multiple_of(i * ROWS, ROWS)
            a = pl.ds(step + (0 if rows_d is None else rows_d.start), ROWS)
            b = pl.ds(step + (0 if rows_s is None else rows_s.start), ROWS)
            dst[a, :] = (dst[a, :].astype(F32) + src[b, :].astype(F32)).astype(BF16)

    def rz_at(n, k, cols):
        return wi.at[(0, 1, 3, 3)[n], (k - 1) * ROWS:k * ROWS, cols]

    class Chunk:
        def __init__(self, index, even, odd, rc, rx, ry, cols, x_first):
            self.n, self.even, self.odd, self.rc = index, even, odd, rc
            self.rx, self.ry, self.cols, self.x_first = rx, ry, cols, x_first

        def sems(self, k):
            return os.at[self.n, k], orr.at[self.n, k]

        def core_send(self, k):
            return remote(self.odd[k], self.rc[k], *self.sems(k), core)

        def x_send(self):
            if self.x_first:
                return remote(self.even[1], self.rx, *self.sems(2), xdev)
            return remote(self.even[1].at[own_half], self.rx, *self.sems(2), xdev)

        def y_send(self, k):
            return remote(self.even[k].at[other_half], self.ry[k], *self.sems(3 + k), ydev)

        def z_send(self, k):
            return remote(
                self.even[0].at[block(k)], rz_at(self.n, k, self.cols), *self.sems(4 + k), zdev[k]
            )

        def core_sum(self, k):
            self.core_send(k).wait_recv()
            add(self.even[k], self.rc[k])
            if self.x_first:
                if k == 1:
                    self.x_send().start()
            else:
                self.y_send(k).start()

        def middle(self):
            if self.x_first:
                self.x_send().wait_recv()
                add(self.even[0], self.rx)
                self.y_send(0).start()
            else:
                self.y_send(1).wait_recv()
                add(self.even[1], self.ry[1], own_half)
                self.x_send().start()

        def last(self):
            self.y_send(0).wait_recv()
            add(self.even[0], self.ry[0], own_half)
            if not self.x_first:
                self.x_send().wait_recv()
                add(self.even[0], self.rx, own_half)
            for k in (1, 2, 3):
                self.z_send(k).start()

        def finish(self, out):
            total = self.even[0][block(0), :].astype(F32)
            for k in (1, 2, 3):
                self.z_send(k).wait_recv()
                total = total + rz_at(self.n, k, self.cols)[...].astype(F32)
            g_res[out, :, self.cols] = total

        def sent(self):
            for k in (0, 1) if self.n > 1 else (0,):
                self.core_send(k).wait_send()
            self.x_send().wait_send()
            self.y_send(0).wait_send()
            if not self.x_first:
                self.y_send(1).wait_send()
            for k in (1, 2, 3):
                self.z_send(k).wait_send()

    whole = pl.ds(0, D)
    first, second = pl.ds(0, D // 2), pl.ds(D // 2, D // 2)
    A = Chunk(0, (ga.at[0], ga.at[1]), (ga.at[2], ga.at[2]), (rca.at[0], rca.at[1]), rxa, (w2.at[0, HROWS:D], None), whole, True)
    B = Chunk(1, (gb.at[0], gb.at[1]), (gb.at[2], gb.at[2]), (rcb.at[0], rcb.at[1]), w2.at[0, 0:HROWS], (ryb.at[0], ryb.at[1]), whole, False)

    def c_part(index, cols, x_first):
        g = lambda s: act.at[s, 0:D, cols]
        r = lambda ref: ref.at[:, cols]
        if x_first:
            rx, ry = w2.at[1, :, cols], (w2.at[3, 0:HROWS, cols], None)
        else:
            rx, ry = w2.at[1, 0:HROWS, cols], (w2.at[3, 0:HROWS, cols], w2.at[3, HROWS:D, cols])
        return Chunk(index, (g(0), g(2)), (g(1), g(3)), (r(rca.at[0]), r(rca.at[1])), rx, ry, cols, x_first)

    C1 = c_part(2, first, True)
    C2 = c_part(3, second, False)

    def buffer_of(s):
        odd = lax.rem(s, 2)
        return 2 * odd + (1 - odd) * lax.div(s, 2)

    def after(chunks, s):
        for k in (1, 0):
            @pl.when(s == 2 * k + 1)
            def _():
                for chunk in chunks:
                    chunk.core_send(k).start()

            @pl.when(s == 2 * k)
            def _():
                for chunk in chunks:
                    chunk.core_sum(k)

    @pl.loop(0, SLOTS)
    def _(i):
        s = 3 - i

        @pl.when(s == 1)
        def _():
            A.core_send(1).wait_send()

        for r in (slice(0, HROWS), slice(HROWS, D)):
            ga[buffer_of(s), r] = nn(tA[r], act[s]).astype(BF16)
        after((A,), s)

    @pl.loop(0, SLOTS)
    def _(i):
        s = 3 - i
        place = lax.rem(s, 2) * lax.div(s, 2) + (1 - lax.rem(s, 2)) * (3 + lax.div(s, 2))
        for j in range(0, D, 256):
            part = jnp.zeros((1, 256), F32)
            for st in range(2):
                r = slice(st * S, st * S + S)
                dact = nt(dlow[r], w2[s, j:j + 256, :])
                low = (dact * dg[s, r, j:j + 256].astype(F32)).astype(BF16)
                dg[s, r, j:j + 256] = low
                part = part + col_sum(low.astype(F32))
            smx[place, 0:1, j:j + 256] = part

        @pl.when(s == 1)
        def _():
            B.core_send(1).wait_send()

        for r in (slice(0, HROWS), slice(HROWS, D)):
            gb[buffer_of(s), r] = nn(tB[r], dg[s]).astype(BF16)
        after((B,), s)
        for r in (slice(0, S), slice(S, 2 * S)):
            acc[r] += nt(dg[s, r], wi[s])
        for k in range(SLOTS):
            @pl.when(s == k)
            def _():
                stash_copy(k, True).start()

    for k, who in enumerate((core, xdev, ydev, zdev[1], zdev[2], zdev[3])):
        pl.semaphore_signal(credit.at[k], inc=1, device_id=who, device_id_type=MESH)

    @pl.loop(0, 4)
    def _(i):
        r = pl.ds(pl.multiple_of(i * HALF, HALF), HALF)
        dy = acc[r, :]
        xh = xhat[r, :].astype(F32)
        dxh = dy * n1g[...]
        dres = rstd1[r, :] * (dxh - row_mean(dxh) - xh * row_mean(dxh * xh))
        acc[r, :] = dres
        xin[r, :] = dres.astype(BF16)
        smx[2, 0:1] += col_sum(dres)
        smx[2, 1:2] += col_sum(dy * xh)
        smx[2, 2:3] += col_sum(dy)

    transposed(tB, dlow)
    for r in (slice(0, HROWS), slice(HROWS, D)):
        tA[r] = nt(wo[r], dlow[...]).astype(BF16)
    for copy in rows_out:
        copy.wait()
    rows_in = fetch(x_hbm, g_hbm)
    for copy in rows_in:
        copy.start()
    for k in range(6):
        pl.semaphore_wait(credit.at[k], 1)
    B.middle()
    for r in (slice(0, HROWS), slice(HROWS, D)):
        gwo = nn(tB[r], attn[...]).astype(BF16)
        for s in range(SLOTS):
            act[s, r, 3 * QW:D] = gwo[:, s * QW:s * QW + QW]
    for st in range(2):
        r = slice(st * S, st * S + S)
        for f in (slice(0, HROWS), slice(HROWS, D)):
            tA[f, r] = nt(tA[f, r], perm[...]).astype(BF16)
    permuted(attn)
    transposed(tB, attn)
    xpT = tB

    ones = jnp.ones((16, S), BF16)
    @pl.loop(0, SLOTS)
    def _(i):
        s = 3 - i
        for k in range(SLOTS):
            @pl.when(s == k)
            def _():
                stash_copy(k, True).wait()

        @pl.loop(0, SLOT_HEADS)
        def _(h):
            hr = pl.multiple_of(h * HD, HD)
            for b in range(2):
                c = slice(HALF * b, HALF * b + HALF)
                kT = qkv[s, pl.ds(QW + hr, HD), c]
                vT = qkv[s, pl.ds(2 * QW + hr, HD), c]
                dk = dv = None
                for st in range(2):
                    qT = qkv[s, pl.ds(hr, HD), c] if st == 0 else qg[s, pl.ds(hr, HD), c]
                    dOT = tA[pl.ds(pl.multiple_of(s * QW + hr, HD), HD), st * S + HALF * b:st * S + HALF * b + HALF]
                    p = prob_at(s, h, b, st)[...]
                    pf = p.astype(F32)
                    dp = tn(vT, dOT)
                    dsl = (pf * (dp - jnp.sum(dp * pf, axis=0, keepdims=True))).astype(BF16)
                    if b == 0 and st == 0:
                        dsacc[...] = dsl.astype(F32)
                    else:
                        dsacc[...] += dsl.astype(F32)
                    dq = (nn(kT, dsl) * 0.125).astype(BF16)
                    dk1 = nt(qT, dsl)
                    dv1 = nt(dOT, p)
                    dk = dk1 if dk is None else dk + dk1
                    dv = dv1 if dv is None else dv + dv1
                    if st == 0:
                        qkv[s, pl.ds(hr, HD), c] = dq
                    else:
                        qg[s, pl.ds(hr, HD), c] = dq
                qkv[s, pl.ds(QW + hr, HD), c] = dk.astype(BF16)
                qkv[s, pl.ds(2 * QW + hr, HD), c] = dv.astype(BF16)
            total = jnp.zeros((8, S), F32)
            for a in range(HALF // 8):
                wide = jnp.concatenate([dsacc[8 * a:8 * a + 8, :], jnp.zeros((8, HALF), F32)], axis=1)
                total = total + (wide if a == 0 else pltpu.roll(wide, S - 8 * a, 1))
            flipped = jnp.concatenate([total[7 - i:8 - i] for i in range(8)], axis=0)
            unskew = pltpu.roll(flipped, S - 7, 1, stride=1, stride_axis=0)
            diag[pl.ds(8 * s + h, 1), :] = col_sum(unskew)

        for r in (slice(0, HROWS), slice(HROWS, D)):
            gq = nt(xpT[r, 0:S], qkv[s])
            extra = nt(xpT[r, S:2 * S], qg[s])
            act[s, r, 0:QW] = (gq[:, 0:QW] + extra).astype(BF16)
            act[s, r, QW:3 * QW] = gq[:, QW:3 * QW].astype(BF16)
        after((C1, C2), s)
        place = lax.rem(s, 2) * lax.div(s, 2) + (1 - lax.rem(s, 2)) * (3 + lax.div(s, 2))
        smx[place, 1:2, 0:QW] = (nt(ones, qkv[s, 0:QW]) + nt(ones, qg[s]))[0:1]
        smx[place, 1:2, QW:2 * QW] = nt(ones, qkv[s, 2 * QW:3 * QW])[0:1]
        table = lax.dot_general(
            diag[pl.ds(pl.multiple_of(8 * s, 8), 8), :], onehot, (((1,), (1,)), ((), ())),
            precision=lax.Precision.HIGHEST, preferred_element_type=F32,
        )
        smx[place, 2:5, 0:32] = table[0:3]

        @pl.when(s == 2)
        def _():
            A.middle()

        @pl.when(s == 1)
        def _():
            C2.middle()

    def small_send(k):
        if k == 0:
            return remote(smx.at[0:3], r1, ps.at[0], pr.at[0], core)
        if k == 1:
            return remote(smy, r2, ps.at[1], pr.at[1], xdev)
        if k == 2:
            return remote(smz, r3, ps.at[2], pr.at[2], ydev)
        return remote(smw, r4.at[k - 3], ps.at[k], pr.at[k], zdev[k - 2])

    small_send(0).start()
    A.last()
    for s in range(SLOTS):
        dg[s, 0:S, 0:3 * QW] = nt(unperm[...], qkv[s]).astype(BF16)
        dg[s, S:2 * S, 0:QW] = nt(unperm[...], qg[s]).astype(BF16)
    small_send(0).wait_recv()
    smy[0] = smx[4] + r1[1]
    smy[1] = smx[2] + r1[2]
    small_send(1).start()
    smz[0] = smx[3] + r1[0]
    B.last()
    for s in range(SLOTS):
        acc[0:S] += nn(dg[s, 0:S, 0:3 * QW], wq[s])
        acc[S:2 * S] += nn(dg[s, S:2 * S, 0:QW], wq[s, 0:QW])
    rows_out = [
        pltpu.make_async_copy(acc.at[0:S], gc_hbm, lsem.at[0]),
        pltpu.make_async_copy(acc.at[S:2 * S], gg_hbm, lsem.at[1]),
    ]
    for copy in rows_out:
        copy.start()
    small_send(1).wait_recv()
    smz[0] = smz[0] + r2[0]
    smz[1] = smy[1] + r2[1]
    small_send(2).start()
    C1.middle()
    small_send(2).wait_recv()
    smw[...] = smz[...] + r3[...]
    for k in (3, 4, 5):
        small_send(k).start()
    C2.last()
    C1.last()
    for k in (3, 4, 5):
        small_send(k).wait_recv()
    sm_res[...] = smw[...] + r4[0] + r4[1] + r4[2]
    A.finish(0)
    B.finish(1)
    C2.finish(2)
    C1.finish(2)

    for copy in rows_out:
        copy.wait()
    for p in range(4):
        core_copy(p).wait_send()
    for i in range(len(items)):
        x_copy(i).wait_send()
        y_copy(i).wait_send()
        c_copy(i, False).wait_send()
        c_copy(i, True).wait_send()
    for k in (1, 2, 3):
        small_copy(k).wait_send()
    for k in range(6):
        small_send(k).wait_send()
    A.sent()
    B.sent()
    C1.sent()
    C2.sent()


def layer(stride, dl, rank, pc, x, g, cc, cg, wq, wo, wi, w2, small, vectors):
    vmem = pl.BlockSpec(memory_space=pltpu.VMEM)
    smem = pl.BlockSpec(memory_space=pltpu.SMEM)
    hbm = pl.BlockSpec(memory_space=pl.ANY)
    sd = jax.ShapeDtypeStruct
    vm = pltpu.VMEM
    dma = pltpu.SemaphoreType.DMA
    return pl.pallas_call(
        functools.partial(kernel, stride),
        out_shape=(
            sd((S, D), BF16), sd((S, D), BF16), sd((S, D), F32), sd((S, D), F32),
            sd((SLOTS, 2 * S, D), BF16), sd((3, ROWS, D), F32), sd((2, 8, D), F32),
        ),
        in_specs=[smem, smem, vmem] + [hbm] * 9 + [vmem],
        out_specs=(hbm, hbm, hbm, hbm, hbm, vmem, vmem),
        scratch_shapes=[
            vm((S, S), BF16), vm((S, S), BF16), vm((2 * S, D), BF16), vm((2 * S, D), BF16),
            vm((D, 2 * S), BF16), vm((D, 2 * S), BF16), vm((2 * S, D), BF16),
            vm((SLOTS, 3 * QW, S), BF16), vm((SLOTS, QW, S), BF16), vm((2 * S, D), BF16), vm((2 * S, 1), F32),
            vm((SLOTS, 2 * S, D), BF16), vm((SLOTS, 2 * S, D), BF16), vm((2 * S, D), F32),
            vm((2, HALF, S), BF16), vm((HALF, HALF), F32), vm((32, S), F32),
            vm((SLOTS, 3 * QW, D), BF16), vm((D, D), BF16), vm((SLOTS, D, D), BF16), vm((SLOTS, D, D), BF16),
            vm((SLOTS, 16, D), F32),
            vm((3, D, D), BF16), vm((3, D, D), BF16), vm((2, D, D), BF16), vm((2, D, D), BF16),
            vm((D, D), BF16), vm((2, HROWS, D), BF16),
            vm((5, 8, D), F32), vm((2, 8, D), F32), vm((2, 8, D), F32), vm((2, 8, D), F32),
            vm((3, 8, D), F32), vm((2, 8, D), F32), vm((2, 8, D), F32), vm((3, 2, 8, D), F32),
            dma((11,)), dma((7, 4)), dma((7, 4)), dma((4,)), dma((4,)), dma((3,)), dma((3,)),
            dma((4, 8)), dma((4, 8)), dma((6,)), dma((6,)), pltpu.SemaphoreType.REGULAR((6,)),
        ],
        compiler_params=pltpu.CompilerParams(
            vmem_limit_bytes=int(63.5 * (1 << 20)), collective_id=0, has_side_effects=True
        ),
    )(dl, pc, rank, x, g, cc, cg, wq, wo, wi, w2, small, vectors)


def local(
    stride,
    content, query_stream, cot_content, cot_query, doc_lengths, rank_order, pred_counts, w_qkv, bias_qv,
    w_attn_out, b_attn_out, norm1_gain, norm1_shift, w_in, b_in, w_out, b_out, norm2_gain, norm2_shift, rel_table,
):
    wide = lambda v: jnp.pad(v.astype(F32), ((0, 0), (0, D - v.shape[1])))
    line = lambda v: v.astype(F32).reshape(1, D)
    small = jnp.concatenate([line(b_in), wide(bias_qv), wide(rel_table.T), jnp.zeros((10, D), F32)], axis=0)
    vectors = jnp.concatenate(
        [line(v) for v in (b_attn_out, norm1_gain, norm1_shift, b_out, norm2_gain, norm2_shift)]
        + [jnp.zeros((2, D), F32)],
        axis=0,
    )
    outs = layer(
        stride, doc_lengths, rank_order, pred_counts, content, query_stream, cot_content, cot_query,
        jnp.transpose(w_qkv, (0, 2, 1)).reshape(3 * QW, D), w_attn_out, w_in, w_out, small, vectors,
    )
    out_c, out_g, gc, gg, _, gw, sm = outs
    if stride > 1:
        groups = [list(range(k * stride, k * stride + stride)) for k in range(8)]
        gw = lax.psum_scatter(gw, "dp", scatter_dimension=1, axis_index_groups=groups, tiled=True)
        sm = lax.psum(sm, "dp") / 8.0
    rows = gw.shape[1]
    own, shared = sm[0], sm[1]
    return (
        out_c, out_g, gc, gg,
        jnp.transpose(gw[2, :, 0:3 * QW].reshape(rows, 3, QW), (1, 0, 2)),
        own[1, 0:2 * QW].reshape(2, QW),
        gw[2, :, 3 * QW:].T,
        shared[0], shared[1], shared[2],
        gw[1], own[0], gw[0].T, shared[3], shared[4], shared[5], own[2:5, 0:32].T,
    )


def solution(mesh):
    in_specs = (
        P(("dp", "tensor"), None),
        P(("dp", "tensor"), None),
        P(("dp", "tensor"), None),
        P(("dp", "tensor"), None),
        P("dp", None),
        P("dp", None),
        P("dp"),
        P(None, None, "tensor"),
        P(None, "tensor"),
        P("tensor", None),
        P(),
        P(),
        P(),
        P(None, "tensor"),
        P("tensor"),
        P("tensor", None),
        P(),
        P(),
        P(),
        P(None, "tensor"),
    )
    out_specs = (
        P(("dp", "tensor"), None),
        P(("dp", "tensor"), None),
        P(("dp", "tensor"), None),
        P(("dp", "tensor"), None),
        P(None, "dp", "tensor"),
        P(None, "tensor"),
        P("tensor", "dp"),
        P(),
        P(),
        P(),
        P("dp", "tensor"),
        P("tensor"),
        P("tensor", "dp"),
        P(),
        P(),
        P(),
        P(None, "tensor"),
    )
    stride = mesh.shape["dp"] // 8
    return jax.shard_map(functools.partial(local, stride), mesh=mesh, in_specs=in_specs, out_specs=out_specs, check_vma=False)
```

time: 1220 us -> 213 us (0.17)
  waiting for transfers between devices: 663 us -> 0 us
  matrix products: 284 us -> 0 us
  Pallas kernels: 0 us -> 190 us
  other arithmetic: 85.7 us -> 2.06 us
  local copies, waits for them, and re-layouts: 97.8 us -> 19.8 us
  blocking collectives: 62.9 us -> 0 us
  between operations: 16.1 us -> 0.7 us
    reduce_scatter x10 -> x0, waiting for transfers between devices: 485 us -> none  [the longest x1 72 us: local(): lax.psum_scatter(grad_w_in_part, 'dp', scatter_dimension=0, tiled=True)]
    dot_general x102 -> x0, matrix products: 284 us -> none  [the longest x10 72.2 us: plain_dot(): return jnp.dot(rows_in, weight, preferred_element_type=jnp.float32)]
    pallas_call x0 -> x1, Pallas kernels: none -> 190 us  [layer(): pl.pallas_call(functools.partial(kernel, stride), out_shape=(sd((S, D), B...]
    all_gather x8 -> x0, waiting for transfers between devices: 176 us -> none  [the longest x1 28.1 us: local(): lax.all_gather(hidden_c, 'tensor', axis=0, tiled=True)]
    psum x2 -> x0, blocking collectives: 62.9 us -> none  [the longest x1 40.8 us: local(): lax.psum((jnp.sum(dres1_c, axis=0) + jnp.sum(dres1_g, axis=0), gain1_c +...]
    add x16 -> x0, other arithmetic: 44 us -> none  [the longest x4 36.7 us: attend_grads(): accum = accum + ds_one.astype(jnp.float32) + ds_two.astype(jnp.float32)]
    reduce_sum x26 -> x0, other arithmetic: 29.5 us -> none  [the longest x2 7.01 us: layer_norm(): return centred * lax.rsqrt(variance + EPSILON) * gain_vec + norm_shift]
    unnamed x196 -> x14, local copies, waits for them, and re-layouts: 30.5 us -> 6.51 us
  transfers between devices with their start and end apart: 20 -> 0, of which waited for: 17 -> 0; matrix products, arithmetic and copies ran while one was open for 26% -> 0% of each run, Pallas kernels for 0% -> 0%
where the time goes in v1:
time: 213 us
  Pallas kernels  190 us (89%)
  local copies, waits for them, and re-layouts  19.8 us (9%)
    pallas_call x1, Pallas kernels, layer(): pl.pallas_call(functools.partial(kernel, stride), out_shape=(sd((S, D), B...  190 us
    unnamed x14, local copies, waits for them, and re-layouts  6.51 us
    reshape x7, local copies, waits for them, and re-layouts, local(): line = lambda v: v.astype(F32).reshape(1, D)  4.81 us

profile of v1, /device:TPU:0, one launch (start us, length us, event | category | flops | bytes accessed | tf_op | source)
XLA Modules:
  0.0 212.7 jit_solution(17325369408959829478)
XLA Ops:
  0.7 0.1 pad.21.clone
  0.7 0.7 reshape.95
  1.4 0.7 reshape.86
  2.1 0.7 reshape.87
  2.8 0.7 reshape.93
  3.5 0.7 reshape.97
  4.2 0.7 reshape.90
  4.9 0.7 reshape.91
  5.6 0.7 pad_convert_fusion.1
  6.2 0.6 concatenate.7.vectors
  6.9 0.7 pad_convert_fusion
  7.6 0.7 maximum_maximum_fusion.sm_in
  8.3 190.2 %shard_map.323 = (bf16[512,768]{1,0:T(8,128)(2,1)}, bf16[512,768]{1,0:T(8,128)(2,1)}, f32[512,768]{1,0:T(8,128)}, f32[512,768]{1,0:T(8,128)}, bf16[4,1024,768]{2...) custom-call(s32[4,8]{1,0:T(4,128)} %dl.1, s32[4]{0:T(128)} %pc.1, s32[4,512]{1,0:T(4,128)} %rank.1, ...), custom_call_target="tpu_custom_call" | custom-call | tf_op jit(solution)/shard_map/pallas_call | solution.py:758
  198.5 0.7 slice_bitcast_fusion.3
  199.2 1.7 slice_reduce_fusion
  200.9 0.6 slice_bitcast_fusion.4
  201.5 0.7 reshape_squeeze.7
  202.1 0.0 copy-start.3
  202.1 1.0 slice_bitcast_fusion.2
  203.2 0.7 copy.41
  203.9 1.0 slice.57
  204.9 1.9 slice_bitcast_fusion
  206.8 0.1 copy.39
  207.0 0.9 copy.40
  207.8 0.0 copy-done.3
  207.8 0.9 copy.46
  208.7 0.0 copy-done.2
  208.7 0.9 copy.47
  209.6 0.0 copy-done.1
  209.6 1.1 copy.48
  210.8 0.8 copy-done
  211.6 1.1 copy.49
  (6 shorter events, 0.0 us)
Async XLA Ops:
  202.1 5.7 %copy-start.3 = (bf16[512,768]{1,0:T(8,128)(2,1)S(1)}, bf16[512,768]{1,0:T(8,128)(2,1)}, u32[]{:S(2)}) copy-start(bf16[512,768]{1,0:T(8,128)(2,1)} %get-tuple-element.89) | copy-start | bytes 2359300
  206.8 1.9 copy-start.2
  207.8 1.8 copy-start.1
  209.6 2.0 copy-start

commit v2 on v1

--- a/solution.py
+++ b/solution.py
@@ -65,14 +65,21 @@
 
 def kernel(
     stride,
-    dl, pc, rank, x_hbm, g_hbm, cc_hbm, cg_hbm, wq_in, wo_in, wi_in, w2_in, sm_in, vectors,
+    dl, pc, rank, x_hbm, g_hbm, cc_hbm, cg_hbm, wq_in, wo_in, wi_in, w2_in,
+    b_in, bias_qv, table_in, b_attn_in, n1g_in, n1s_in, b_out_in, n2g_in, n2s_in,
     oc_hbm, og_hbm, gc_hbm, gg_hbm, stash, g_res, sm_res,
     perm, unperm, xin, hid, tA, tB, attn, qkv, qg, xhat, rstd1, act, dg, acc,
-    mask, square, lines, wq, wo, wi, w2, wsm,
-    ga, gb, rca, rcb, rxa, ryb, smx, smy, smz, smw, r1, r2, r3, r4,
+    mask, square, lines, wq, wo, wi, w2, wsm, vectors,
+    ga, gb, rca, rcb, rza, rya, rxa, rxb, ryb, smx, smy, smz, smw, r1, r2, r3, r4,
     lsem, xs, xr, cs, cr, ss, sr, os, orr, ps, pr, credit,
 ):
     b_attn, n1g, n1s, b_out, n2g, n2s = (vectors.at[k:k + 1] for k in range(6))
+    for k, ref in enumerate((b_attn_in, n1g_in, n1s_in, b_out_in, n2g_in, n2s_in)):
+        vectors[k:k + 1] = ref[...].astype(F32).reshape(1, D)
+    wsm[0] = jnp.zeros((8, D), F32)
+    wsm[0, 0:1] = b_in[...].astype(F32).reshape(1, D)
+    wsm[0, 1:3, 0:QW] = bias_qv[...].astype(F32)
+    wsm[0, 3:3 + SLOT_HEADS, 0:32] = table_in[...].astype(F32)
     bias = dsacc = square
     text = diag = lines
     t = lax.axis_index("tensor")
@@ -133,14 +140,11 @@
         return remote(src, place(1, 0, n), cs.at[p], cr.at[p], core)
 
     def small_copy(k):
-        return remote(sm_in, wsm.at[k], ss.at[k - 1], sr.at[k - 1], (core, xdev, diagonal)[k - 1])
+        return remote(wsm.at[0], wsm.at[k], ss.at[k - 1], sr.at[k - 1], (core, xdev, diagonal)[k - 1])
 
     def own_copy(p):
         src, place, n, _ = parts[p]
         return pltpu.make_async_copy(src, place(0, 0, n), lsem.at[2 + p])
-
-    def small_own():
-        return pltpu.make_async_copy(sm_in, wsm.at[0], lsem.at[6])
 
     def arrived_x(i):
         x_copy(i).wait_recv()
@@ -165,7 +169,6 @@
         ends = (stash.at[s], dg.at[s]) if back else (dg.at[s], stash.at[s])
         return pltpu.make_async_copy(ends[0], ends[1], lsem.at[7 + s])
 
-    small_own().start()
     own_copy(0).start()
     rows_in = fetch(x_hbm, g_hbm)
     for copy in rows_in:
@@ -220,10 +223,7 @@
     def transposed(dst, src):
         for st in range(2):
             r = slice(st * S, st * S + S)
-            flipped = src[r].T
-            for k in range(8):
-                to = (k % 2) * 4 * ROWS + (k // 2) * ROWS
-                dst[to:to + ROWS, r] = flipped[k * ROWS:k * ROWS + ROWS]
+            dst[:, r] = src[r].T
 
     def permuted(dst):
         for copy in rows_in:
@@ -235,7 +235,6 @@
 
     xp = hid
     permuted(xp)
-    small_own().wait()
     own_copy(0).wait()
 
     def prob_at(s, h, b, st):
@@ -248,28 +247,24 @@
         def _():
             core_copy(0).wait_recv()
             small_copy(1).wait_recv()
-            arrived_x(0)
+            arrived_x(1)
 
         @pl.when(s == 2)
         def _():
-            arrived_x(1)
             small_copy(2).wait_recv()
-            arrived_y(0)
             arrived_y(1)
 
         @pl.when(s == 3)
         def _():
-            arrived_x(2)
             small_copy(3).wait_recv()
             arrived_core(0)
             arrived_core(1)
 
         small = wsm[s].astype(BF16)
-        table = nn(small[:, 0:32], onehot.astype(BF16))
-        text[pl.ds(pl.multiple_of(8 * s, 8), 8), :] = table[3:11]
-        sel = jnp.where(iota((16, 128), 0) == 1, 1.0, 0.0).astype(BF16)
+        text[pl.ds(pl.multiple_of(8 * s, 8), 8), :] = nn(small[:, 0:32], onehot.astype(BF16))
+        sel = jnp.where(iota((8, 128), 0) == 1, 1.0, 0.0).astype(BF16)
         bq = tn(small[:, 0:QW], sel)[:, 0:1]
-        sel = jnp.where(iota((16, 128), 0) == 2, 1.0, 0.0).astype(BF16)
+        sel = jnp.where(iota((8, 128), 0) == 2, 1.0, 0.0).astype(BF16)
         bv = tn(small[:, 0:QW], sel)[:, 0:1]
         r = nt(wq[s], xp[0:S])
         qkv[s, 0:QW] = ((r[0:QW] + bq).astype(BF16) * 0.125).astype(BF16)
@@ -279,8 +274,21 @@
 
         @pl.loop(0, SLOT_HEADS)
         def _(h):
+            n = SLOT_HEADS * s + h
+            pl.when(n == 1)(lambda: arrived_x(0))
+
+            @pl.when(n == 5)
+            def _():
+                arrived_x(2)
+                arrived_y(0)
+
+            @pl.when(n == 8)
+            def _():
+                arrived_x(3)
+                arrived_y(2)
+
             hr = pl.multiple_of(h * HD, HD)
-            rowvec = text[pl.ds(8 * s + h, 1), :]
+            rowvec = text[pl.ds(8 * s + 3 + h, 1), :]
             rolled = pltpu.roll(jnp.broadcast_to(rowvec, (HALF, S)), 0, 1, stride=1, stride_axis=0)
             bias[...] = rolled[:, 0:HALF]
             for b in range(2):
@@ -302,13 +310,13 @@
             def _():
                 stash_copy(k, False).start()
 
-    arrived_y(2)
     own_copy(1).wait()
     core_copy(1).wait_recv()
     for st in range(2):
         r = slice(st * S, st * S + S)
         attn[r] = nt(unperm[...], tA[:, r]).astype(BF16)
     arrived_core(2)
+    arrived_x(4)
     for r in (slice(k * HALF, k * HALF + HALF) for k in range(4)):
         res = xin[r].astype(F32) + nn(attn[r], wo[...]) + b_attn[...]
         cen = res - row_mean(res)
@@ -327,23 +335,19 @@
 
     @pl.loop(0, SLOTS)
     def _(s):
-        @pl.when(s == 0)
-        def _():
-            arrived_x(3)
-
         @pl.when(s == 1)
         def _():
             core_copy(2).wait_recv()
+            arrived_y(3)
+            arrived_x(5)
 
         @pl.when(s == 2)
         def _():
-            arrived_x(4)
-            arrived_y(3)
             arrived_y(4)
 
         @pl.when(s == 3)
         def _():
-            arrived_x(5)
+            arrived_x(6)
             arrived_core(3)
             arrived_core(4)
 
@@ -367,11 +371,10 @@
         @pl.when(s == 1)
         def _():
             core_copy(3).wait_recv()
+            arrived_y(5)
 
         @pl.when(s == 2)
         def _():
-            arrived_x(6)
-            arrived_y(5)
             arrived_y(6)
 
         @pl.when(s == 3)
@@ -411,126 +414,155 @@
     for copy in rows_out:
         copy.start()
 
-    own_half = pl.ds(pl.multiple_of(yb * HROWS, HROWS), HROWS)
-    other_half = pl.ds(pl.multiple_of((1 - yb) * HROWS, HROWS), HROWS)
+    def rows_at(lo, n):
+        return pl.ds(pl.multiple_of(lo, ROWS), n)
+
+    own_half = rows_at(yb * HROWS, HROWS)
+    other_half = rows_at((1 - yb) * HROWS, HROWS)
+    zlow, zhigh = zbit, lax.div(zb, 2)
+    z_own = rows_at(zlow * HROWS, HROWS)
+    z_other = rows_at((1 - zlow) * HROWS, HROWS)
+    zy_own = rows_at(zlow * HROWS + yb * 2 * ROWS, 2 * ROWS)
+    zy_other = rows_at(zlow * HROWS + (1 - yb) * 2 * ROWS, 2 * ROWS)
+    zyz_own = rows_at(zlow * HROWS + yb * 2 * ROWS + zhigh * ROWS, ROWS)
+    zyz_other = rows_at(zlow * HROWS + yb * 2 * ROWS + (1 - zhigh) * ROWS, ROWS)
 
     def block(k):
-        return pl.ds(pl.multiple_of(yb * HROWS + z_of[k] * ROWS, ROWS), ROWS)
-
-    def add(dst, src, rows_d=None, rows_s=None):
-        count = dst.shape[0] if rows_d is None else HROWS
+        return rows_at(yb * HROWS + z_of[k] * ROWS, ROWS)
+
+    def store(dst, lead, lo, half_index, value, z_first):
+        for b in range(4):
+            y, z = (4 * half_index + b) % 2, (4 * half_index + b) // 2
+            to = ((z % 2) * 4 + y * 2 + z // 2 if z_first else y * 4 + z) * ROWS
+            dst[lead, to:to + ROWS, lo:lo + value.shape[1]] = value[b * ROWS:b * ROWS + ROWS, :]
+
+    def add(dst, at, *sources):
+        base = 0 if at is None else at.start
+        count = dst.shape[0] if at is None else at.size
 
         @pl.loop(0, count // ROWS)
         def _(i):
             step = pl.multiple_of(i * ROWS, ROWS)
-            a = pl.ds(step + (0 if rows_d is None else rows_d.start), ROWS)
-            b = pl.ds(step + (0 if rows_s is None else rows_s.start), ROWS)
-            dst[a, :] = (dst[a, :].astype(F32) + src[b, :].astype(F32)).astype(BF16)
-
-    def rz_at(n, k, cols):
-        return wi.at[(0, 1, 3, 3)[n], (k - 1) * ROWS:k * ROWS, cols]
+            a = pl.ds(pl.multiple_of(base + step, ROWS), ROWS)
+            total = dst[a, :].astype(F32)
+            for src in sources:
+                total = total + src[pl.ds(step, ROWS), :].astype(F32)
+            dst[a, :] = total.astype(BF16)
 
     class Chunk:
-        def __init__(self, index, even, odd, rc, rx, ry, cols, x_first):
-            self.n, self.even, self.odd, self.rc = index, even, odd, rc
-            self.rx, self.ry, self.cols, self.x_first = rx, ry, cols, x_first
-
-        def sems(self, k):
-            return os.at[self.n, k], orr.at[self.n, k]
+        def __init__(self, index, even, odd, rc, parts, out):
+            self.n, self.even, self.odd, self.rc, self.out = index, even, odd, rc, out
+            self.moves = {}
+            for k, (name, src, dst, who) in enumerate(parts):
+                self.moves[name] = (src, dst, k + 2, who)
 
         def core_send(self, k):
-            return remote(self.odd[k], self.rc[k], *self.sems(k), core)
-
-        def x_send(self):
-            if self.x_first:
-                return remote(self.even[1], self.rx, *self.sems(2), xdev)
-            return remote(self.even[1].at[own_half], self.rx, *self.sems(2), xdev)
-
-        def y_send(self, k):
-            return remote(self.even[k].at[other_half], self.ry[k], *self.sems(3 + k), ydev)
-
-        def z_send(self, k):
-            return remote(
-                self.even[0].at[block(k)], rz_at(self.n, k, self.cols), *self.sems(4 + k), zdev[k]
-            )
+            return remote(self.odd[k], self.rc[k], os.at[self.n, k], orr.at[self.n, k], core)
+
+        def move(self, name):
+            src, dst, k, who = self.moves[name]
+            return remote(src, dst, os.at[self.n, k], orr.at[self.n, k], who)
+
+        def go(self, *names):
+            for name in names:
+                self.move(name).start()
+
+        def here(self, *names):
+            for name in names:
+                self.move(name).wait_recv()
+            return [self.moves[name][1] for name in names]
 
         def core_sum(self, k):
             self.core_send(k).wait_recv()
-            add(self.even[k], self.rc[k])
-            if self.x_first:
-                if k == 1:
-                    self.x_send().start()
-            else:
-                self.y_send(k).start()
-
-        def middle(self):
-            if self.x_first:
-                self.x_send().wait_recv()
-                add(self.even[0], self.rx)
-                self.y_send(0).start()
-            else:
-                self.y_send(1).wait_recv()
-                add(self.even[1], self.ry[1], own_half)
-                self.x_send().start()
-
-        def last(self):
-            self.y_send(0).wait_recv()
-            add(self.even[0], self.ry[0], own_half)
-            if not self.x_first:
-                self.x_send().wait_recv()
-                add(self.even[0], self.rx, own_half)
-            for k in (1, 2, 3):
-                self.z_send(k).start()
-
-        def finish(self, out):
-            total = self.even[0][block(0), :].astype(F32)
-            for k in (1, 2, 3):
-                self.z_send(k).wait_recv()
-                total = total + rz_at(self.n, k, self.cols)[...].astype(F32)
-            g_res[out, :, self.cols] = total
+            add(self.even[k], None, self.rc[k])
+
+        def finish(self, at, *names):
+            total = self.even[0][at, :].astype(F32)
+            for ref in self.here(*names):
+                total = total + ref[...].astype(F32)
+            which, cols = self.out
+            g_res[which, :, cols] = total
 
         def sent(self):
-            for k in (0, 1) if self.n > 1 else (0,):
+            for k in (0, 1) if self.n > 3 else (0,):
                 self.core_send(k).wait_send()
-            self.x_send().wait_send()
-            self.y_send(0).wait_send()
-            if not self.x_first:
-                self.y_send(1).wait_send()
-            for k in (1, 2, 3):
-                self.z_send(k).wait_send()
-
-    whole = pl.ds(0, D)
-    first, second = pl.ds(0, D // 2), pl.ds(D // 2, D // 2)
-    A = Chunk(0, (ga.at[0], ga.at[1]), (ga.at[2], ga.at[2]), (rca.at[0], rca.at[1]), rxa, (w2.at[0, HROWS:D], None), whole, True)
-    B = Chunk(1, (gb.at[0], gb.at[1]), (gb.at[2], gb.at[2]), (rcb.at[0], rcb.at[1]), w2.at[0, 0:HROWS], (ryb.at[0], ryb.at[1]), whole, False)
-
-    def c_part(index, cols, x_first):
-        g = lambda s: act.at[s, 0:D, cols]
-        r = lambda ref: ref.at[:, cols]
-        if x_first:
-            rx, ry = w2.at[1, :, cols], (w2.at[3, 0:HROWS, cols], None)
-        else:
-            rx, ry = w2.at[1, 0:HROWS, cols], (w2.at[3, 0:HROWS, cols], w2.at[3, HROWS:D, cols])
-        return Chunk(index, (g(0), g(2)), (g(1), g(3)), (r(rca.at[0]), r(rca.at[1])), rx, ry, cols, x_first)
-
-    C1 = c_part(2, first, True)
-    C2 = c_part(3, second, False)
+            for name in self.moves:
+                self.move(name).wait_send()
+
+    whole, first, second = pl.ds(0, D), pl.ds(0, D // 2), pl.ds(D // 2, D // 2)
+
+    def x_flow(index, even, odd, rc, rx, ry, rz, out):
+        e0, e2 = even
+        parts = [("x", e2, rx, xdev), ("y", e0.at[other_half], ry, ydev)]
+        parts += [("z%d" % k, e0.at[block(k)], rz(k), zdev[k]) for k in (1, 2, 3)]
+        return Chunk(index, even, odd, rc, parts, out)
+
+    def y_flow(index, even, odd, rc, rx, ry, rz, out):
+        e0, e2 = even
+        parts = [
+            ("y2", e2.at[other_half], ry[1], ydev), ("y0", e0.at[other_half], ry[0], ydev),
+            ("x", e2.at[own_half], rx, xdev),
+        ]
+        parts += [("z%d" % k, e0.at[block(k)], rz(k), zdev[k]) for k in (1, 2, 3)]
+        return Chunk(index, even, odd, rc, parts, out)
+
+    def dead(slot, lo, n, cols):
+        return w2.at[slot, lo:lo + n, cols]
+
+    def z_flow(index, even, odd, rc, rz, ry, rx, rh, out):
+        e0, e2 = even
+        parts = [
+            ("l2", e2.at[z_other], rz[1], zdev[1]), ("l0", e0.at[z_other], rz[0], zdev[1]),
+            ("y2", e2.at[zy_other], ry[1], ydev), ("y0", e0.at[zy_other], ry[0], ydev),
+            ("x", e2.at[zy_own], rx, xdev), ("h", e0.at[zyz_other], rh, zdev[2]),
+        ]
+        return Chunk(index, even, odd, rc, parts, out)
+
+    def in_wi(slot, cols):
+        return lambda k: wi.at[slot, (k - 1) * ROWS:k * ROWS, cols]
+
+    def ab_even(g, cols):
+        return (g.at[0, :, cols], g.at[1, :, cols]), (g.at[2, :, cols], g.at[2, :, cols])
+
+    def c_even(cols):
+        return (act.at[0, 0:D, cols], act.at[2, 0:D, cols]), (act.at[1, 0:D, cols], act.at[3, 0:D, cols])
+
+    def pair(ref, cols):
+        return ref.at[0, :, cols], ref.at[1, :, cols]
+
+    A1 = z_flow(
+        0, *ab_even(ga, first), pair(rca, first), (rza.at[0], rza.at[1]),
+        (dead(0, 0, 2 * ROWS, first), rya), dead(0, 2 * ROWS, 2 * ROWS, first), dead(0, 4 * ROWS, ROWS, first),
+        (0, first),
+    )
+    A2 = x_flow(
+        1, *ab_even(ga, second), pair(rca, second), rxa, dead(0, 0, HROWS, second), in_wi(0, second), (0, second),
+    )
+    B1 = y_flow(
+        2, *ab_even(gb, first), pair(rcb, first), dead(1, 0, HROWS, first),
+        (ryb.at[0], ryb.at[1]), in_wi(0, first), (1, first),
+    )
+    B2 = x_flow(
+        3, *ab_even(gb, second), pair(rcb, second), rxb, dead(1, 0, HROWS, second), in_wi(1, second), (1, second),
+    )
+    Ca = z_flow(
+        4, *c_even(first), pair(rca, first),
+        (dead(3, 0, HROWS, first), dead(3, HROWS, HROWS, first)),
+        (dead(0, 5 * ROWS, 2 * ROWS, first), dead(1, HROWS, 2 * ROWS, first)),
+        dead(1, HROWS + 2 * ROWS, 2 * ROWS, first), dead(0, 7 * ROWS, ROWS, first), (2, first),
+    )
+    Cb = y_flow(
+        5, *c_even(second), pair(rca, second), dead(1, HROWS, HROWS, second),
+        (dead(3, 0, HROWS, second), dead(3, HROWS, HROWS, second)), in_wi(3, second), (2, second),
+    )
 
     def buffer_of(s):
         odd = lax.rem(s, 2)
         return 2 * odd + (1 - odd) * lax.div(s, 2)
 
-    def after(chunks, s):
-        for k in (1, 0):
-            @pl.when(s == 2 * k + 1)
-            def _():
-                for chunk in chunks:
-                    chunk.core_send(k).start()
-
-            @pl.when(s == 2 * k)
-            def _():
-                for chunk in chunks:
-                    chunk.core_sum(k)
+    def after(s, three, two, one, zero):
+        for k, step in ((3, three), (2, two), (1, one), (0, zero)):
+            pl.when(s == k)(step)
 
     @pl.loop(0, SLOTS)
     def _(i):
@@ -538,11 +570,34 @@
 
         @pl.when(s == 1)
         def _():
-            A.core_send(1).wait_send()
-
-        for r in (slice(0, HROWS), slice(HROWS, D)):
-            ga[buffer_of(s), r] = nn(tA[r], act[s]).astype(BF16)
-        after((A,), s)
+            A1.core_send(1).wait_send()
+            A2.core_send(1).wait_send()
+
+        for k in range(2):
+            value = nn(tA[k * HROWS:k * HROWS + HROWS], act[s]).astype(BF16)
+            store(ga, buffer_of(s), 0, k, value[:, 0:D // 2], True)
+            store(ga, buffer_of(s), D // 2, k, value[:, D // 2:], False)
+
+        def three():
+            A1.core_send(1).start()
+            A2.core_send(1).start()
+
+        def two():
+            A1.core_sum(1)
+            A1.go("l2")
+            A2.core_sum(1)
+            A2.go("x")
+
+        def one():
+            A1.core_send(0).start()
+            A2.core_send(0).start()
+
+        def zero():
+            A1.core_sum(0)
+            A1.go("l0")
+            A2.core_sum(0)
+
+        after(s, three, two, one, zero)
 
     @pl.loop(0, SLOTS)
     def _(i):
@@ -560,11 +615,35 @@
 
         @pl.when(s == 1)
         def _():
-            B.core_send(1).wait_send()
-
-        for r in (slice(0, HROWS), slice(HROWS, D)):
-            gb[buffer_of(s), r] = nn(tB[r], dg[s]).astype(BF16)
-        after((B,), s)
+            B1.core_send(1).wait_send()
+            B2.core_send(1).wait_send()
+
+        for k in range(2):
+            value = nn(tB[k * HROWS:k * HROWS + HROWS], dg[s]).astype(BF16)
+            store(gb, buffer_of(s), 0, k, value, False)
+
+        def three():
+            B1.core_send(1).start()
+            B2.core_send(1).start()
+
+        def two():
+            B1.core_sum(1)
+            B1.go("y2")
+            B2.core_sum(1)
+            B2.go("x")
+            add(ga.at[1, :, first], z_own, *A1.here("l2"))
+            A1.go("y2")
+
+        def one():
+            B1.core_send(0).start()
+            B2.core_send(0).start()
+
+        def zero():
+            B1.core_sum(0)
+            B1.go("y0")
+            B2.core_sum(0)
+
+        after(s, three, two, one, zero)
         for r in (slice(0, S), slice(S, 2 * S)):
             acc[r] += nt(dg[s, r], wi[s])
         for k in range(SLOTS):
@@ -598,11 +677,18 @@
         copy.start()
     for k in range(6):
         pl.semaphore_wait(credit.at[k], 1)
-    B.middle()
-    for r in (slice(0, HROWS), slice(HROWS, D)):
-        gwo = nn(tB[r], attn[...]).astype(BF16)
+    add(ga.at[0, :, second], None, *A2.here("x"))
+    A2.go("y")
+    add(ga.at[1, :, first], zy_own, *A1.here("y2"))
+    A1.go("x")
+    add(ga.at[0, :, first], z_own, *A1.here("l0"))
+    A1.go("y0")
+    add(gb.at[1, :, first], own_half, *B1.here("y2"))
+    B1.go("x")
+    for k in range(2):
+        gwo = nn(tB[k * HROWS:k * HROWS + HROWS], attn[...]).astype(BF16)
         for s in range(SLOTS):
-            act[s, r, 3 * QW:D] = gwo[:, s * QW:s * QW + QW]
+            store(act, s, 0, k, gwo[:, s * QW:s * QW + QW], True)
     for st in range(2):
         r = slice(st * S, st * S + S)
         for f in (slice(0, HROWS), slice(HROWS, D)):
@@ -612,6 +698,43 @@
     xpT = tB
 
     ones = jnp.ones((16, S), BF16)
+    def head_backward(s, h):
+        hr = h * HD if isinstance(h, int) else pl.multiple_of(h * HD, HD)
+        for b in range(2):
+            c = slice(HALF * b, HALF * b + HALF)
+            kT = qkv[s, pl.ds(QW + hr, HD), c]
+            vT = qkv[s, pl.ds(2 * QW + hr, HD), c]
+            dk = dv = None
+            for st in range(2):
+                qT = qkv[s, pl.ds(hr, HD), c] if st == 0 else qg[s, pl.ds(hr, HD), c]
+                dOT = tA[pl.ds(pl.multiple_of(s * QW + hr, HD), HD), st * S + HALF * b:st * S + HALF * b + HALF]
+                p = prob_at(s, h, b, st)[...]
+                pf = p.astype(F32)
+                dp = tn(vT, dOT)
+                dsl = (pf * (dp - jnp.sum(dp * pf, axis=0, keepdims=True))).astype(BF16)
+                if b == 0 and st == 0:
+                    dsacc[...] = dsl.astype(F32)
+                else:
+                    dsacc[...] += dsl.astype(F32)
+                dq = (nn(kT, dsl) * 0.125).astype(BF16)
+                dk1 = nt(qT, dsl)
+                dv1 = nt(dOT, p)
+                dk = dk1 if dk is None else dk + dk1
+                dv = dv1 if dv is None else dv + dv1
+                if st == 0:
+                    qkv[s, pl.ds(hr, HD), c] = dq
+                else:
+                    qg[s, pl.ds(hr, HD), c] = dq
+            qkv[s, pl.ds(QW + hr, HD), c] = dk.astype(BF16)
+            qkv[s, pl.ds(2 * QW + hr, HD), c] = dv.astype(BF16)
+        total = jnp.zeros((8, S), F32)
+        for a in range(HALF // 8):
+            wide = jnp.concatenate([dsacc[8 * a:8 * a + 8, :], jnp.zeros((8, HALF), F32)], axis=1)
+            total = total + (wide if a == 0 else pltpu.roll(wide, S - 8 * a, 1))
+        flipped = jnp.concatenate([total[7 - i:8 - i] for i in range(8)], axis=0)
+        unskew = pltpu.roll(flipped, S - 7, 1, stride=1, stride_axis=0)
+        diag[pl.ds(8 * s + h, 1), :] = col_sum(unskew)
+
     @pl.loop(0, SLOTS)
     def _(i):
         s = 3 - i
@@ -619,51 +742,51 @@
             @pl.when(s == k)
             def _():
                 stash_copy(k, True).wait()
-
-        @pl.loop(0, SLOT_HEADS)
+        head_backward(s, 0)
+        dqkv = jnp.concatenate([qkv[s, k * QW:k * QW + HD] for k in range(3)], axis=0)
+        for k in range(2):
+            r = slice(k * HROWS, k * HROWS + HROWS)
+            gq = nt(xpT[r, 0:S], dqkv)
+            extra = nt(xpT[r, S:2 * S], qg[s, 0:HD])
+            store(act, s, QW, k, (gq[:, 0:HD] + extra).astype(BF16), True)
+            store(act, s, QW + HD, k, gq[:, HD:QW].astype(BF16), True)
+
+        def three():
+            Ca.core_send(1).start()
+
+        def two():
+            Ca.core_sum(1)
+            Ca.go("l2")
+            add(gb.at[0, :, second], None, *B2.here("x"))
+            B2.go("y")
+
+        def one():
+            Ca.core_send(0).start()
+
+        def zero():
+            Ca.core_sum(0)
+            Ca.go("l0")
+            add(ga.at[0, :, second], own_half, *A2.here("y"))
+            A2.go("z1", "z2", "z3")
+
+        after(s, three, two, one, zero)
+
+    @pl.loop(0, SLOTS)
+    def _(i):
+        s = 3 - i
+
+        @pl.loop(1, SLOT_HEADS)
         def _(h):
-            hr = pl.multiple_of(h * HD, HD)
-            for b in range(2):
-                c = slice(HALF * b, HALF * b + HALF)
-                kT = qkv[s, pl.ds(QW + hr, HD), c]
-                vT = qkv[s, pl.ds(2 * QW + hr, HD), c]
-                dk = dv = None
-                for st in range(2):
-                    qT = qkv[s, pl.ds(hr, HD), c] if st == 0 else qg[s, pl.ds(hr, HD), c]
-                    dOT = tA[pl.ds(pl.multiple_of(s * QW + hr, HD), HD), st * S + HALF * b:st * S + HALF * b + HALF]
-                    p = prob_at(s, h, b, st)[...]
-                    pf = p.astype(F32)
-                    dp = tn(vT, dOT)
-                    dsl = (pf * (dp - jnp.sum(dp * pf, axis=0, keepdims=True))).astype(BF16)
-                    if b == 0 and st == 0:
-                        dsacc[...] = dsl.astype(F32)
-                    else:
-                        dsacc[...] += dsl.astype(F32)
-                    dq = (nn(kT, dsl) * 0.125).astype(BF16)
-                    dk1 = nt(qT, dsl)
-                    dv1 = nt(dOT, p)
-                    dk = dk1 if dk is None else dk + dk1
-                    dv = dv1 if dv is None else dv + dv1
-                    if st == 0:
-                        qkv[s, pl.ds(hr, HD), c] = dq
-                    else:
-                        qg[s, pl.ds(hr, HD), c] = dq
-                qkv[s, pl.ds(QW + hr, HD), c] = dk.astype(BF16)
-                qkv[s, pl.ds(2 * QW + hr, HD), c] = dv.astype(BF16)
-            total = jnp.zeros((8, S), F32)
-            for a in range(HALF // 8):
-                wide = jnp.concatenate([dsacc[8 * a:8 * a + 8, :], jnp.zeros((8, HALF), F32)], axis=1)
-                total = total + (wide if a == 0 else pltpu.roll(wide, S - 8 * a, 1))
-            flipped = jnp.concatenate([total[7 - i:8 - i] for i in range(8)], axis=0)
-            unskew = pltpu.roll(flipped, S - 7, 1, stride=1, stride_axis=0)
-            diag[pl.ds(8 * s + h, 1), :] = col_sum(unskew)
-
-        for r in (slice(0, HROWS), slice(HROWS, D)):
-            gq = nt(xpT[r, 0:S], qkv[s])
-            extra = nt(xpT[r, S:2 * S], qg[s])
-            act[s, r, 0:QW] = (gq[:, 0:QW] + extra).astype(BF16)
-            act[s, r, QW:3 * QW] = gq[:, QW:3 * QW].astype(BF16)
-        after((C1, C2), s)
+            head_backward(s, h)
+
+        dqkv = jnp.concatenate([qkv[s, k * QW + HD:k * QW + QW] for k in range(3)], axis=0)
+        for k in range(2):
+            r = slice(k * HROWS, k * HROWS + HROWS)
+            gq = nt(xpT[r, 0:S], dqkv)
+            extra = nt(xpT[r, S:2 * S], qg[s, HD:QW])
+            store(act, s, 2 * QW, k, (gq[:, 0:2 * HD] + extra).astype(BF16), False)
+            store(act, s, 2 * QW + 2 * HD, k, gq[:, 2 * HD:].astype(BF16), False)
+
         place = lax.rem(s, 2) * lax.div(s, 2) + (1 - lax.rem(s, 2)) * (3 + lax.div(s, 2))
         smx[place, 1:2, 0:QW] = (nt(ones, qkv[s, 0:QW]) + nt(ones, qg[s]))[0:1]
         smx[place, 1:2, QW:2 * QW] = nt(ones, qkv[s, 2 * QW:3 * QW])[0:1]
@@ -673,13 +796,39 @@
         )
         smx[place, 2:5, 0:32] = table[0:3]
 
-        @pl.when(s == 2)
-        def _():
-            A.middle()
-
-        @pl.when(s == 1)
-        def _():
-            C2.middle()
+        def three():
+            Cb.core_send(1).start()
+            add(ga.at[0, :, first], zy_own, *A1.here("y0", "x"))
+            A1.go("h")
+            add(gb.at[0, :, first], own_half, *B1.here("y0", "x"))
+            B1.go("z1", "z2", "z3")
+            add(act.at[2, 0:D, first], z_own, *Ca.here("l2"))
+            Ca.go("y2")
+
+        def two():
+            Cb.core_sum(1)
+            Cb.go("y2")
+            add(gb.at[0, :, second], own_half, *B2.here("y"))
+            B2.go("z1", "z2", "z3")
+            add(act.at[0, 0:D, first], z_own, *Ca.here("l0"))
+            Ca.go("y0")
+            add(act.at[2, 0:D, first], zy_own, *Ca.here("y2"))
+            Ca.go("x")
+
+        def one():
+            Cb.core_send(0).start()
+            A2.finish(block(0), "z1", "z2", "z3")
+            A1.finish(zyz_own, "h")
+
+        def zero():
+            Cb.core_sum(0)
+            Cb.go("y0")
+            add(act.at[2, 0:D, second], own_half, *Cb.here("y2"))
+            Cb.go("x")
+            add(act.at[0, 0:D, first], zy_own, *Ca.here("y0", "x"))
+            Ca.go("h")
+
+        after(s, three, two, one, zero)
 
     def small_send(k):
         if k == 0:
@@ -691,7 +840,6 @@
         return remote(smw, r4.at[k - 3], ps.at[k], pr.at[k], zdev[k - 2])
 
     small_send(0).start()
-    A.last()
     for s in range(SLOTS):
         dg[s, 0:S, 0:3 * QW] = nt(unperm[...], qkv[s]).astype(BF16)
         dg[s, S:2 * S, 0:QW] = nt(unperm[...], qg[s]).astype(BF16)
@@ -700,8 +848,18 @@
     smy[1] = smx[2] + r1[2]
     small_send(1).start()
     smz[0] = smx[3] + r1[0]
-    B.last()
-    for s in range(SLOTS):
+    B1.finish(block(0), "z1", "z2", "z3")
+    B2.finish(block(0), "z1", "z2", "z3")
+    for s in range(2):
+        acc[0:S] += nn(dg[s, 0:S, 0:3 * QW], wq[s])
+        acc[S:2 * S] += nn(dg[s, S:2 * S, 0:QW], wq[s, 0:QW])
+    small_send(1).wait_recv()
+    smz[0] = smz[0] + r2[0]
+    smz[1] = smy[1] + r2[1]
+    small_send(2).start()
+    add(act.at[0, 0:D, second], own_half, *Cb.here("y0", "x"))
+    Cb.go("z1", "z2", "z3")
+    for s in range(2, SLOTS):
         acc[0:S] += nn(dg[s, 0:S, 0:3 * QW], wq[s])
         acc[S:2 * S] += nn(dg[s, S:2 * S, 0:QW], wq[s, 0:QW])
     rows_out = [
@@ -710,24 +868,15 @@
     ]
     for copy in rows_out:
         copy.start()
-    small_send(1).wait_recv()
-    smz[0] = smz[0] + r2[0]
-    smz[1] = smy[1] + r2[1]
-    small_send(2).start()
-    C1.middle()
     small_send(2).wait_recv()
     smw[...] = smz[...] + r3[...]
     for k in (3, 4, 5):
         small_send(k).start()
-    C2.last()
-    C1.last()
+    Ca.finish(zyz_own, "h")
     for k in (3, 4, 5):
         small_send(k).wait_recv()
     sm_res[...] = smw[...] + r4[0] + r4[1] + r4[2]
-    A.finish(0)
-    B.finish(1)
-    C2.finish(2)
-    C1.finish(2)
+    Cb.finish(block(0), "z1", "z2", "z3")
 
     for copy in rows_out:
         copy.wait()
@@ -742,13 +891,11 @@
         small_copy(k).wait_send()
     for k in range(6):
         small_send(k).wait_send()
-    A.sent()
-    B.sent()
-    C1.sent()
-    C2.sent()
-
-
-def layer(stride, dl, rank, pc, x, g, cc, cg, wq, wo, wi, w2, small, vectors):
+    for chunk in (A1, A2, B1, B2, Ca, Cb):
+        chunk.sent()
+
+
+def layer(stride, *args):
     vmem = pl.BlockSpec(memory_space=pltpu.VMEM)
     smem = pl.BlockSpec(memory_space=pltpu.SMEM)
     hbm = pl.BlockSpec(memory_space=pl.ANY)
@@ -761,7 +908,7 @@
             sd((S, D), BF16), sd((S, D), BF16), sd((S, D), F32), sd((S, D), F32),
             sd((SLOTS, 2 * S, D), BF16), sd((3, ROWS, D), F32), sd((2, 8, D), F32),
         ),
-        in_specs=[smem, smem, vmem] + [hbm] * 9 + [vmem],
+        in_specs=[smem, smem, vmem] + [hbm] * 8 + [vmem] * 9,
         out_specs=(hbm, hbm, hbm, hbm, hbm, vmem, vmem),
         scratch_shapes=[
             vm((S, S), BF16), vm((S, S), BF16), vm((2 * S, D), BF16), vm((2 * S, D), BF16),
@@ -770,18 +917,48 @@
             vm((SLOTS, 2 * S, D), BF16), vm((SLOTS, 2 * S, D), BF16), vm((2 * S, D), F32),
             vm((2, HALF, S), BF16), vm((HALF, HALF), F32), vm((32, S), F32),
             vm((SLOTS, 3 * QW, D), BF16), vm((D, D), BF16), vm((SLOTS, D, D), BF16), vm((SLOTS, D, D), BF16),
-            vm((SLOTS, 16, D), F32),
+            vm((SLOTS, 8, D), F32), vm((8, D), F32),
             vm((3, D, D), BF16), vm((3, D, D), BF16), vm((2, D, D), BF16), vm((2, D, D), BF16),
-            vm((D, D), BF16), vm((2, HROWS, D), BF16),
+            vm((2, HROWS, D // 2), BF16), vm((2 * ROWS, D // 2), BF16), vm((D, D // 2), BF16), vm((D, D // 2), BF16),
+            vm((2, HROWS, D // 2), BF16),
             vm((5, 8, D), F32), vm((2, 8, D), F32), vm((2, 8, D), F32), vm((2, 8, D), F32),
             vm((3, 8, D), F32), vm((2, 8, D), F32), vm((2, 8, D), F32), vm((3, 2, 8, D), F32),
             dma((11,)), dma((7, 4)), dma((7, 4)), dma((4,)), dma((4,)), dma((3,)), dma((3,)),
-            dma((4, 8)), dma((4, 8)), dma((6,)), dma((6,)), pltpu.SemaphoreType.REGULAR((6,)),
+            dma((6, 8)), dma((6, 8)), dma((6,)), dma((6,)), pltpu.SemaphoreType.REGULAR((6,)),
         ],
         compiler_params=pltpu.CompilerParams(
             vmem_limit_bytes=int(63.5 * (1 << 20)), collective_id=0, has_side_effects=True
         ),
-    )(dl, pc, rank, x, g, cc, cg, wq, wo, wi, w2, small, vectors)
+    )(*args)
+
+
+def hand_out(
+    oc_in, og_in, gc_in, gg_in, gw, sm,
+    oc, og, gc, gg, g_qkv, g_bias, g_attn, b_attn, n1g, n1s, g_in, b_in, g_out, b_out, n2g, n2s, g_table,
+    wide, narrow, sems,
+):
+    ways = ((gc_in, wide.at[0], gc), (gg_in, wide.at[1], gg), (oc_in, narrow.at[0], oc), (og_in, narrow.at[1], og))
+    arrivals = [pltpu.make_async_copy(src, via, sems.at[0, k]) for k, (src, via, _) in enumerate(ways)]
+    copies = [pltpu.make_async_copy(via, dst, sems.at[1, k]) for k, (_, via, dst) in enumerate(ways)]
+    for copy in arrivals:
+        copy.start()
+    g_out[...] = gw[0]
+    g_in[...] = gw[1]
+    g_attn[...] = gw[2, :, 0:QW].T
+    for k in range(3):
+        g_qkv[k, :, 0:HD] = gw[2, :, QW + HD * k:QW + HD * k + HD]
+        g_qkv[k, :, HD:QW] = gw[2, :, 2 * (QW + HD * k):2 * (QW + HD * k) + 2 * HD]
+    for arrival, copy in zip(arrivals, copies):
+        arrival.wait()
+        copy.start()
+    b_in[...] = sm[0, 0:1].reshape(D)
+    g_bias[0:1] = sm[0, 1:2, 0:QW]
+    g_bias[1:2] = sm[0, 1:2, QW:2 * QW]
+    g_table[...] = sm[0, 2:2 + SLOT_HEADS, 0:32]
+    for k, ref in enumerate((b_attn, n1g, n1s, b_out, n2g, n2s)):
+        ref[...] = sm[1, k:k + 1].reshape(D)
+    for copy in copies:
+        copy.wait()
 
 
 def local(
@@ -789,33 +966,38 @@
     content, query_stream, cot_content, cot_query, doc_lengths, rank_order, pred_counts, w_qkv, bias_qv,
     w_attn_out, b_attn_out, norm1_gain, norm1_shift, w_in, b_in, w_out, b_out, norm2_gain, norm2_shift, rel_table,
 ):
-    wide = lambda v: jnp.pad(v.astype(F32), ((0, 0), (0, D - v.shape[1])))
-    line = lambda v: v.astype(F32).reshape(1, D)
-    small = jnp.concatenate([line(b_in), wide(bias_qv), wide(rel_table.T), jnp.zeros((10, D), F32)], axis=0)
-    vectors = jnp.concatenate(
-        [line(v) for v in (b_attn_out, norm1_gain, norm1_shift, b_out, norm2_gain, norm2_shift)]
-        + [jnp.zeros((2, D), F32)],
-        axis=0,
+    out_c, out_g, gc, gg, _, gw, sm = layer(
+        stride, doc_lengths, pred_counts, rank_order, content, query_stream, cot_content, cot_query,
+        jnp.transpose(w_qkv, (0, 2, 1)).reshape(3 * QW, D), w_attn_out, w_in, w_out,
+        b_in, bias_qv, rel_table.T, b_attn_out, norm1_gain, norm1_shift, b_out, norm2_gain, norm2_shift,
     )
-    outs = layer(
-        stride, doc_lengths, rank_order, pred_counts, content, query_stream, cot_content, cot_query,
-        jnp.transpose(w_qkv, (0, 2, 1)).reshape(3 * QW, D), w_attn_out, w_in, w_out, small, vectors,
-    )
-    out_c, out_g, gc, gg, _, gw, sm = outs
     if stride > 1:
         groups = [list(range(k * stride, k * stride + stride)) for k in range(8)]
         gw = lax.psum_scatter(gw, "dp", scatter_dimension=1, axis_index_groups=groups, tiled=True)
         sm = lax.psum(sm, "dp") / 8.0
     rows = gw.shape[1]
-    own, shared = sm[0], sm[1]
-    return (
-        out_c, out_g, gc, gg,
-        jnp.transpose(gw[2, :, 0:3 * QW].reshape(rows, 3, QW), (1, 0, 2)),
-        own[1, 0:2 * QW].reshape(2, QW),
-        gw[2, :, 3 * QW:].T,
-        shared[0], shared[1], shared[2],
-        gw[1], own[0], gw[0].T, shared[3], shared[4], shared[5], own[2:5, 0:32].T,
-    )
+    sd = jax.ShapeDtypeStruct
+    vmem = pl.BlockSpec(memory_space=pltpu.VMEM)
+    hbm = pl.BlockSpec(memory_space=pl.ANY)
+    line = sd((D,), F32)
+    outs = pl.pallas_call(
+        hand_out,
+        out_shape=(
+            sd((S, D), BF16), sd((S, D), BF16), sd((S, D), F32), sd((S, D), F32),
+            sd((3, rows, QW), F32), sd((2, QW), F32), sd((QW, rows), F32), line, line, line,
+            sd((rows, D), F32), line, sd((rows, D), F32), line, line, line, sd((SLOT_HEADS, 32), F32),
+        ),
+        in_specs=[hbm] * 4 + [vmem] * 2,
+        out_specs=[hbm] * 4 + [vmem] * 13,
+        scratch_shapes=[
+            pltpu.VMEM((2, S, D), F32), pltpu.VMEM((2, S, D), BF16), pltpu.SemaphoreType.DMA((2, 4)),
+        ],
+        compiler_params=pltpu.CompilerParams(vmem_limit_bytes=int(63.5 * (1 << 20))),
+    )(out_c, out_g, gc, gg, gw, sm)
+    outs = list(outs)
+    outs[12] = outs[12].T
+    outs[16] = outs[16].T
+    return tuple(outs)
 
 
 def solution(mesh):

time: 213 us -> 159 us (0.75)
  Pallas kernels: 190 us -> 158 us
  local copies, waits for them, and re-layouts: 19.8 us -> 0 us
    pallas_call x1, Pallas kernels: 190 us -> 152 us  [layer(): pl.pallas_call(functools.partial(kernel, stride), out_shape=(sd((S, D), B...]
    unnamed x14 -> x0, local copies, waits for them, and re-layouts: 6.51 us -> none
    pallas_call x0 -> x1, Pallas kernels: none -> 5.81 us  [local(): pl.pallas_call(hand_out, out_shape=(sd((S, D), BF16), sd((S, D), BF16), s...]
    reshape x7 -> x0, local copies, waits for them, and re-layouts: 4.81 us -> none  [local(): line = lambda v: v.astype(F32).reshape(1, D)]
    transpose x3 -> x0, local copies, waits for them, and re-layouts: 3.53 us -> none  [the longest x1 1.9 us: local(): gw[0]]
    slice x4 -> x0, local copies, waits for them, and re-layouts: 2.8 us -> none  [the longest x1 1.68 us: local(): shared[5]]
where the time goes in v2:
time: 159 us
  Pallas kernels  158 us (99%)
    pallas_call x1, Pallas kernels, layer(): pl.pallas_call(functools.partial(kernel, stride), out_shape=(sd((S, D), B...  152 us
    pallas_call x1, Pallas kernels, local(): pl.pallas_call(hand_out, out_shape=(sd((S, D), BF16), sd((S, D), BF16), s...  5.81 us

profile of v2, /device:TPU:0, one launch (start us, length us, event | category | flops | bytes accessed | tf_op | source)
XLA Modules:
  0.0 159.0 jit_solution(4037285036271876746)
XLA Ops:
  0.7 152.4 %shard_map.323 = (bf16[512,768]{1,0:T(8,128)(2,1)}, bf16[512,768]{1,0:T(8,128)(2,1)}, f32[512,768]{1,0:T(8,128)}, f32[512,768]{1,0:T(8,128)}, bf16[4,1024,768]{2...) custom-call(s32[4,8]{1,0:T(4,128)} %dl.1, s32[4]{0:T(128)} %pc.1, s32[4,512]{1,0:T(4,128)} %rank.1, ...), custom_call_target="tpu_custom_call" | custom-call | tf_op jit(solution)/shard_map/pallas_call | solution.py:905
  153.0 5.8 %shard_map.324 = (bf16[512,768]{1,0:T(8,128)(2,1)}, bf16[512,768]{1,0:T(8,128)(2,1)}, f32[512,768]{1,0:T(8,128)}, f32[512,768]{1,0:T(8,128)}, f32[3,96,192]{2,1,...) custom-call(bf16[512,768]{1,0:T(8,128)(2,1)} %get-tuple-element.40.o, ...), custom_call_target="tpu_custom_call" | custom-call | tf_op jit(solution)/shard_map/pallas_call | solution.py:983

commit v3 on v2

v3 whole, which is shorter than its diff:
```python
import functools

import jax
import jax.numpy as jnp
from jax import lax
from jax.experimental import pallas as pl
from jax.experimental.pallas import tpu as pltpu
from jax.sharding import PartitionSpec as P

EDGES = (1, 2, 3, 4, 5, 6, 7, 8, 12, 16, 23, 32, 46, 64, 91)
EPSILON = 1e-05
F32 = jnp.float32
BF16 = jnp.bfloat16
S = 512
HALF = 256
D = 768
HD = 64
SLOTS = 4
SLOT_HEADS = 3
QW = SLOT_HEADS * HD
NEGATIVE = -1e30
ROWS = D // 8
HROWS = D // 2
MESH = pl.DeviceIdType.MESH
ITEMS = (
    (0, 0, 64, 0, 32),
    (0, 64, 80, 0, 48),
    (1, 0, 48, 16, 16),
    (2, 0, 96, 32, 32),
    (2, 96, 96, 32, 32),
    (3, 0, 96, 32, 32),
    (3, 96, 96, 64, 16),
)
FORWARD = {
    "p0": (("s", 0), ("K", 3),),
    "p1": (("s", 1), ("x", 0), ("s", 2),),
    "a00": (("K", 2), ("s", 3), ("x", 1),),
    "a01": (("m", 0),),
    "a02": (("x", 2), ("s", 4), ("K", 0), ("m", 1),),
    "a10": (("l", 0), ("k", 0),),
    "a11": (("s", 6), ("x", 3), ("K", 1),),
    "a20": (("k", 1), ("m", 2), ("l", 1),),
    "a22": (("c", 0),),
    "a30": (("c", 1), ("x", 4),),
    "a31": (("l", 2),),
    "a32": (("c", 2), ("s", 5),),
    "o1": (("m", 3), ("x", 6),),
    "f00": (("m", 4), ("k", 2),),
    "f10": (("x", 5),),
    "f20": (("l", 4), ("l", 3), ("m", 6),),
    "f30": (("c", 4), ("c", 3),),
    "f32": (("m", 5),),
    "g0": (("l", 6), ("k", 3),),
    "g1": (("c", 6),),
    "g2": (("l", 5),),
    "g3": (("c", 5),),
}
KINDS = "xyzxyzyxyzxy"
BACKWARD = {
    "gb3c": (("A1", "YA"),),
    "gb2a": (("A2", "ZA2"),),
    "gb2b": (("A0", "XA"),),
    "gb1a": (("A2", "ZA0"),),
    "tr": (("A0", "XL"), ("A2", "ZM"), ("B0", "XA"),),
    "do": (("B2", "ZA2"), ("B1", "YA"), ("A1", "YF"), ("A2", "ZF"),),
    "xt": (("B0", "XL"),),
    "p3c": (("B2", "ZM"),),
    "p1c": (("B1", "YF"), ("A0", "FN"),),
    "p0a": (("W", "YA"), ("B2", "ZA0"),),
    "p0c": (("C2", "ZA2"),),
    "q3b": (("C0", "XA"), ("C1", "YA"),),
    "q2a": (("B2", "ZF"),),
    "q2b": (("C2", "ZM"),),
    "q1a": (("W", "YF"),),
    "q1b": (("B1", "FN"), ("B0", "FN"),),
    "q0b": (("C1", "YF"), ("C0", "XL"), ("C2", "ZA0"),),
    "t0": (("D1", "YA"),),
    "t3": (("D0", "XA"), ("B2", "FN"),),
    "t4": (("C2", "ZF"), ("A1", "FN"), ("D1", "YF"),),
    "t5": (("A2", "FN"),),
    "t6": (("D0", "XL"), ("C0", "FN"),),
    "t7": (("C2", "FN"), ("C1", "FN"),),
    "t9": (("D1", "FN"), ("W", "FN"), ("D0", "FN"),),
}


def nn(a, b):
    return jnp.dot(a, b, preferred_element_type=F32)


def nt(a, b):
    return lax.dot_general(a, b, (((1,), (1,)), ((), ())), preferred_element_type=F32)


def tn(a, b):
    return lax.dot_general(a, b, (((0,), (0,)), ((), ())), preferred_element_type=F32)


def iota(shape, axis):
    return lax.broadcasted_iota(jnp.int32, shape, axis)


def bucket_onehot():
    lanes = iota((32, S), 1)
    offset = jnp.where(lanes < HALF, -lanes, S - lanes)
    distance = jnp.abs(offset)
    bucket = jnp.where(offset > 0, 16, 0)
    for edge in EDGES:
        bucket = bucket + (distance >= edge).astype(jnp.int32)
    return (bucket == iota((32, S), 0)).astype(F32)


def gelu_pair(v):
    w = v * 0.7071067811865476
    cdf = 0.5 + 0.5 * lax.erf(w)
    return v * cdf, cdf + w * jnp.exp2(w * w * -1.4426950408889634) * 0.5641895835477563


def row_mean(v):
    return jnp.sum(v, axis=-1, keepdims=True) * (1.0 / D)


def col_sum(v):
    return jnp.sum(v, axis=0, keepdims=True)


def kernel(
    stride,
    dl, pc, x_hbm, g_hbm, cc_hbm, cg_hbm, wq_in, wo_in, wi_in, w2_in, rank_hbm,
    b_in_hbm, bias_hbm, table_hbm, b_attn_hbm, n1g_hbm, n1s_hbm, b_out_hbm, n2g_hbm, n2s_hbm,
    oc_hbm, og_hbm, gc_hbm, gg_hbm, stash, g_out, gw_out, sm_out,
    perm, unperm, xin, hid, tA, tB, attn, qkv, qg, xhat, rstd1, act, dg, acc,
    mask, lines, wq, wo, wi, w2, wsm, vectors,
    ga, gb, rca, rcb, first_in, second_a, shared, early, e_core, e_part, e_x, e_y, e_sum, e_z, late_x, l_core, l_part, l_x, l_y, l_sum, l_z,
    rank, b_in, bias_qv, table_in, b_attn_in, n1g_in, n1s_in, b_out_in, n2g_in, n2s_in, g_res, g_w, sm_res, osem, isem,
    lsem, xs, xr, cs, cr, ss, sr, os, orr, ps, pr, credit,
):
    b_attn, n1g, n1s, b_out, n2g, n2s = (vectors.at[k:k + 1] for k in range(6))
    text = diag = lines
    t = lax.axis_index("tensor")
    d = lax.axis_index("dp")
    yb = lax.rem(lax.div(d, stride), 2)
    zb = lax.rem(lax.div(d, 2 * stride), 4)
    zbit = lax.rem(zb, 2)
    z_of = (zb, zb + 1 - 2 * zbit, lax.rem(zb + 2, 4), 3 - zb)
    core = (d, t + 1 - 2 * lax.rem(t, 2))
    xdev = (d, lax.rem(t + 2, 4))
    ydev = (d + stride - 2 * stride * yb, t)
    zdev = [None] + [(d + 2 * stride * (z_of[k] - zb), t) for k in (1, 2, 3)]

    barrier = pltpu.get_barrier_semaphore()
    for who in (core, xdev, ydev, zdev[1], zdev[2], zdev[3]):
        pl.semaphore_signal(barrier, inc=1, device_id=who, device_id_type=MESH)

    def remote(src, dst, send, recv, who):
        return pltpu.make_async_remote_copy(
            src_ref=src, dst_ref=dst, send_sem=send, recv_sem=recv, device_id=who, device_id_type=MESH
        )

    parts = (
        (wq_in, lambda s, lo, n: wq.at[s, pl.ds(lo, n)], 3 * QW),
        (wo_in, lambda s, lo, n: wo.at[pl.ds(s * QW + lo, n)], QW),
        (wi_in, lambda s, lo, n: wi.at[s, pl.ds(lo, n)], D),
        (w2_in, lambda s, lo, n: w2.at[s, pl.ds(lo, n)], D),
    )
    items = ITEMS
    zl = zbit

    def spot(i, y, z, lo=0, n=None):
        p, first, count = items[i][:3]
        at = (2 * y + z) * (parts[p][2] // 4) + first + lo
        return pl.multiple_of(at, 16), count if n is None else n

    def x_copy(i):
        src, place, _ = parts[items[i][0]]
        lo, n = spot(i, yb, zl)
        return remote(src.at[pl.ds(lo, n)], place(2, lo, n), xs.at[i, 0], xr.at[i, 0], xdev)

    def pass_on(i, k, at, slot, who):
        place = parts[items[i][0]][1]
        return remote(place(2, *at), place(slot, *at), xs.at[i, k], xr.at[i, k], who)

    def y_copy(i):
        return pass_on(i, 1, spot(i, yb, zl), 2, ydev)

    def z_copy(i):
        return pass_on(i, 2, spot(i, yb, zl), 2, zdev[1])

    def last_parts(i):
        _, _, n, nx, ny = items[i]
        src, place, _ = parts[items[i][0]]
        lo, count = spot(i, 1 - yb, 1 - zl, 0, nx)
        nz = n - nx - ny
        return (
            nx and (lambda: remote(src.at[pl.ds(lo, count)], place(2, lo, count), xs.at[i, 9], xr.at[i, 9], xdev)),
            ny and (lambda: pass_on(i, 3, spot(i, yb, 1 - zl, nx, ny), 2, ydev)),
            nz and (lambda: pass_on(i, 4, spot(i, 1 - yb, zl, nx + ny, nz), 2, zdev[1])),
        )

    def begin(copy):
        if copy:
            copy().start()

    def x_start(i):
        x_copy(i).start()
        begin(last_parts(i)[0])

    def c_copy(i, k):
        at = (spot(i, yb, zl), spot(i, 1 - yb, zl), spot(i, yb, 1 - zl), spot(i, 1 - yb, 1 - zl))[k]
        return pass_on(i, 5 + k, at, 3, core)

    def core_copy(p):
        src, place, n = parts[p]
        return remote(src, place(1, 0, n), cs.at[p], cr.at[p], core)

    def small_copy(k):
        return remote(wsm.at[2 if k == 3 else 0], wsm.at[k], ss.at[k - 1], sr.at[k - 1], (core, xdev, core)[k - 1])

    def own_copy(p):
        src, place, n = parts[p]
        return pltpu.make_async_copy(src, place(0, 0, n), lsem.at[2 + p])

    def arrived_x(i):
        x_copy(i).wait_recv()
        y_copy(i).start()
        z_copy(i).start()
        c_copy(i, 0).start()

    def arrived_yz(i):
        _, over_y, over_z = last_parts(i)
        y_copy(i).wait_recv()
        begin(over_z)
        c_copy(i, 1).start()
        z_copy(i).wait_recv()
        begin(over_y)
        c_copy(i, 2).start()

    def arrived_last(i):
        for copy in last_parts(i):
            if copy:
                copy().wait_recv()
        c_copy(i, 3).start()

    def arrived_core(i):
        for k in range(4):
            c_copy(i, k).wait_recv()

    def hook(name):
        steps = {
            "s": x_start, "x": arrived_x, "m": arrived_yz, "l": arrived_last, "c": arrived_core,
            "K": lambda p: core_copy(p).start(), "k": lambda p: core_copy(p).wait_recv(),
        }
        for what, which in FORWARD.get(name, ()):
            steps[what](which)

    def at_slot(table, run, s, before, behind):
        for k in range(SLOTS):
            name = before + str(k) + behind
            if name in table:
                pl.when(s == k)(lambda name=name: run(name))

    def hook_at(s, before, behind=""):
        at_slot(FORWARD, hook, s, before, behind)

    def fetch(one, two):
        return [
            pltpu.make_async_copy(one, xin.at[0:S], lsem.at[0]),
            pltpu.make_async_copy(two, xin.at[S:2 * S], lsem.at[1]),
        ]

    def stash_copy(s, back):
        ends = (stash.at[s], dg.at[s]) if back else (dg.at[s], stash.at[s])
        return pltpu.make_async_copy(ends[0], ends[1], lsem.at[7 + s])

    rows_in = fetch(x_hbm, g_hbm)
    for copy in rows_in:
        copy.start()
    own_copy(0).start()
    inputs_in = [
        pltpu.make_async_copy(src, dst, isem.at[k])
        for k, (src, dst) in enumerate((
            (rank_hbm, rank), (b_in_hbm, b_in), (bias_hbm, bias_qv), (table_hbm, table_in), (b_attn_hbm, b_attn_in),
            (n1g_hbm, n1g_in), (n1s_hbm, n1s_in), (b_out_hbm, b_out_in), (n2g_hbm, n2g_in), (n2s_hbm, n2s_in),
        ))
    ]
    for copy in inputs_in:
        copy.start()
    pl.semaphore_wait(barrier, 6)
    hook("p0")
    for copy in inputs_in:
        copy.wait()
    for k, ref in enumerate((b_attn_in, n1g_in, n1s_in, b_out_in, n2g_in, n2s_in)):
        vectors[k:k + 1] = ref[...].astype(F32).reshape(1, D)
    wsm[0] = jnp.zeros((8, D), F32)
    wsm[0, 0:1] = b_in[...].astype(F32).reshape(1, D)
    wsm[0, 1:3, 0:QW] = bias_qv[...].astype(F32)
    wsm[0, 3:3 + SLOT_HEADS, 0:32] = table_in[...].astype(F32)
    for k in (1, 2):
        small_copy(k).start()
    for p in (1, 2, 3):
        own_copy(p).start()
    shared[...] = jnp.zeros(shared.shape, F32)
    early[...] = jnp.zeros(early.shape, F32)
    late_x[...] = jnp.zeros(late_x.shape, F32)

    end = jnp.int32(0)
    start = jnp.int32(0)
    ends = []
    for k in range(8):
        length = dl[t, k]
        start = jnp.where(length == HALF, end, start)
        end = end + length
        ends.append(end)
    limit = (S - pc[t]).astype(F32)
    rows = iota((S, 1), 0)
    lanes = iota((1, S), 1)
    source_r = (rows + start) & (S - 1)
    source_l = (lanes + start) & (S - 1)
    perm[...] = jnp.where(source_r == lanes, 1.0, 0.0).astype(BF16)
    unperm[...] = jnp.where(((rows - start) & (S - 1)) == lanes, 1.0, 0.0).astype(BF16)
    hook("p1")
    doc_r = jnp.zeros((S, 1), F32)
    doc_l = jnp.zeros((1, S), F32)
    for e in ends:
        doc_r = doc_r + jnp.where(source_r >= e, 1.0, 0.0)
        doc_l = doc_l + jnp.where(source_l >= e, 1.0, 0.0)
    rank_row = rank[pl.ds(t, 1), :]
    sub = iota((16, S), 0)
    pieces = jnp.where(sub == 0, rank_row >> 4, jnp.where(sub == 1, rank_row & 15, 0))
    pieces = pieces.astype(F32).astype(BF16)
    ranks = nt(pieces, perm[...])
    rank_l = 16.0 * ranks[0:1] + ranks[1:2]
    ranks = nt(perm[...], pieces)
    rank_r = 16.0 * ranks[:, 0:1] + ranks[:, 1:2]
    lim_c = jnp.maximum(limit - 1.0, rank_l)
    lim_g = jnp.maximum(limit, rank_l) - 1.0
    for b in range(2):
        c = slice(HALF * b, HALF * b + HALF)
        same = doc_r[c] == doc_l[:, c]
        mask[b, :, 0:HALF] = jnp.where(same & (rank_r[c] <= lim_c[:, c]), 0.0, NEGATIVE).astype(BF16)
        mask[b, :, HALF:S] = jnp.where(same & (rank_r[c] <= lim_g[:, c]), 0.0, NEGATIVE).astype(BF16)
    onehot = bucket_onehot()

    def transposed(dst, src):
        for st in range(2):
            r = slice(st * S, st * S + S)
            dst[:, r] = src[r].T

    def permuted(dst):
        for copy in rows_in:
            copy.wait()
        for st in range(2):
            r = slice(st * S, st * S + S)
            for f in (slice(0, HROWS), slice(HROWS, D)):
                dst[r, f] = nn(perm[...], xin[r, f]).astype(BF16)

    xp = hid
    permuted(xp)
    own_copy(0).wait()

    def prob_at(s, h, b, st):
        k = 2 * b + st
        return dg.at[s, k * HALF:k * HALF + HALF, pl.ds(pl.multiple_of(h * HALF, HALF), HALF)]

    @pl.loop(0, SLOTS)
    def _(s):
        hook_at(s, "a", "0")

        @pl.when(s == 1)
        def _():
            small_copy(1).wait_recv()
            small_copy(2).wait_recv()
            small_copy(3).start()

        pl.when(s == 3)(lambda: small_copy(3).wait_recv())

        small = wsm[s].astype(BF16)
        text[pl.ds(pl.multiple_of(8 * s, 8), 8), :] = nn(small[:, 0:32], onehot.astype(BF16))
        sel = jnp.where(iota((8, 128), 0) == 1, 1.0, 0.0).astype(BF16)
        bq = tn(small[:, 0:QW], sel)[:, 0:1]
        sel = jnp.where(iota((8, 128), 0) == 2, 1.0, 0.0).astype(BF16)
        bv = tn(small[:, 0:QW], sel)[:, 0:1]
        r = nt(wq[s], xp[0:S])
        qkv[s, 0:QW] = ((r[0:QW] + bq).astype(BF16) * 0.125).astype(BF16)
        qkv[s, QW:2 * QW] = r[QW:2 * QW].astype(BF16)
        qkv[s, 2 * QW:3 * QW] = (r[2 * QW:3 * QW] + bv).astype(BF16)
        qg[s] = ((nt(wq[s, 0:QW], xp[S:2 * S]) + bq).astype(BF16) * 0.125).astype(BF16)

        hook_at(s, "a", "1")

        units = [(h, b, st) for h in range(SLOT_HEADS) for b in range(2) for st in range(2)]

        def score_at(h, b, st):
            k = 2 * b + st
            return slice(k * HALF, k * HALF + HALF), slice(h * HALF, h * HALF + HALF)

        def block_of(b):
            return slice(HALF * b, HALF * b + HALF)

        for h, b, st in units:
            q = qkv if st == 0 else qg
            lo = h * HD
            acc[score_at(h, b, st)] = tn(qkv[s, QW + lo:QW + lo + HD, block_of(b)], q[s, lo:lo + HD, block_of(b)])

        for h in range(SLOT_HEADS):
            rowvec = text[pl.ds(8 * s + 3 + h, 1), :]
            rolled = pltpu.roll(jnp.broadcast_to(rowvec, (HALF, S)), 0, 1, stride=1, stride_axis=0)
            bias = rolled[:, 0:HALF]
            for b in range(2):
                for st in range(2):
                    sc = acc[score_at(h, b, st)] + bias + mask[b, :, st * HALF:st * HALF + HALF].astype(F32)
                    e = jnp.exp(sc - jnp.max(sc, axis=0, keepdims=True))
                    p = (e * (1.0 / jnp.sum(e, axis=0, keepdims=True))).astype(BF16)
                    dg[(s,) + score_at(h, b, st)] = p

        hook_at(s, "a", "2")

        for h, b, st in units:
            lo = h * HD
            o = nn(qkv[s, 2 * QW + lo:2 * QW + lo + HD, block_of(b)], dg[(s,) + score_at(h, b, st)])
            to = slice(st * S + HALF * b, st * S + HALF * b + HALF)
            tA[pl.ds(pl.multiple_of(s * QW + lo, HD), HD), to] = o.astype(BF16)

        for k in range(SLOTS):
            @pl.when(s == k)
            def _():
                stash_copy(k, False).start()

    hook("o0")
    own_copy(1).wait()
    for st in range(2):
        r = slice(st * S, st * S + S)
        attn[r] = nt(unperm[...], tA[:, r]).astype(BF16)
    hook("o1")
    for r in (slice(k * HALF, k * HALF + HALF) for k in range(4)):
        res = xin[r].astype(F32) + nn(attn[r], wo[...]) + b_attn[...]
        cen = res - row_mean(res)
        rs = lax.rsqrt(row_mean(cen * cen) + EPSILON)
        xh = cen * rs
        xhat[r] = xh.astype(BF16)
        rstd1[r] = rs
        hid[r] = (xh * n1g[...] + n1s[...]).astype(BF16)
    transposed(tB, hid)
    rows_in = fetch(cc_hbm, cg_hbm)
    for copy in rows_in:
        copy.start()

    own_copy(2).wait()
    own_copy(3).wait()
    hook("o2")

    @pl.loop(0, SLOTS)
    def _(s):
        for k in range(SLOTS):
            @pl.when(s == k)
            def _():
                stash_copy(k, False).wait()
        for j in range(0, D, 256):
            hook_at(s, "f", str(j // 256))
            a, g = gelu_pair(nn(hid[...], wi[s, :, j:j + 256]) + wsm[s, 0:1, j:j + 256])
            act[s, :, j:j + 256] = a.astype(BF16)
            dg[s, :, j:j + 256] = g.astype(BF16)

    hook("g0")
    for j in range(0, D, 256):
        acc[:, j:j + 256] = nn(act[0], w2[0, :, j:j + 256])

    @pl.loop(1, SLOTS)
    def _(s):
        hook_at(s, "g")
        for j in range(0, D, 256):
            acc[:, j:j + 256] += nn(act[s], w2[s, :, j:j + 256])

    for copy in rows_in:
        copy.wait()

    @pl.loop(0, 4)
    def _(i):
        r = pl.ds(pl.multiple_of(i * HALF, HALF), HALF)
        res = hid[r, :].astype(F32) + acc[r, :] + b_out[...]
        cen = res - row_mean(res)
        rs = lax.rsqrt(row_mean(cen * cen) + EPSILON)
        xh = cen * rs
        cot = xin[r, :].astype(F32)
        hid[r, :] = (xh * n2g[...] + n2s[...]).astype(BF16)
        dxh = cot * n2g[...]
        dres = rs * (dxh - row_mean(dxh) - xh * row_mean(dxh * xh))
        acc[r, :] = dres
        xin[r, :] = dres.astype(BF16)
        shared[3:4] += col_sum(dres)
        shared[4:5] += col_sum(cot * xh)
        shared[5:6] += col_sum(cot)

    dlow = xin
    transposed(tA, dlow)
    rows_out = [
        pltpu.make_async_copy(hid.at[0:S], oc_hbm, lsem.at[0]),
        pltpu.make_async_copy(hid.at[S:2 * S], og_hbm, lsem.at[1]),
    ]
    for copy in rows_out:
        copy.start()

    def rows_at(lo, n):
        return pl.ds(pl.multiple_of(lo, ROWS), n)

    own_half = rows_at(yb * HROWS, HROWS)
    other_half = rows_at((1 - yb) * HROWS, HROWS)
    zlow, zhigh = zbit, lax.div(zb, 2)
    z_own = rows_at(zlow * HROWS, HROWS)
    z_other = rows_at((1 - zlow) * HROWS, HROWS)
    zy_own = rows_at(zlow * HROWS + yb * 2 * ROWS, 2 * ROWS)
    zy_other = rows_at(zlow * HROWS + (1 - yb) * 2 * ROWS, 2 * ROWS)
    zyz_own = rows_at(zlow * HROWS + yb * 2 * ROWS + zhigh * ROWS, ROWS)
    zyz_other = rows_at(zlow * HROWS + yb * 2 * ROWS + (1 - zhigh) * ROWS, ROWS)

    def block(k):
        return rows_at(yb * HROWS + z_of[k] * ROWS, ROWS)

    def store_at(dst, lo, value, z_first):
        for b in range(8):
            y, z = b % 2, b // 2
            to = ((z % 2) * 4 + y * 2 + z // 2 if z_first else y * 4 + z) * ROWS
            dst[to:to + ROWS, lo:lo + value.shape[1]] = value[b * ROWS:b * ROWS + ROWS, :]

    def store(dst, lead, lo, value, z_first):
        for b in range(8):
            y, z = b % 2, b // 2
            to = ((z % 2) * 4 + y * 2 + z // 2 if z_first else y * 4 + z) * ROWS
            dst[lead, to:to + ROWS, lo:lo + value.shape[1]] = value[b * ROWS:b * ROWS + ROWS, :]

    def add(dst, at, *sources):
        at = slice(None) if at is None else at
        total = dst[at, :]
        for src in sources:
            total = total + src[...]
        dst[at, :] = total

    class Lines:
        def __init__(self, base, given, over_core, part, over_x, over_y, whole_y, over_z):
            self.base, self.given, self.over_core, self.part = base, given, over_core, part
            self.over_x, self.over_y, self.whole_y, self.over_z = over_x, over_y, whole_y, over_z

        def send(self, k):
            sem = ps.at[self.base + k], pr.at[self.base + k]
            if k < 2:
                return remote(self.given.at[(3, 1)[k]], self.over_core.at[k], *sem, core)
            if k == 2:
                return remote(self.part.at[1], self.over_x, *sem, xdev)
            if k == 3:
                return remote(self.part.at[0], self.over_y, *sem, ydev)
            return remote(self.whole_y, self.over_z.at[k - 4], *sem, zdev[k - 3])

        def to_x(self):
            self.send(0).wait_recv()
            self.part[1] = self.given[2] + self.over_core[0]
            self.send(2).start()

        def to_y(self):
            self.send(1).wait_recv()
            self.send(2).wait_recv()
            self.part[0] = self.given[0] + self.over_core[1] + self.over_x[...]
            self.send(3).start()

        def to_z(self):
            self.send(3).wait_recv()
            self.whole_y[...] = self.part[0] + self.over_y[...]
            for k in (4, 5, 6):
                self.send(k).start()

        def total(self):
            for k in (4, 5, 6):
                self.send(k).wait_recv()
            return self.whole_y[...] + self.over_z[0] + self.over_z[1] + self.over_z[2]

    early_sum = Lines(0, early, e_core, e_part, e_x, e_y, e_sum, e_z)
    late_sum = Lines(7, late_x, l_core, l_part, l_x, l_y, l_sum, l_z)

    class Chunk:
        def __init__(self, kind, index, even, odd, rc, parts, out):
            self.kind = kind
            self.n, self.even, self.odd, self.rc, self.out = index, even, odd, rc, out
            self.moves = {}
            for k, (name, src, dst, who) in enumerate(parts):
                self.moves[name] = (src, dst, k + 2, who)

        def core_send(self, k):
            return remote(self.odd[k], self.rc[k], os.at[self.n, k], orr.at[self.n, k], core)

        def move(self, name):
            src, dst, k, who = self.moves[name]
            return remote(src, dst, os.at[self.n, k], orr.at[self.n, k], who)

        def go(self, *names):
            for name in names:
                self.move(name).start()

        def here(self, *names):
            for name in names:
                self.move(name).wait_recv()
            return [self.moves[name][1] for name in names]

        def core_sum(self, k):
            self.core_send(k).wait_recv()
            add(self.even[k], None, self.rc[k])

        def finish(self, at, *names):
            total = self.even[0][at, :].astype(F32)
            for ref in self.here(*names):
                total = total + ref[...].astype(F32)
            self.out[...] = total

        def sent(self):
            for k in (0, 1) if self.n > 5 else (0,):
                self.core_send(k).wait_send()
            for name in self.moves:
                self.move(name).wait_send()

    first, second = pl.ds(0, D // 2), pl.ds(D // 2, D // 2)
    third = [pl.ds(256 * k, 256) for k in range(3)]

    def x_flow(index, even, odd, rc, rx, ry, rz, out):
        e0, e2 = even
        parts = [("x", e2, rx, xdev), ("y", e0.at[other_half], ry, ydev)]
        parts += [("z%d" % k, e0.at[block(k)], rz(k), zdev[k]) for k in (1, 2, 3)]
        return Chunk("x", index, even, odd, rc, parts, out)

    def y_flow(index, even, odd, rc, rx, ry, rz, out):
        e0, e2 = even
        parts = [
            ("y2", e2.at[other_half], ry[1], ydev), ("y0", e0.at[other_half], ry[0], ydev),
            ("x", e2.at[own_half], rx, xdev),
        ]
        parts += [("z%d" % k, e0.at[block(k)], rz(k), zdev[k]) for k in (1, 2, 3)]
        return Chunk("y", index, even, odd, rc, parts, out)

    def z_flow(index, even, odd, rc, rz, ry, rx, rh, out):
        e0, e2 = even
        parts = [
            ("l2", e2.at[z_other], rz[1], zdev[1]), ("l0", e0.at[z_other], rz[0], zdev[1]),
            ("y2", e2.at[zy_other], ry[1], ydev), ("y0", e0.at[zy_other], ry[0], ydev),
            ("x", e2.at[zy_own], rx, xdev), ("h", e0.at[zyz_other], rh, zdev[2]),
        ]
        return Chunk("z", index, even, odd, rc, parts, out)

    def ab_even(g, cols):
        return (g.at[0, :, cols], g.at[1, :, cols]), (g.at[2, :, cols], g.at[2, :, cols])

    def c_even(cols):
        return (act.at[0, 0:D, cols], act.at[2, 0:D, cols]), (act.at[1, 0:D, cols], act.at[3, 0:D, cols])

    def pair(ref, cols):
        return ref.at[0, :, cols], ref.at[1, :, cols]

    def halves(ref):
        return ref.at[0:HROWS], ref.at[HROWS:D]

    def late(slot, k, lo, n):
        return w2.at[slot, lo:lo + n, third[k]]

    chunks = []
    for n, (g, rc) in enumerate(((ga, rca), (gb, rcb))):
        place = (lambda k, lo, c: second_a.at[lo:lo + c, third[k]]) if n == 0 else (lambda k, lo, c: late(0, k, lo, c))
        blocks = lambda k: lambda z: wi.at[n, (z - 1) * ROWS:z * ROWS, third[k]]
        for k in range(3):
            recv = first_in.at[n, k]
            base = 3 * n + k, *ab_even(g, third[k]), pair(rc, third[k])
            out = g_res.at[n, :, third[k]]
            kind = KINDS[3 * n + k]
            if kind == "x":
                chunks.append(x_flow(*base, recv, place(k, 0, HROWS), blocks(k), out))
            elif kind == "y":
                chunks.append(y_flow(*base, place(k, 0, HROWS), halves(recv), blocks(k), out))
            else:
                turns = place(k, 0, 2 * ROWS), place(k, 2 * ROWS, 2 * ROWS)
                chunks.append(z_flow(*base, halves(recv), turns, place(k, 4 * ROWS, 2 * ROWS), blocks(k)(1), out))

    def c_flow(index, k):
        kind = KINDS[index + 1]
        cols = pl.ds(128 * k, 128)
        a, b, out = w2.at[1, :, cols], w2.at[3, :, cols], g_res.at[2, :, cols]
        ends = lambda z: wi.at[3, (z - 1) * ROWS:z * ROWS, cols]
        if kind == "x":
            return x_flow(index, *c_even(cols), pair(rca, cols), a, b.at[0:HROWS], ends, out)
        if kind == "y":
            return y_flow(index, *c_even(cols), pair(rca, cols), b.at[0:HROWS], halves(a), ends, out)
        return z_flow(
            index, *c_even(cols), pair(rca, cols), halves(a), (b.at[0:2 * ROWS], b.at[2 * ROWS:4 * ROWS]),
            b.at[4 * ROWS:6 * ROWS], ends(1), out,
        )

    C0, C1, C2, D0, D1 = (c_flow(6 + k, k) for k in range(5))
    w_slots = [xhat.at[0:D, third[k]] for k in range(3)] + [hid.at[0:D, third[0]]]
    W = y_flow(
        11, (w_slots[0], w_slots[2]), (w_slots[1], w_slots[3]), (w2.at[2, :, third[0]], w2.at[2, :, third[1]]),
        wi.at[2, 0:HROWS, third[0]], halves(w2.at[2, :, third[2]]),
        lambda z: wi.at[2, HROWS + (z - 1) * ROWS:HROWS + z * ROWS, third[0]], g_w,
    )

    A0, A1, A2, B0, B1, B2 = chunks
    named = dict(A0=A0, A1=A1, A2=A2, B0=B0, B1=B1, B2=B2, C0=C0, C1=C1, C2=C2, D0=D0, D1=D1, W=W)

    def buffer_of(s):
        odd = lax.rem(s, 2)
        return 2 * odd + (1 - odd) * lax.div(s, 2)

    def after(s, three, two, one, zero):
        for k, step in ((3, three), (2, two), (1, one), (0, zero)):
            pl.when(s == k)(step)

    def x_arrived(c):
        add(c.even[0], None, *c.here("x"))
        c.go("y")

    def x_last(c):
        add(c.even[0], own_half, *c.here("y"))
        c.go("z1", "z2", "z3")

    def y_arrived(c):
        add(c.even[1], own_half, *c.here("y2"))
        c.go("x")

    def y_final(c):
        add(c.even[0], own_half, *c.here("y0", "x"))
        c.go("z1", "z2", "z3")

    def z_arrived(c, k):
        add(c.even[1 if k == 2 else 0], z_own, *c.here("l%d" % k))
        c.go("y%d" % k)

    def z_middle(c):
        add(c.even[1], zy_own, *c.here("y2"))
        c.go("x")

    def z_final(c):
        add(c.even[0], zy_own, *c.here("y0", "x"))
        c.go("h")

    def steps_of(c):
        if c.kind == "x":
            return {"XA": lambda: x_arrived(c), "XL": lambda: x_last(c), "FN": lambda: c.finish(block(0), "z1", "z2", "z3")}
        if c.kind == "y":
            return {"YA": lambda: y_arrived(c), "YF": lambda: y_final(c), "FN": lambda: c.finish(block(0), "z1", "z2", "z3")}
        return {
            "ZA2": lambda: z_arrived(c, 2), "ZA0": lambda: z_arrived(c, 0), "ZM": lambda: z_middle(c),
            "ZF": lambda: z_final(c), "FN": lambda: c.finish(zyz_own, "h"),
        }

    def turn(name):
        for which, what in BACKWARD.get(name, ()):
            steps_of(named[which])[what]()

    def turn_at(s, before, behind=""):
        at_slot(BACKWARD, turn, s, before, behind)

    def first_steps(*group):
        def odd(k):
            for c in group:
                c.core_send(k).start()

        def two():
            for c in group:
                c.core_sum(1)
                c.go({"x": "x", "y": "y2", "z": "l2"}[c.kind])

        def zero():
            for c in group:
                c.core_sum(0)
                if c.kind != "x":
                    c.go({"y": "y0", "z": "l0"}[c.kind])

        return lambda: odd(1), two, lambda: odd(0), zero

    @pl.loop(0, SLOTS)
    def _(i):
        s = 3 - i

        @pl.when(s == 1)
        def _():
            for c in (A0, A1, A2):
                c.core_send(1).wait_send()

        for k in range(3):
            value = nn(tA[...], act[s, :, 256 * k:256 * k + 256]).astype(BF16)
            store(ga, buffer_of(s), 256 * k, value, KINDS[k] == "z")
        after(s, *first_steps(A0, A1, A2))

    @pl.loop(0, SLOTS)
    def _(i):
        s = 3 - i
        turn_at(s, "gb", "a")
        for j in range(0, D, 256):
            low = (nt(dlow[...], w2[s, j:j + 256, :]) * dg[s, :, j:j + 256].astype(F32)).astype(BF16)
            dg[s, :, j:j + 256] = low
            early[s, 0:1, j:j + 256] = col_sum(low.astype(F32))

        @pl.when(s == 1)
        def _():
            for c in (B0, B1, B2):
                c.core_send(1).wait_send()

        turn_at(s, "gb", "b")
        for k in range(3):
            value = nn(tB[...], dg[s, :, 256 * k:256 * k + 256]).astype(BF16)
            store(gb, buffer_of(s), 256 * k, value, KINDS[3 + k] == "z")
        after(s, *first_steps(B0, B1, B2))
        turn_at(s, "gb", "c")
        for j in range(0, D, 256):
            acc[:, j:j + 256] += nt(dg[s], wi[s, j:j + 256, :])
        for k in range(SLOTS):
            @pl.when(s == k)
            def _():
                stash_copy(k, True).start()

    for p in range(4):
        core_copy(p).wait_send()
    for i in range(len(items)):
        for copy in (x_copy(i), y_copy(i), z_copy(i)):
            copy.wait_send()
        for copy in last_parts(i):
            if copy:
                copy().wait_send()
        for k in range(4):
            c_copy(i, k).wait_send()
    for k in (1, 2, 3):
        small_copy(k).wait_send()
    for k, who in enumerate((core, xdev, ydev, zdev[1], zdev[2], zdev[3])):
        pl.semaphore_signal(credit.at[k], inc=1, device_id=who, device_id_type=MESH)

    turn("ln")
    @pl.loop(0, 4)
    def _(i):
        r = pl.ds(pl.multiple_of(i * HALF, HALF), HALF)
        dy = acc[r, :]
        xh = xhat[r, :].astype(F32)
        dxh = dy * n1g[...]
        dres = rstd1[r, :] * (dxh - row_mean(dxh) - xh * row_mean(dxh * xh))
        acc[r, :] = dres
        xin[r, :] = dres.astype(BF16)
        shared[0:1] += col_sum(dres)
        shared[1:2] += col_sum(dy * xh)
        shared[2:3] += col_sum(dy)

    for k in range(6):
        pl.semaphore_wait(credit.at[k], 1)
    turn("tr")
    transposed(tB, dlow)
    turn("da")
    early[0, 1:7] = shared[0:6]
    for k in range(3):
        early[k + 1, 1:7] = shared[0:6]
    early_sum.send(0).start()
    early_sum.send(1).start()
    for r in (slice(0, HROWS), slice(HROWS, D)):
        tA[r] = nt(wo[r], dlow[...]).astype(BF16)
    for copy in rows_out:
        copy.wait()
    rows_in = fetch(x_hbm, g_hbm)
    for copy in rows_in:
        copy.start()
    turn("wo")
    for k in range(3):
        gwo = nn(tB[...], attn[:, 256 * k:256 * k + 256]).astype(BF16)
        for s in range(SLOTS):
            lo, hi = max(s * QW, 256 * k), min(s * QW + QW, 256 * k + 256)
            if lo < hi:
                ref, base = (xhat, 256 * s) if s < 3 else (hid, 0)
                store_at(ref, base + lo - s * QW, gwo[:, lo - 256 * k:hi - 256 * k], False)
    W.core_send(1).start()
    W.core_send(0).start()
    turn("do")
    for st in range(2):
        r = slice(st * S, st * S + S)
        for f in (slice(0, HROWS), slice(HROWS, D)):
            tA[f, r] = nt(tA[f, r], perm[...]).astype(BF16)
    _, two, _, zero = first_steps(W)
    two()
    zero()
    turn("xp")
    permuted(attn)
    turn("xt")
    transposed(tB, attn)
    xpT = tB

    ones = jnp.ones((16, S), BF16)
    def head_backward(s, h):
        at = (lambda v, m: v) if isinstance(h, int) else pl.multiple_of
        row = at(h * HD, HD)
        column = pl.ds(at(h * HALF, HALF), HALF)
        qr, kr, vr = pl.ds(row, HD), pl.ds(QW + row, HD), pl.ds(2 * QW + row, HD)
        oT = pl.ds(pl.multiple_of(s * QW + row, HD), HD)
        block_of = [slice(0, HALF), slice(HALF, S)]

        def out_grad(b, st):
            return tA[oT, st * S + HALF * b:st * S + HALF * b + HALF]

        def unit(b, st):
            return s, slice((2 * b + st) * HALF, (2 * b + st) * HALF + HALF), column

        pairs = [(b, st) for b in range(2) for st in range(2)]
        dps = [tn(qkv[s, vr, block_of[b]], out_grad(b, st)) for b, st in pairs]
        dv = [sum(nt(out_grad(b, st), dg[unit(b, st)]) for st in range(2)).astype(BF16) for b in range(2)]
        total = None
        for (b, st), dp in zip(pairs, dps):
            pf = dg[unit(b, st)].astype(F32)
            ds = (pf * (dp - jnp.sum(dp * pf, axis=0, keepdims=True))).astype(BF16)
            dg[unit(b, st)] = ds
            total = ds.astype(F32) if total is None else total + ds.astype(F32)
        skewed = jnp.zeros((8, S), F32)
        for a in range(HALF // 8):
            wide = jnp.concatenate([total[8 * a:8 * a + 8, :], jnp.zeros((8, HALF), F32)], axis=1)
            skewed = skewed + (wide if a == 0 else pltpu.roll(wide, S - 8 * a, 1))
        flipped = jnp.concatenate([skewed[7 - i:8 - i] for i in range(8)], axis=0)
        diag[pl.ds(8 * s + h, 1), :] = col_sum(pltpu.roll(flipped, S - 7, 1, stride=1, stride_axis=0))
        grads = []
        for b in range(2):
            kT = qkv[s, kr, block_of[b]]
            d0, d1 = dg[unit(b, 0)], dg[unit(b, 1)]
            dk = nt(qkv[s, qr, block_of[b]], d0) + nt(qg[s, qr, block_of[b]], d1)
            grads.append((nn(kT, d0) * 0.125, nn(kT, d1) * 0.125, dk))
        for b in range(2):
            dq_c, dq_g, dk = grads[b]
            qkv[s, qr, block_of[b]] = dq_c.astype(BF16)
            qg[s, qr, block_of[b]] = dq_g.astype(BF16)
            qkv[s, kr, block_of[b]] = dk.astype(BF16)
            qkv[s, vr, block_of[b]] = dv[b]

    @pl.loop(0, SLOTS)
    def _(i):
        s = 3 - i
        for k in range(SLOTS):
            @pl.when(s == k)
            def _():
                stash_copy(k, True).wait()

        @pl.loop(0, 2)
        def _(h):
            pl.when(h == 0)(lambda: turn_at(s, "p", "a"))
            pl.when(h == 1)(lambda: turn_at(s, "p", "b"))
            head_backward(s, h)

        turn_at(s, "p", "c")
        gq = nt(xpT[:, 0:S], qkv[s, 0:2 * HD])
        extra = nt(xpT[:, S:2 * S], qg[s, 0:2 * HD])
        store(act, s, 0, (gq + extra).astype(BF16), KINDS[7] == "z")
        dkv = jnp.concatenate([qkv[s, k * QW:k * QW + 2 * HD] for k in (1, 2)], axis=0)
        dkv = nt(xpT[:, 0:S], dkv).astype(BF16)
        store(act, s, 2 * HD, dkv[:, 0:2 * HD], KINDS[8] == "z")
        store(act, s, 4 * HD, dkv[:, 2 * HD:], KINDS[9] == "z")

        three, two, one, zero = first_steps(C0, C1, C2)

        def with_three():
            three()
            early_sum.to_x()

        def with_two():
            two()
            early_sum.to_y()

        def with_one():
            one()
            early_sum.to_z()

        after(s, with_three, with_two, with_one, zero)

    @pl.loop(0, SLOTS)
    def _(i):
        s = 3 - i

        turn_at(s, "q", "a")
        head_backward(s, 2)
        turn_at(s, "q", "b")
        dqkv = jnp.concatenate([qkv[s, k * QW + 2 * HD:k * QW + QW] for k in range(3)], axis=0)
        extra = jnp.concatenate([qg[s, 2 * HD:QW], jnp.zeros((2 * HD, S), BF16)], axis=0)
        store(act, s, D // 2, (nt(xpT[:, 0:S], dqkv) + nt(xpT[:, S:2 * S], extra)).astype(BF16), False)

        late_x[s, :, 0:QW] = (nt(ones, qkv[s, 0:QW]) + nt(ones, qg[s]))[0:1]
        late_x[s, :, QW:2 * QW] = nt(ones, qkv[s, 2 * QW:3 * QW])[0:1]
        table = lax.dot_general(
            diag[pl.ds(pl.multiple_of(8 * s, 8), 8), :], onehot, (((1,), (1,)), ((), ())),
            precision=lax.Precision.HIGHEST, preferred_element_type=F32,
        )
        for k in range(SLOT_HEADS):
            late_x[s, :, 2 * QW + 32 * k:2 * QW + 32 * k + 32] = table[k:k + 1]

        three, two, one, zero = first_steps(D0, D1)

        def with_three():
            late_sum.send(0).start()
            three()

        def with_two():
            late_sum.to_x()
            two()

        def with_one():
            late_sum.send(1).start()
            one()

        after(s, with_three, with_two, with_one, zero)

    late_sum.to_y()
    for s in range(SLOTS):
        turn("t%d" % s)
        dg[s, 0:S, 0:3 * QW] = nt(unperm[...], qkv[s]).astype(BF16)
        dg[s, S:2 * S, 0:QW] = nt(unperm[...], qg[s]).astype(BF16)
    late_sum.to_z()
    sm_res[0] = early_sum.total()

    def row_grads(s):
        for j in range(0, D, 256):
            acc[0:S, j:j + 256] += nn(dg[s, 0:S, 0:3 * QW], wq[s, :, j:j + 256])
            acc[S:2 * S, j:j + 256] += nn(dg[s, S:2 * S, 0:QW], wq[s, 0:QW, j:j + 256])

    for s in range(SLOTS):
        turn("t%d" % (SLOTS + s))
        row_grads(s)
    rows_out = [
        pltpu.make_async_copy(acc.at[0:S], gc_hbm, lsem.at[0]),
        pltpu.make_async_copy(acc.at[S:2 * S], gg_hbm, lsem.at[1]),
    ]
    for copy in rows_out:
        copy.start()
    turn("t8")
    sm_res[1, 0:1] = late_sum.total()
    sm_res[1, 1:8] = jnp.zeros((7, D), F32)
    turn("t9")
    g_res[2, :, 5 * 128:] = jnp.zeros((ROWS, 128), F32)
    results = [
        pltpu.make_async_copy(src, dst, osem.at[k])
        for k, (src, dst) in enumerate(((g_res, g_out), (g_w, gw_out), (sm_res, sm_out)))
    ]
    for copy in results:
        copy.start()

    for copy in rows_out:
        copy.wait()
    for k in range(7):
        early_sum.send(k).wait_send()
        late_sum.send(k).wait_send()
    for copy in results:
        copy.wait()
    for chunk in named.values():
        chunk.sent()


def layer(stride, *args):
    smem = pl.BlockSpec(memory_space=pltpu.SMEM)
    hbm = pl.BlockSpec(memory_space=pl.ANY)
    sd = jax.ShapeDtypeStruct
    vm = pltpu.VMEM
    dma = pltpu.SemaphoreType.DMA
    return pl.pallas_call(
        functools.partial(kernel, stride),
        out_shape=(
            sd((S, D), BF16), sd((S, D), BF16), sd((S, D), F32), sd((S, D), F32),
            sd((SLOTS, 2 * S, D), BF16), sd((3, ROWS, D), F32), sd((ROWS, 256), F32), sd((2, 8, D), F32),
        ),
        in_specs=[smem, smem] + [hbm] * 18,
        out_specs=(hbm,) * 8,
        scratch_shapes=[
            vm((S, S), BF16), vm((S, S), BF16), vm((2 * S, D), BF16), vm((2 * S, D), BF16),
            vm((D, 2 * S), BF16), vm((D, 2 * S), BF16), vm((2 * S, D), BF16),
            vm((SLOTS, 3 * QW, S), BF16), vm((SLOTS, QW, S), BF16), vm((2 * S, D), BF16), vm((2 * S, 1), F32),
            vm((SLOTS, 2 * S, D), BF16), vm((SLOTS, 2 * S, D), BF16), vm((2 * S, D), F32),
            vm((2, HALF, S), BF16), vm((32, S), F32),
            vm((SLOTS, 3 * QW, D), BF16), vm((D, D), BF16), vm((SLOTS, D, D), BF16), vm((SLOTS, D, D), BF16),
            vm((SLOTS, 8, D), F32), vm((8, D), F32),
            vm((3, D, D), BF16), vm((3, D, D), BF16), vm((2, D, D), BF16), vm((2, D, D), BF16),
            vm((2, 3, D, 256), BF16), vm((6 * ROWS, D), BF16),
            vm((8, D), F32),
            vm((SLOTS, 8, D), F32), vm((2, 8, D), F32), vm((2, 8, D), F32), vm((8, D), F32), vm((8, D), F32),
            vm((8, D), F32), vm((3, 8, D), F32),
            vm((SLOTS, 1, D), F32), vm((2, 1, D), F32), vm((2, 1, D), F32), vm((1, D), F32), vm((1, D), F32),
            vm((1, D), F32), vm((3, 1, D), F32),
            vm((SLOTS, S), jnp.int32), vm((D,), BF16), vm((2, QW), BF16), vm((SLOT_HEADS, 32), BF16),
            vm((D,), BF16), vm((D,), F32), vm((D,), F32), vm((D,), BF16), vm((D,), F32), vm((D,), F32),
            vm((3, ROWS, D), F32), vm((ROWS, 256), F32), vm((2, 8, D), F32), dma((3,)), dma((10,)),
            dma((11,)), dma((8, 10)), dma((8, 10)), dma((4,)), dma((4,)), dma((3,)), dma((3,)),
            dma((12, 8)), dma((12, 8)), dma((20,)), dma((20,)), pltpu.SemaphoreType.REGULAR((6,)),
        ],
        compiler_params=pltpu.CompilerParams(
            vmem_limit_bytes=int(63.5 * (1 << 20)), collective_id=0, has_side_effects=True
        ),
    )(*args)


def hand_out(
    oc_in, og_in, gc_in, gg_in, gw_hbm, gwo_hbm, sm_hbm,
    oc, og, gc, gg, g_qkv, g_bias, g_attn, b_attn, n1g, n1s, g_in, b_in, g_out, b_out, n2g, n2s, g_table,
    wide, narrow, gw, gwo, sm, v_qkv, v_bias, v_attn, lines, v_table, sems,
):
    def moves(pairs, base):
        copies = [pltpu.make_async_copy(src, dst, sems.at[base + k]) for k, (src, dst) in enumerate(pairs)]
        for copy in copies:
            copy.start()
        return copies

    smalls = moves(((sm_hbm, sm), (gwo_hbm, gwo), (gw_hbm, gw)), 0)
    vias = (wide.at[0], wide.at[1], narrow.at[0], narrow.at[1])
    rows_in = moves(tuple(zip((gc_in, gg_in, oc_in, og_in), vias)), 3)
    for copy in smalls:
        copy.wait()
    v_attn[...] = gwo[:, 0:QW].T
    for k in range(3):
        v_qkv[k, :, 0:2 * HD] = gw[2, :, 2 * HD * k:2 * HD * k + 2 * HD]
        v_qkv[k, :, 2 * HD:QW] = gw[2, :, D // 2 + HD * k:D // 2 + HD * k + HD]
    v_bias[0:1] = sm[1, 0:1, 0:QW]
    v_bias[1:2] = sm[1, 0:1, QW:2 * QW]
    for k in range(SLOT_HEADS):
        v_table[k:k + 1] = sm[1, 0:1, 2 * QW + 32 * k:2 * QW + 32 * k + 32]
    for k, line in enumerate(lines):
        line[...] = sm[0, k:k + 1].reshape(D)
    outs = moves(
        ((gw.at[0], g_out), (gw.at[1], g_in), (v_qkv, g_qkv), (v_attn, g_attn), (v_bias, g_bias), (v_table, g_table))
        + tuple(zip(lines, (b_in, b_attn, n1g, n1s, b_out, n2g, n2s))),
        7,
    )
    for k, (copy, via, dst) in enumerate(zip(rows_in, vias, (gc, gg, oc, og))):
        copy.wait()
        outs += moves(((via, dst),), 20 + k)
    for copy in outs:
        copy.wait()


def local(
    stride,
    content, query_stream, cot_content, cot_query, doc_lengths, rank_order, pred_counts, w_qkv, bias_qv,
    w_attn_out, b_attn_out, norm1_gain, norm1_shift, w_in, b_in, w_out, b_out, norm2_gain, norm2_shift, rel_table,
):
    out_c, out_g, gc, gg, _, gw, gwo, sm = layer(
        stride, doc_lengths, pred_counts, content, query_stream, cot_content, cot_query,
        jnp.transpose(w_qkv, (0, 2, 1)).reshape(3 * QW, D), w_attn_out, w_in, w_out,
        rank_order, b_in, bias_qv, rel_table.T, b_attn_out, norm1_gain, norm1_shift, b_out, norm2_gain, norm2_shift,
    )
    if stride > 1:
        groups = [list(range(k * stride, k * stride + stride)) for k in range(8)]
        gw = lax.psum_scatter(gw, "dp", scatter_dimension=1, axis_index_groups=groups, tiled=True)
        gwo = lax.psum_scatter(gwo, "dp", scatter_dimension=0, axis_index_groups=groups, tiled=True)
        sm = lax.psum(sm, "dp") / 8.0
    rows = gw.shape[1]
    sd = jax.ShapeDtypeStruct
    hbm = pl.BlockSpec(memory_space=pl.ANY)
    vm = pltpu.VMEM
    line = sd((D,), F32)
    outs = pl.pallas_call(
        hand_out,
        out_shape=(
            sd((S, D), BF16), sd((S, D), BF16), sd((S, D), F32), sd((S, D), F32),
            sd((3, rows, QW), F32), sd((2, QW), F32), sd((QW, rows), F32), line, line, line,
            sd((rows, D), F32), line, sd((rows, D), F32), line, line, line, sd((SLOT_HEADS, 32), F32),
        ),
        in_specs=[hbm] * 7,
        out_specs=[hbm] * 17,
        scratch_shapes=[
            vm((2, S, D), F32), vm((2, S, D), BF16), vm((3, rows, D), F32), vm((rows, 256), F32), vm((2, 8, D), F32),
            vm((3, rows, QW), F32), vm((2, QW), F32), vm((QW, rows), F32), [vm((D,), F32)] * 7,
            vm((SLOT_HEADS, 32), F32), pltpu.SemaphoreType.DMA((24,)),
        ],
        compiler_params=pltpu.CompilerParams(vmem_limit_bytes=int(63.5 * (1 << 20))),
    )(out_c, out_g, gc, gg, gw, gwo, sm)
    outs = list(outs)
    outs[12] = outs[12].T
    outs[16] = outs[16].T
    return tuple(outs)


def solution(mesh):
    in_specs = (
        P(("dp", "tensor"), None),
        P(("dp", "tensor"), None),
        P(("dp", "tensor"), None),
        P(("dp", "tensor"), None),
        P("dp", None),
        P("dp", None),
        P("dp"),
        P(None, None, "tensor"),
        P(None, "tensor"),
        P("tensor", None),
        P(),
        P(),
        P(),
        P(None, "tensor"),
        P("tensor"),
        P("tensor", None),
        P(),
        P(),
        P(),
        P(None, "tensor"),
    )
    out_specs = (
        P(("dp", "tensor"), None),
        P(("dp", "tensor"), None),
        P(("dp", "tensor"), None),
        P(("dp", "tensor"), None),
        P(None, "dp", "tensor"),
        P(None, "tensor"),
        P("tensor", "dp"),
        P(),
        P(),
        P(),
        P("dp", "tensor"),
        P("tensor"),
        P("tensor", "dp"),
        P(),
        P(),
        P(),
        P(None, "tensor"),
    )
    stride = mesh.shape["dp"] // 8
    return jax.shard_map(functools.partial(local, stride), mesh=mesh, in_specs=in_specs, out_specs=out_specs, check_vma=False)
```

time: 159 us -> 138 us (0.87)
  Pallas kernels: 158 us -> 137 us
    pallas_call x1, Pallas kernels: 152 us -> 132 us  [layer(): pl.pallas_call(functools.partial(kernel, stride), out_shape=(sd((S, D), B...]
where the time goes in v3:
time: 138 us; the launch traced here: 137 us
  Pallas kernels  137 us (99%)
    pallas_call x1, Pallas kernels, layer(): pl.pallas_call(functools.partial(kernel, stride), out_shape=(sd((S, D), B...  132 us
    pallas_call x1, Pallas kernels, local(): pl.pallas_call(hand_out, out_shape=(sd((S, D), BF16), sd((S, D), BF16), s...  4.95 us

profile of v3, /device:TPU:0, one launch (start us, length us, event | category | flops | bytes accessed | tf_op | source)
XLA Modules:
  0.0 137.4 jit_solution(1061372569785239021)
XLA Ops:
  0.7 131.6 %shard_map.323 = (bf16[512,768]{1,0:T(8,128)(2,1)}, bf16[512,768]{1,0:T(8,128)(2,1)}, f32[512,768]{1,0:T(8,128)}, f32[512,768]{1,0:T(8,128)}, bf16[4,1024,768]{2...) custom-call(s32[4,8]{1,0:T(4,128)} %dl.1, s32[4]{0:T(128)} %pc.1, ...), custom_call_target="tpu_custom_call" | custom-call | tf_op jit(solution)/shard_map/pallas_call | solution.py:1053
  132.3 5.0 %shard_map.324 = (bf16[512,768]{1,0:T(8,128)(2,1)}, bf16[512,768]{1,0:T(8,128)(2,1)}, f32[512,768]{1,0:T(8,128)}, f32[512,768]{1,0:T(8,128)}, f32[3,96,192]{2,1,...) custom-call(bf16[512,768]{1,0:T(8,128)(2,1)} %get-tuple-element.41.o, ...), custom_call_target="tpu_custom_call" | custom-call | tf_op jit(solution)/shard_map/pallas_call | solution.py:1146

commit v4 on v3

--- a/solution.py
+++ b/solution.py
@@ -32,55 +32,55 @@
     (3, 96, 96, 64, 16),
 )
 FORWARD = {
-    "p0": (("s", 0), ("K", 3),),
-    "p1": (("s", 1), ("x", 0), ("s", 2),),
-    "a00": (("K", 2), ("s", 3), ("x", 1),),
-    "a01": (("m", 0),),
-    "a02": (("x", 2), ("s", 4), ("K", 0), ("m", 1),),
-    "a10": (("l", 0), ("k", 0),),
-    "a11": (("s", 6), ("x", 3), ("K", 1),),
-    "a20": (("k", 1), ("m", 2), ("l", 1),),
-    "a22": (("c", 0),),
-    "a30": (("c", 1), ("x", 4),),
-    "a31": (("l", 2),),
-    "a32": (("c", 2), ("s", 5),),
-    "o1": (("m", 3), ("x", 6),),
-    "f00": (("m", 4), ("k", 2),),
-    "f10": (("x", 5),),
-    "f20": (("l", 4), ("l", 3), ("m", 6),),
-    "f30": (("c", 4), ("c", 3),),
-    "f32": (("m", 5),),
-    "g0": (("l", 6), ("k", 3),),
-    "g1": (("c", 6),),
-    "g2": (("l", 5),),
-    "g3": (("c", 5),),
+    "p0": (("s", 1),),
+    "p1": (("K", 0),),
+    "a01": (("s", 0), ("k", 0),),
+    "a02": (("s", 2), ("x", 1), ("K", 3),),
+    "a10": (("K", 1),),
+    "a11": (("s", 4), ("x", 0),),
+    "a12": (("K", 2), ("x", 2), ("s", 3), ("m", 1),),
+    "a20": (("m", 0), ("m", 2), ("s", 5), ("x", 4), ("l", 1), ("l", 0), ("w", 0),),
+    "a22": (("x", 3), ("u", 2), ("k", 1),),
+    "a30": (("l", 2), ("w", 1), ("c", 0), ("s", 6),),
+    "a32": (("m", 4),),
+    "o0": (("x", 5), ("c", 1),),
+    "o2": (("k", 2),),
+    "f01": (("m", 3), ("v", 2),),
+    "f10": (("x", 6), ("u", 3),),
+    "f12": (("l", 4),),
+    "f20": (("l", 3), ("w", 2),),
+    "f30": (("c", 2),),
+    "f31": (("m", 5),),
+    "f32": (("m", 6), ("v", 3),),
+    "g1": (("k", 3),),
+    "g2": (("l", 6), ("l", 5), ("w", 3),),
+    "g3": (("c", 3),),
 }
-KINDS = "xyzxyzyxyzxy"
+KINDS = "xyzxyzxxyzyx"
 BACKWARD = {
-    "gb3c": (("A1", "YA"),),
-    "gb2a": (("A2", "ZA2"),),
-    "gb2b": (("A0", "XA"),),
-    "gb1a": (("A2", "ZA0"),),
-    "tr": (("A0", "XL"), ("A2", "ZM"), ("B0", "XA"),),
-    "do": (("B2", "ZA2"), ("B1", "YA"), ("A1", "YF"), ("A2", "ZF"),),
-    "xt": (("B0", "XL"),),
-    "p3c": (("B2", "ZM"),),
-    "p1c": (("B1", "YF"), ("A0", "FN"),),
-    "p0a": (("W", "YA"), ("B2", "ZA0"),),
-    "p0c": (("C2", "ZA2"),),
-    "q3b": (("C0", "XA"), ("C1", "YA"),),
-    "q2a": (("B2", "ZF"),),
-    "q2b": (("C2", "ZM"),),
-    "q1a": (("W", "YF"),),
-    "q1b": (("B1", "FN"), ("B0", "FN"),),
-    "q0b": (("C1", "YF"), ("C0", "XL"), ("C2", "ZA0"),),
-    "t0": (("D1", "YA"),),
-    "t3": (("D0", "XA"), ("B2", "FN"),),
-    "t4": (("C2", "ZF"), ("A1", "FN"), ("D1", "YF"),),
-    "t5": (("A2", "FN"),),
-    "t6": (("D0", "XL"), ("C0", "FN"),),
-    "t7": (("C2", "FN"), ("C1", "FN"),),
-    "t9": (("D1", "FN"), ("W", "FN"), ("D0", "FN"),),
+    "gb2b": (("A1", "YA"),),
+    "gb1a": (("A2", "ZA2"), ("A0", "XA"),),
+    "tr": (("B1", "YA"), ("B0", "XA"), ("A1", "YF"),),
+    "do": (("A0", "XL"), ("A2", "ZM"),),
+    "p3a": (("A2", "ZA0"), ("B0", "XL"),),
+    "p2a": (("B2", "ZA2"),),
+    "p2b": (("B1", "YF"),),
+    "p2c": (("B2", "ZA0"), ("A2", "ZF"),),
+    "p1b": (("B2", "ZM"),),
+    "p0a": (("W", "XA"),),
+    "q2a": (("C2", "ZA2"), ("B2", "ZF"), ("C1", "YA"),),
+    "q1a": (("W", "XL"),),
+    "q1b": (("C0", "XA"), ("A0", "FN"),),
+    "q0b": (("A2", "FN"), ("C2", "ZM"), ("C1", "YF"), ("C2", "ZA0"),),
+    "t0": (("D0", "YA"),),
+    "t2": (("C0", "XL"), ("D1", "XA"),),
+    "t3": (("C2", "ZF"),),
+    "t4": (("A1", "FN"),),
+    "t5": (("D0", "YF"), ("B2", "FN"),),
+    "t6": (("W", "FN"), ("D1", "XL"),),
+    "t7": (("C0", "FN"),),
+    "t8": (("D0", "FN"), ("C1", "FN"), ("B0", "FN"),),
+    "t9": (("B1", "FN"), ("C2", "FN"), ("D1", "FN"),),
 }
 
 
@@ -128,11 +128,11 @@
     stride,
     dl, pc, x_hbm, g_hbm, cc_hbm, cg_hbm, wq_in, wo_in, wi_in, w2_in, rank_hbm,
     b_in_hbm, bias_hbm, table_hbm, b_attn_hbm, n1g_hbm, n1s_hbm, b_out_hbm, n2g_hbm, n2s_hbm,
-    oc_hbm, og_hbm, gc_hbm, gg_hbm, stash, g_out, gw_out, sm_out,
+    oc_hbm, og_hbm, gc_hbm, gg_hbm, stash, kept, g_out, gw_out, sm_out,
     perm, unperm, xin, hid, tA, tB, attn, qkv, qg, xhat, rstd1, act, dg, acc,
     mask, lines, wq, wo, wi, w2, wsm, vectors,
     ga, gb, rca, rcb, first_in, second_a, shared, early, e_core, e_part, e_x, e_y, e_sum, e_z, late_x, l_core, l_part, l_x, l_y, l_sum, l_z,
-    rank, b_in, bias_qv, table_in, b_attn_in, n1g_in, n1s_in, b_out_in, n2g_in, n2s_in, g_res, g_w, sm_res, osem, isem,
+    rank, b_in, bias_qv, table_in, b_attn_in, n1g_in, n1s_in, b_out_in, n2g_in, n2s_in, g_res, g_w, sm_res, osem, isem, gs, gr, ks, kr,
     lsem, xs, xr, cs, cr, ss, sr, os, orr, ps, pr, credit,
 ):
     b_attn, n1g, n1s, b_out, n2g, n2s = (vectors.at[k:k + 1] for k in range(6))
@@ -174,11 +174,11 @@
     def x_copy(i):
         src, place, _ = parts[items[i][0]]
         lo, n = spot(i, yb, zl)
-        return remote(src.at[pl.ds(lo, n)], place(2, lo, n), xs.at[i, 0], xr.at[i, 0], xdev)
+        return remote(src.at[pl.ds(lo, n)], place(2, lo, n), xs.at[0], xr.at[i, 0], xdev)
 
     def pass_on(i, k, at, slot, who):
         place = parts[items[i][0]][1]
-        return remote(place(2, *at), place(slot, *at), xs.at[i, k], xr.at[i, k], who)
+        return remote(place(2, *at), place(slot, *at), xs.at[0], xr.at[i, k], who)
 
     def y_copy(i):
         return pass_on(i, 1, spot(i, yb, zl), 2, ydev)
@@ -192,7 +192,7 @@
         lo, count = spot(i, 1 - yb, 1 - zl, 0, nx)
         nz = n - nx - ny
         return (
-            nx and (lambda: remote(src.at[pl.ds(lo, count)], place(2, lo, count), xs.at[i, 9], xr.at[i, 9], xdev)),
+            nx and (lambda: remote(src.at[pl.ds(lo, count)], place(2, lo, count), xs.at[0], xr.at[i, 5], xdev)),
             ny and (lambda: pass_on(i, 3, spot(i, yb, 1 - zl, nx, ny), 2, ydev)),
             nz and (lambda: pass_on(i, 4, spot(i, 1 - yb, zl, nx + ny, nz), 2, zdev[1])),
         )
@@ -205,13 +205,18 @@
         x_copy(i).start()
         begin(last_parts(i)[0])
 
-    def c_copy(i, k):
-        at = (spot(i, yb, zl), spot(i, 1 - yb, zl), spot(i, yb, 1 - zl), spot(i, 1 - yb, 1 - zl))[k]
-        return pass_on(i, 5 + k, at, 3, core)
+    def c_copy(p, k):
+        place, n = parts[p][1:]
+        if p < 2:
+            at = 0, n
+        else:
+            y, z = ((yb, zl), (1 - yb, zl), (yb, 1 - zl), (1 - yb, 1 - zl))[k]
+            at = pl.multiple_of((2 * y + z) * (n // 4), 16), n // 4
+        return remote(place(2, *at), place(3, *at), ks.at[0], kr.at[p], core)
 
     def core_copy(p):
         src, place, n = parts[p]
-        return remote(src, place(1, 0, n), cs.at[p], cr.at[p], core)
+        return remote(src, place(1, 0, n), cs.at[0], cr.at[p], core)
 
     def small_copy(k):
         return remote(wsm.at[2 if k == 3 else 0], wsm.at[k], ss.at[k - 1], sr.at[k - 1], (core, xdev, core)[k - 1])
@@ -224,30 +229,34 @@
         x_copy(i).wait_recv()
         y_copy(i).start()
         z_copy(i).start()
-        c_copy(i, 0).start()
 
     def arrived_yz(i):
         _, over_y, over_z = last_parts(i)
         y_copy(i).wait_recv()
         begin(over_z)
-        c_copy(i, 1).start()
         z_copy(i).wait_recv()
         begin(over_y)
-        c_copy(i, 2).start()
 
     def arrived_last(i):
         for copy in last_parts(i):
             if copy:
                 copy().wait_recv()
-        c_copy(i, 3).start()
-
-    def arrived_core(i):
-        for k in range(4):
-            c_copy(i, k).wait_recv()
+
+    def drain(ref, sem):
+        pltpu.make_async_copy(ref, ref, sem).wait()
+
+    def arrived_core(p):
+        place, n = parts[p][1:]
+        drain(place(3, 0, n), kr.at[p])
+
+    def to_core(p, which):
+        for k in (0,) if p < 2 else which:
+            c_copy(p, k).start()
 
     def hook(name):
         steps = {
             "s": x_start, "x": arrived_x, "m": arrived_yz, "l": arrived_last, "c": arrived_core,
+            "u": lambda p: to_core(p, (0,)), "v": lambda p: to_core(p, (1, 2)), "w": lambda p: to_core(p, (3,)),
             "K": lambda p: core_copy(p).start(), "k": lambda p: core_copy(p).wait_recv(),
         }
         for what, which in FORWARD.get(name, ()):
@@ -267,6 +276,10 @@
             pltpu.make_async_copy(one, xin.at[0:S], lsem.at[0]),
             pltpu.make_async_copy(two, xin.at[S:2 * S], lsem.at[1]),
         ]
+
+    def kept_copy(back):
+        ends = (kept, tB) if back else (tB, kept)
+        return pltpu.make_async_copy(ends[0], ends[1], lsem.at[11])
 
     def stash_copy(s, back):
         ends = (stash.at[s], dg.at[s]) if back else (dg.at[s], stash.at[s])
@@ -364,6 +377,15 @@
 
     @pl.loop(0, SLOTS)
     def _(s):
+
+        @pl.when(s == 2)
+        def _():
+            transposed(tB, xp)
+            kept_copy(False).start()
+            for st in range(2):
+                r = slice(st * S, st * S + S)
+                attn[r, 0:2 * QW] = nt(unperm[...], tA[0:2 * QW, r]).astype(BF16)
+
         hook_at(s, "a", "0")
 
         @pl.when(s == 1)
@@ -430,7 +452,7 @@
     own_copy(1).wait()
     for st in range(2):
         r = slice(st * S, st * S + S)
-        attn[r] = nt(unperm[...], tA[:, r]).astype(BF16)
+        attn[r, 2 * QW:] = nt(unperm[...], tA[2 * QW:, r]).astype(BF16)
     hook("o1")
     for r in (slice(k * HALF, k * HALF + HALF) for k in range(4)):
         res = xin[r].astype(F32) + nn(attn[r], wo[...]) + b_attn[...]
@@ -440,6 +462,7 @@
         xhat[r] = xh.astype(BF16)
         rstd1[r] = rs
         hid[r] = (xh * n1g[...] + n1s[...]).astype(BF16)
+    kept_copy(False).wait()
     transposed(tB, hid)
     rows_in = fetch(cc_hbm, cg_hbm)
     for copy in rows_in:
@@ -575,20 +598,26 @@
     early_sum = Lines(0, early, e_core, e_part, e_x, e_y, e_sum, e_z)
     late_sum = Lines(7, late_x, l_core, l_part, l_x, l_y, l_sum, l_z)
 
+    def piece(z, lo=0):
+        return slice(lo, lo + 3 * ROWS) if z == 0 else slice(lo + (z - 1) * ROWS, lo + z * ROWS)
+
     class Chunk:
-        def __init__(self, kind, index, even, odd, rc, parts, out):
-            self.kind = kind
-            self.n, self.even, self.odd, self.rc, self.out = index, even, odd, rc, out
+        def __init__(self, kind, index, even, parts, out, ends=None):
+            self.kind, self.ends = kind, ends
+            self.n, self.even, self.out = index, even, out
+            self.base = sum({"x": 3, "y": 4, "z": 6}[KINDS[k + (k > 5)]] for k in range(index)) if index < 11 else 0
+            if index == 11:
+                self.base = sum({"x": 3, "y": 4, "z": 6}[KINDS[k]] for k in range(12) if k != 6)
+            slots = {"z1": 0, "z2": 0, "z3": 0}
             self.moves = {}
             for k, (name, src, dst, who) in enumerate(parts):
-                self.moves[name] = (src, dst, k + 2, who)
-
-        def core_send(self, k):
-            return remote(self.odd[k], self.rc[k], os.at[self.n, k], orr.at[self.n, k], core)
+                if name not in slots:
+                    slots[name] = len(slots) - (3 if kind == "z" else 2)
+                self.moves[name] = (src, dst, slots[name], who)
 
         def move(self, name):
             src, dst, k, who = self.moves[name]
-            return remote(src, dst, os.at[self.n, k], orr.at[self.n, k], who)
+            return remote(src, dst, os.at[self.n // 6], orr.at[self.base + k], who)
 
         def go(self, *names):
             for name in names:
@@ -599,54 +628,45 @@
                 self.move(name).wait_recv()
             return [self.moves[name][1] for name in names]
 
-        def core_sum(self, k):
-            self.core_send(k).wait_recv()
-            add(self.even[k], None, self.rc[k])
-
         def finish(self, at, *names):
             total = self.even[0][at, :].astype(F32)
-            for ref in self.here(*names):
+            if len(names) > 1:
+                drain(self.ends, orr.at[self.base])
+            else:
+                self.here(*names)
+            for ref in (self.moves[name][1] for name in names):
                 total = total + ref[...].astype(F32)
             self.out[...] = total
 
-        def sent(self):
-            for k in (0, 1) if self.n > 5 else (0,):
-                self.core_send(k).wait_send()
-            for name in self.moves:
-                self.move(name).wait_send()
-
     first, second = pl.ds(0, D // 2), pl.ds(D // 2, D // 2)
     third = [pl.ds(256 * k, 256) for k in range(3)]
 
-    def x_flow(index, even, odd, rc, rx, ry, rz, out):
+    def x_flow(index, even, rx, ry, rz, out):
         e0, e2 = even
         parts = [("x", e2, rx, xdev), ("y", e0.at[other_half], ry, ydev)]
         parts += [("z%d" % k, e0.at[block(k)], rz(k), zdev[k]) for k in (1, 2, 3)]
-        return Chunk("x", index, even, odd, rc, parts, out)
-
-    def y_flow(index, even, odd, rc, rx, ry, rz, out):
+        return Chunk("x", index, even, parts, out, rz(0))
+
+    def y_flow(index, even, rx, ry, rz, out):
         e0, e2 = even
         parts = [
             ("y2", e2.at[other_half], ry[1], ydev), ("y0", e0.at[other_half], ry[0], ydev),
             ("x", e2.at[own_half], rx, xdev),
         ]
         parts += [("z%d" % k, e0.at[block(k)], rz(k), zdev[k]) for k in (1, 2, 3)]
-        return Chunk("y", index, even, odd, rc, parts, out)
-
-    def z_flow(index, even, odd, rc, rz, ry, rx, rh, out):
+        return Chunk("y", index, even, parts, out, rz(0))
+
+    def z_flow(index, even, rz, ry, rx, rh, out):
         e0, e2 = even
         parts = [
             ("l2", e2.at[z_other], rz[1], zdev[1]), ("l0", e0.at[z_other], rz[0], zdev[1]),
             ("y2", e2.at[zy_other], ry[1], ydev), ("y0", e0.at[zy_other], ry[0], ydev),
             ("x", e2.at[zy_own], rx, xdev), ("h", e0.at[zyz_other], rh, zdev[2]),
         ]
-        return Chunk("z", index, even, odd, rc, parts, out)
-
-    def ab_even(g, cols):
-        return (g.at[0, :, cols], g.at[1, :, cols]), (g.at[2, :, cols], g.at[2, :, cols])
+        return Chunk("z", index, even, parts, out)
 
     def c_even(cols):
-        return (act.at[0, 0:D, cols], act.at[2, 0:D, cols]), (act.at[1, 0:D, cols], act.at[3, 0:D, cols])
+        return act.at[0, 0:D, cols], act.at[2, 0:D, cols]
 
     def pair(ref, cols):
         return ref.at[0, :, cols], ref.at[1, :, cols]
@@ -660,10 +680,10 @@
     chunks = []
     for n, (g, rc) in enumerate(((ga, rca), (gb, rcb))):
         place = (lambda k, lo, c: second_a.at[lo:lo + c, third[k]]) if n == 0 else (lambda k, lo, c: late(0, k, lo, c))
-        blocks = lambda k: lambda z: wi.at[n, (z - 1) * ROWS:z * ROWS, third[k]]
+        blocks = lambda k: lambda z: wi.at[n, piece(z), third[k]]
         for k in range(3):
             recv = first_in.at[n, k]
-            base = 3 * n + k, *ab_even(g, third[k]), pair(rc, third[k])
+            base = 3 * n + k, pair(g, third[k])
             out = g_res.at[n, :, third[k]]
             kind = KINDS[3 * n + k]
             if kind == "x":
@@ -678,26 +698,61 @@
         kind = KINDS[index + 1]
         cols = pl.ds(128 * k, 128)
         a, b, out = w2.at[1, :, cols], w2.at[3, :, cols], g_res.at[2, :, cols]
-        ends = lambda z: wi.at[3, (z - 1) * ROWS:z * ROWS, cols]
+        ends = lambda z: wi.at[3, piece(z), cols]
         if kind == "x":
-            return x_flow(index, *c_even(cols), pair(rca, cols), a, b.at[0:HROWS], ends, out)
+            return x_flow(index, c_even(cols), a, b.at[0:HROWS], ends, out)
         if kind == "y":
-            return y_flow(index, *c_even(cols), pair(rca, cols), b.at[0:HROWS], halves(a), ends, out)
+            return y_flow(index, c_even(cols), b.at[0:HROWS], halves(a), ends, out)
         return z_flow(
-            index, *c_even(cols), pair(rca, cols), halves(a), (b.at[0:2 * ROWS], b.at[2 * ROWS:4 * ROWS]),
+            index, c_even(cols), halves(a), (b.at[0:2 * ROWS], b.at[2 * ROWS:4 * ROWS]),
             b.at[4 * ROWS:6 * ROWS], ends(1), out,
         )
 
     C0, C1, C2, D0, D1 = (c_flow(6 + k, k) for k in range(5))
     w_slots = [xhat.at[0:D, third[k]] for k in range(3)] + [hid.at[0:D, third[0]]]
-    W = y_flow(
-        11, (w_slots[0], w_slots[2]), (w_slots[1], w_slots[3]), (w2.at[2, :, third[0]], w2.at[2, :, third[1]]),
-        wi.at[2, 0:HROWS, third[0]], halves(w2.at[2, :, third[2]]),
-        lambda z: wi.at[2, HROWS + (z - 1) * ROWS:HROWS + z * ROWS, third[0]], g_w,
+    W = x_flow(
+        11, (w_slots[0], w_slots[2]),
+        w2.at[2, :, third[2]], wi.at[2, 0:HROWS, third[0]],
+        lambda z: wi.at[2, piece(z, HROWS), third[0]], g_w,
     )
 
     A0, A1, A2, B0, B1, B2 = chunks
     named = dict(A0=A0, A1=A1, A2=A2, B0=B0, B1=B1, B2=B2, C0=C0, C1=C1, C2=C2, D0=D0, D1=D1, W=W)
+
+    class Group:
+        def __init__(self, index, even, odd, rc, *members):
+            self.n, self.even, self.odd, self.rc, self.members = index, even, odd, rc, members
+
+        def send(self, k):
+            return remote(self.odd[k], self.rc[k], gs.at[self.n, k], gr.at[self.n, k], core)
+
+        def sum(self, k):
+            self.send(k).wait_recv()
+            add(self.even[k], None, self.rc[k])
+            for c in self.members:
+                if k == 1:
+                    c.go({"x": "x", "y": "y2", "z": "l2"}[c.kind])
+                elif c.kind != "x":
+                    c.go({"y": "y0", "z": "l0"}[c.kind])
+
+        def steps(self):
+            return (
+                lambda: self.send(1).start(), lambda: self.sum(1), lambda: self.send(0).start(), lambda: self.sum(0),
+            )
+
+    def c_group(index, cols, *members):
+        odd = act.at[1, 0:D, cols], act.at[3, 0:D, cols]
+        return Group(index, c_even(cols), odd, pair(rca, cols), *members)
+
+    every = pl.ds(0, D)
+    GA = Group(0, pair(ga, every), (ga.at[2], ga.at[2]), pair(rca, every), A0, A1, A2)
+    GB = Group(1, pair(gb, every), (gb.at[2], gb.at[2]), pair(rcb, every), B0, B1, B2)
+    GC = c_group(2, first, C0, C1, C2)
+    GD = c_group(3, pl.ds(D // 2, 256), D0, D1)
+    GW = Group(
+        4, (w_slots[0], w_slots[2]), (w_slots[1], w_slots[3]),
+        (w2.at[2, :, third[0]], w2.at[2, :, third[1]]), W,
+    )
 
     def buffer_of(s):
         odd = lax.rem(s, 2)
@@ -752,37 +807,21 @@
     def turn_at(s, before, behind=""):
         at_slot(BACKWARD, turn, s, before, behind)
 
-    def first_steps(*group):
-        def odd(k):
-            for c in group:
-                c.core_send(k).start()
-
-        def two():
-            for c in group:
-                c.core_sum(1)
-                c.go({"x": "x", "y": "y2", "z": "l2"}[c.kind])
-
-        def zero():
-            for c in group:
-                c.core_sum(0)
-                if c.kind != "x":
-                    c.go({"y": "y0", "z": "l0"}[c.kind])
-
-        return lambda: odd(1), two, lambda: odd(0), zero
-
     @pl.loop(0, SLOTS)
     def _(i):
         s = 3 - i
 
-        @pl.when(s == 1)
-        def _():
-            for c in (A0, A1, A2):
-                c.core_send(1).wait_send()
-
+        pl.when(s == 1)(lambda: GA.send(1).wait_send())
         for k in range(3):
             value = nn(tA[...], act[s, :, 256 * k:256 * k + 256]).astype(BF16)
             store(ga, buffer_of(s), 256 * k, value, KINDS[k] == "z")
-        after(s, *first_steps(A0, A1, A2))
+
+        def one():
+            GA.send(0).start()
+            GA.sum(1)
+
+        pl.when(s == 3)(lambda: GA.send(1).start())
+        pl.when(s == 1)(one)
 
     @pl.loop(0, SLOTS)
     def _(i):
@@ -793,16 +832,13 @@
             dg[s, :, j:j + 256] = low
             early[s, 0:1, j:j + 256] = col_sum(low.astype(F32))
 
-        @pl.when(s == 1)
-        def _():
-            for c in (B0, B1, B2):
-                c.core_send(1).wait_send()
-
+        pl.when(s == 3)(lambda: GA.sum(0))
+        pl.when(s == 1)(lambda: GB.send(1).wait_send())
         turn_at(s, "gb", "b")
         for k in range(3):
             value = nn(tB[...], dg[s, :, 256 * k:256 * k + 256]).astype(BF16)
             store(gb, buffer_of(s), 256 * k, value, KINDS[3 + k] == "z")
-        after(s, *first_steps(B0, B1, B2))
+        after(s, *GB.steps())
         turn_at(s, "gb", "c")
         for j in range(0, D, 256):
             acc[:, j:j + 256] += nt(dg[s], wi[s, j:j + 256, :])
@@ -811,16 +847,8 @@
             def _():
                 stash_copy(k, True).start()
 
-    for p in range(4):
-        core_copy(p).wait_send()
-    for i in range(len(items)):
-        for copy in (x_copy(i), y_copy(i), z_copy(i)):
-            copy.wait_send()
-        for copy in last_parts(i):
-            if copy:
-                copy().wait_send()
-        for k in range(4):
-            c_copy(i, k).wait_send()
+    for sem in (xs, ks, cs):
+        drain(w2.at[0:3], sem.at[0])
     for k in (1, 2, 3):
         small_copy(k).wait_send()
     for k, who in enumerate((core, xdev, ydev, zdev[1], zdev[2], zdev[3])):
@@ -854,9 +882,6 @@
         tA[r] = nt(wo[r], dlow[...]).astype(BF16)
     for copy in rows_out:
         copy.wait()
-    rows_in = fetch(x_hbm, g_hbm)
-    for copy in rows_in:
-        copy.start()
     turn("wo")
     for k in range(3):
         gwo = nn(tB[...], attn[:, 256 * k:256 * k + 256]).astype(BF16)
@@ -865,20 +890,19 @@
             if lo < hi:
                 ref, base = (xhat, 256 * s) if s < 3 else (hid, 0)
                 store_at(ref, base + lo - s * QW, gwo[:, lo - 256 * k:hi - 256 * k], False)
-    W.core_send(1).start()
-    W.core_send(0).start()
+    kept_copy(True).start()
+    GW.send(1).start()
+    GW.send(0).start()
     turn("do")
     for st in range(2):
         r = slice(st * S, st * S + S)
         for f in (slice(0, HROWS), slice(HROWS, D)):
             tA[f, r] = nt(tA[f, r], perm[...]).astype(BF16)
-    _, two, _, zero = first_steps(W)
-    two()
-    zero()
+    GW.sum(1)
     turn("xp")
-    permuted(attn)
     turn("xt")
-    transposed(tB, attn)
+    kept_copy(True).wait()
+    GW.sum(0)
     xpT = tB
 
     ones = jnp.ones((16, S), BF16)
@@ -947,7 +971,7 @@
         store(act, s, 2 * HD, dkv[:, 0:2 * HD], KINDS[8] == "z")
         store(act, s, 4 * HD, dkv[:, 2 * HD:], KINDS[9] == "z")
 
-        three, two, one, zero = first_steps(C0, C1, C2)
+        three, two, one, zero = GC.steps()
 
         def with_three():
             three()
@@ -983,7 +1007,7 @@
         for k in range(SLOT_HEADS):
             late_x[s, :, 2 * QW + 32 * k:2 * QW + 32 * k + 32] = table[k:k + 1]
 
-        three, two, one, zero = first_steps(D0, D1)
+        three, two, one, zero = GD.steps()
 
         def with_three():
             late_sum.send(0).start()
@@ -1024,6 +1048,15 @@
     turn("t8")
     sm_res[1, 0:1] = late_sum.total()
     sm_res[1, 1:8] = jnp.zeros((7, D), F32)
+    drain(dg.at[0:3, 0:960], os.at[0])
+    for group in (GA, GB):
+        group.send(0).wait_send()
+    for group in (GC, GD, GW):
+        group.send(0).wait_send()
+        group.send(1).wait_send()
+    for k in range(7):
+        early_sum.send(k).wait_send()
+        late_sum.send(k).wait_send()
     turn("t9")
     g_res[2, :, 5 * 128:] = jnp.zeros((ROWS, 128), F32)
     results = [
@@ -1035,13 +1068,9 @@
 
     for copy in rows_out:
         copy.wait()
-    for k in range(7):
-        early_sum.send(k).wait_send()
-        late_sum.send(k).wait_send()
     for copy in results:
         copy.wait()
-    for chunk in named.values():
-        chunk.sent()
+    drain(dg.at[0:3, 0:560], os.at[1])
 
 
 def layer(stride, *args):
@@ -1054,10 +1083,10 @@
         functools.partial(kernel, stride),
         out_shape=(
             sd((S, D), BF16), sd((S, D), BF16), sd((S, D), F32), sd((S, D), F32),
-            sd((SLOTS, 2 * S, D), BF16), sd((3, ROWS, D), F32), sd((ROWS, 256), F32), sd((2, 8, D), F32),
+            sd((SLOTS, 2 * S, D), BF16), sd((D, 2 * S), BF16), sd((3, ROWS, D), F32), sd((ROWS, 256), F32), sd((2, 8, D), F32),
         ),
         in_specs=[smem, smem] + [hbm] * 18,
-        out_specs=(hbm,) * 8,
+        out_specs=(hbm,) * 9,
         scratch_shapes=[
             vm((S, S), BF16), vm((S, S), BF16), vm((2 * S, D), BF16), vm((2 * S, D), BF16),
             vm((D, 2 * S), BF16), vm((D, 2 * S), BF16), vm((2 * S, D), BF16),
@@ -1075,9 +1104,9 @@
             vm((1, D), F32), vm((3, 1, D), F32),
             vm((SLOTS, S), jnp.int32), vm((D,), BF16), vm((2, QW), BF16), vm((SLOT_HEADS, 32), BF16),
             vm((D,), BF16), vm((D,), F32), vm((D,), F32), vm((D,), BF16), vm((D,), F32), vm((D,), F32),
-            vm((3, ROWS, D), F32), vm((ROWS, 256), F32), vm((2, 8, D), F32), dma((3,)), dma((10,)),
-            dma((11,)), dma((8, 10)), dma((8, 10)), dma((4,)), dma((4,)), dma((3,)), dma((3,)),
-            dma((12, 8)), dma((12, 8)), dma((20,)), dma((20,)), pltpu.SemaphoreType.REGULAR((6,)),
+            vm((3, ROWS, D), F32), vm((ROWS, 256), F32), vm((2, 8, D), F32), dma((3,)), dma((10,)), dma((5, 2)), dma((5, 2)), dma((1,)), dma((4,)),
+            dma((12,)), dma((1,)), dma((len(ITEMS), 6)), dma((1,)), dma((4,)), dma((3,)), dma((3,)),
+            dma((2,)), dma((sum({"x": 3, "y": 4, "z": 6}[k] for k in KINDS),)), dma((14,)), dma((14,)), pltpu.SemaphoreType.REGULAR((6,)),
         ],
         compiler_params=pltpu.CompilerParams(
             vmem_limit_bytes=int(63.5 * (1 << 20)), collective_id=0, has_side_effects=True
@@ -1128,7 +1157,7 @@
     content, query_stream, cot_content, cot_query, doc_lengths, rank_order, pred_counts, w_qkv, bias_qv,
     w_attn_out, b_attn_out, norm1_gain, norm1_shift, w_in, b_in, w_out, b_out, norm2_gain, norm2_shift, rel_table,
 ):
-    out_c, out_g, gc, gg, _, gw, gwo, sm = layer(
+    out_c, out_g, gc, gg, _, _, gw, gwo, sm = layer(
         stride, doc_lengths, pred_counts, content, query_stream, cot_content, cot_query,
         jnp.transpose(w_qkv, (0, 2, 1)).reshape(3 * QW, D), w_attn_out, w_in, w_out,
         rank_order, b_in, bias_qv, rel_table.T, b_attn_out, norm1_gain, norm1_shift, b_out, norm2_gain, norm2_shift,

time: 138 us -> 135 us (0.978)
  Pallas kernels: 137 us -> 134 us
    pallas_call x1, Pallas kernels: 132 us -> 129 us  [layer(): pl.pallas_call(functools.partial(kernel, stride), out_shape=(sd((S, D), B...]
where the time goes in v4:
time: 135 us
  Pallas kernels  134 us (99%)
    pallas_call x1, Pallas kernels, layer(): pl.pallas_call(functools.partial(kernel, stride), out_shape=(sd((S, D), B...  129 us
    pallas_call x1, Pallas kernels, local(): pl.pallas_call(hand_out, out_shape=(sd((S, D), BF16), sd((S, D), BF16), s...  4.95 us

profile of v4, /device:TPU:0, one launch (start us, length us, event | category | flops | bytes accessed | tf_op | source)
XLA Modules:
  0.0 135.2 jit_solution(7683711076054363458)
XLA Ops:
  0.7 129.4 %shard_map.323 = (bf16[512,768]{1,0:T(8,128)(2,1)}, bf16[512,768]{1,0:T(8,128)(2,1)}, f32[512,768]{1,0:T(8,128)}, f32[512,768]{1,0:T(8,128)}, bf16[4,1024,768]{2...) custom-call(s32[4,8]{1,0:T(4,128)} %dl.1, s32[4]{0:T(128)} %pc.1, ...), custom_call_target="tpu_custom_call" | custom-call | tf_op jit(solution)/shard_map/pallas_call | solution.py:1082
  130.1 5.0 %shard_map.324 = (bf16[512,768]{1,0:T(8,128)(2,1)}, bf16[512,768]{1,0:T(8,128)(2,1)}, f32[512,768]{1,0:T(8,128)}, f32[512,768]{1,0:T(8,128)}, f32[3,96,192]{2,1,...) custom-call(bf16[512,768]{1,0:T(8,128)(2,1)} %get-tuple-element.41.o, ...), custom_call_target="tpu_custom_call" | custom-call | tf_op jit(solution)/shard_map/pallas_call | solution.py:1175

commit v5 on v4

--- a/solution.py
+++ b/solution.py
@@ -497,7 +497,7 @@
     for copy in rows_in:
         copy.wait()
 
-    @pl.loop(0, 4)
+    @pl.loop(0, 4, unroll=2)
     def _(i):
         r = pl.ds(pl.multiple_of(i * HALF, HALF), HALF)
         res = hid[r, :].astype(F32) + acc[r, :] + b_out[...]
@@ -855,7 +855,7 @@
         pl.semaphore_signal(credit.at[k], inc=1, device_id=who, device_id_type=MESH)
 
     turn("ln")
-    @pl.loop(0, 4)
+    @pl.loop(0, 4, unroll=2)
     def _(i):
         r = pl.ds(pl.multiple_of(i * HALF, HALF), HALF)
         dy = acc[r, :]

time: 135 us -> 135 us (level)
  no operation moved by 1% of the time
where the time goes in v5:
time: 135 us
  Pallas kernels  134 us (99%)
    pallas_call x1, Pallas kernels, layer(): pl.pallas_call(functools.partial(kernel, stride), out_shape=(sd((S, D), B...  129 us
    pallas_call x1, Pallas kernels, local(): pl.pallas_call(hand_out, out_shape=(sd((S, D), BF16), sd((S, D), BF16), s...  4.95 us

profile of v5, /device:TPU:0, one launch (start us, length us, event | category | flops | bytes accessed | tf_op | source)
XLA Modules:
  0.0 135.3 jit_solution(1435627199575895337)
XLA Ops:
  0.7 129.5 %shard_map.323 = (bf16[512,768]{1,0:T(8,128)(2,1)}, bf16[512,768]{1,0:T(8,128)(2,1)}, f32[512,768]{1,0:T(8,128)}, f32[512,768]{1,0:T(8,128)}, bf16[4,1024,768]{2...) custom-call(s32[4,8]{1,0:T(4,128)} %dl.1, s32[4]{0:T(128)} %pc.1, ...), custom_call_target="tpu_custom_call" | custom-call | tf_op jit(solution)/shard_map/pallas_call | solution.py:1082
  130.1 5.0 %shard_map.324 = (bf16[512,768]{1,0:T(8,128)(2,1)}, bf16[512,768]{1,0:T(8,128)(2,1)}, f32[512,768]{1,0:T(8,128)}, f32[512,768]{1,0:T(8,128)}, f32[3,96,192]{2,1,...) custom-call(bf16[512,768]{1,0:T(8,128)(2,1)} %get-tuple-element.41.o, ...), custom_call_target="tpu_custom_call" | custom-call | tf_op jit(solution)/shard_map/pallas_call | solution.py:1175
